TPU v7x, 32 devices: a whole 2x2x4 slice. The times are simulated.
32 devices in a mesh: gx: 4 (over z), gy: 4 (over x, core), gz: 2 (over y).
Axes of the slice: x: 2, y: 2, z: 4, core: 2. Of those that a mesh axis runs over, the one named last changes fastest.
Arguments:
- forcing: float32 [128, 128, 256], P('gx', 'gy', 'gz'), may hold values from -6 to 6
- kappa_base: float32 [128, 128, 256], P('gx', 'gy', 'gz'), may hold values from 0.5 to 2
- labels: int32 [128, 128, 256], P('gx', 'gy', 'gz'), may hold values from 0 to 3
- contrast: float32 [4], replicated, may hold values from 1 to 100
- channel_weight: float32 [4], replicated, may hold values from 0.25 to 2
- coarse_coef: float32 [4, 4, 2, 64, 8], P('gx', 'gy', 'gz'), may hold values from -6 to 6
- source_link: int32 [4, 4, 2, 40, 4], P('gx', 'gy', 'gz'), may hold values from 0 to 63, as said below
- offsets: int32 [4, 4, 2, 40, 3], P('gx', 'gy', 'gz'), may hold values from 0 to 120, as said below
- live_pieces: int32 [4, 4, 2], P('gx', 'gy', 'gz'), may hold values from 5 to 40, as said below
- resident_bases: float32 [4, 4, 2, 40, 8, 4096], P('gx', 'gy', 'gz'), may hold values from -5 to 5
Outputs:
- update: float32 [128, 128, 256], P('gx', 'gy', 'gz')
- new_basis: float32 [4, 4, 2, 40, 2, 4096], P('gx', 'gy', 'gz')
Inputs may be any that keep to these rules, and one draw needn't show every extreme that they name: `source_link`: each of the three brick offsets of a slot, minus one, leads to a brick inside the mesh; a coefficient slot may be named by several pieces. `offsets`: every piece lies inside its brick's padded frame of (40) x (40) x (136) cells. `live_pieces`: some brick has all 40 slots live in every draw.
All inputs are finite; a program needn't handle non-finite values.
Results may differ from a plain program's by a relative error of at most 0.0003.
Values sent between devices are 32-bit elements; how exact they have to be, the bound alone decides.
No kernel may reach another device: no remote copies, remote signals or barrier semaphores. Data moves between devices by JAX's collectives and lax.ppermute only.
A program may use at most 128 MiB of HBM per device.

v0:
```python
import functools

import jax
import jax.numpy as jnp
from jax import lax
from jax.experimental import pallas as pl
from jax.experimental.pallas import tpu as pltpu
from jax.sharding import PartitionSpec as P

MARGIN = 4
PIECE = 16
SWEEPS = 20
DAMPING = 2.0 / 3.0

H = MARGIN + 1
WIDE = 2 * MARGIN + 1
LANES = 128
SUB = 8
TOP = 8
GROUP = LANES // PIECE
HALVES = PIECE // SUB
CHUNKS = PIECE * HALVES
PROWS = PIECE * PIECE
F32 = jnp.float32


def iotas():
    shape = (SUB, LANES)
    return lax.broadcasted_iota(jnp.int32, shape, 0), lax.broadcasted_iota(jnp.int32, shape, 1)


def loop(count, body, unroll=1):
    while count % unroll:
        unroll -= 1

    def step(i, _):
        for j in range(unroll):
            body(i * unroll + j)
        return 0

    lax.fori_loop(0, count // unroll, step, 0)


def pick(flag, a, b):
    return jnp.where(flag, a, b)


def pack_tiles(tiles, shift, lane):
    packed = jnp.zeros((SUB, LANES), F32)
    for j, tile in enumerate(tiles):
        packed = jnp.where((lane >> 4) == j, pltpu.roll(tile, (shift + PIECE * j) % LANES, 1), packed)
    return packed


def unpack_tile(packed, j, shift):
    return pltpu.roll(packed, (shift - PIECE * j + 2 * LANES) % LANES, 1)


def sum_rows(values, sub):
    for k in (1, 2, 4):
        low = (sub & k) == 0
        values = [
            jnp.where(low, a, b) + pltpu.roll(jnp.where(low, b, a), SUB - k, 0)
            for a, b in zip(values[0::2], values[1::2])
        ]
    return values[0]


def block_transpose(values, sub, lane):
    for k in (4, 2, 1):
        in_group = ((lane >> 4) & k) != 0
        in_sub = (sub & k) != 0
        moves = in_sub != in_group
        if k == 4:
            others = [pltpu.roll(v, 64, 1) for v in values]
            others = [pltpu.roll(v, 4, 0) for v in others]
        else:
            pairs = [(pltpu.roll(v, PIECE * k, 1), pltpu.roll(v, LANES - PIECE * k, 1)) for v in values]
            others = [jnp.where(in_group, q, p) for q, p in pairs]
            others = [jnp.where(in_sub, pltpu.roll(m, k, 0), pltpu.roll(m, SUB - k, 0)) for m in others]
        values = [jnp.where(moves, o, v) for o, v in zip(others, values)]
    return values


class Frame:
    def __init__(self, bx, by, bz, counts):
        self.bx, self.by, self.bz = bx, by, bz
        self.xf = bx + 2 * H
        self.yf = by + 2 * TOP
        self.tiles = self.yf // SUB
        self.blocks = -(-self.xf * self.tiles // GROUP)
        self.rows = self.blocks * GROUP * SUB
        self.live_x = bx + 2 * MARGIN
        self.live_blocks = self.live_x * self.tiles // GROUP
        self.sides = [1 if n == 2 else 2 for n in counts]

    @property
    def frame(self):
        return rows_of(self.rows)


def rows_of(count):
    return jax.ShapeDtypeStruct((-(-count // SUB) * SUB, LANES), F32)


def zero(ref):
    ref[...] = jnp.zeros(ref.shape, ref.dtype)


VMEM = pl.BlockSpec(memory_space=pltpu.VMEM)
SMEM = pl.BlockSpec(memory_space=pltpu.SMEM)
HBM = pl.BlockSpec(memory_space=pl.ANY)


def call(kernel, outs, ins, specs=(), scratch=(), alias=None, limit=12):
    specs = list(specs) + [VMEM] * (len(ins) - len(specs))
    return pl.pallas_call(
        kernel,
        out_shape=outs,
        in_specs=specs,
        out_specs=jax.tree.map(lambda _: VMEM, outs),
        scratch_shapes=list(scratch),
        input_output_aliases=alias or {},
        compiler_params=pltpu.CompilerParams(vmem_limit_bytes=limit * 1024 * 1024),
    )(*ins)


def is_lower(info, axis, phase):
    return ((info[1 + axis] + phase) & 1) == 0


def swap(axis, slabs):
    count = lax.axis_size(axis)
    received = []
    for phase, slab in enumerate(slabs):
        pairs = [(i, i + 1) for i in range(phase, count - 1, 2)]
        received.append(lax.ppermute(slab, axis, pairs + [(j, i) for i, j in pairs]))
    return received


def look_up(labels, values):
    out = jnp.zeros(labels.shape, F32)
    for c in range(values.shape[0]):
        out = out + jnp.where(labels == c, values[c], 0.0)
    return out


def static_x(fr, info, contrast, channel, kappa, labels, forcing, coef, *rest):
    n = fr.sides[0]
    slabs, (k_buf, l_buf, sem) = rest[:n], rest[n:]
    by = fr.by
    f_row, w_row, c_row = H * by, (H + MARGIN) * by, (H + 2 * MARGIN) * by
    copies = []
    for i, slab in enumerate(slabs):
        lower = is_lower(info, 0, i)
        first = pl.multiple_of(pick(lower, (fr.bx - H) * by, 0), SUB)
        four = pl.multiple_of(pick(lower, (fr.bx - MARGIN) * by, 0), SUB)
        for j, (src, dst) in enumerate(
            (
                (kappa.at[pl.ds(first, H * by)], k_buf.at[i]),
                (labels.at[pl.ds(first, H * by)], l_buf.at[i]),
                (forcing.at[pl.ds(four, MARGIN * by)], slab.at[pl.ds(f_row, MARGIN * by)]),
            )
        ):
            copies.append(pltpu.make_async_copy(src, dst, sem.at[i, j]))
    for copy in copies:
        copy.start()
    for slab in slabs:
        slab[c_row : c_row + SUB, :] = jnp.zeros((SUB, LANES), F32)
        slab[c_row : c_row + coef.shape[0], 0 : coef.shape[1]] = coef[...]
    for copy in copies:
        copy.wait()
    for i, slab in enumerate(slabs):
        skip = pl.multiple_of(pick(is_lower(info, 0, i), by, 0), SUB)
        slab[0:f_row, :] = k_buf[i] * look_up(l_buf[i], contrast)
        slab[w_row:c_row, :] = look_up(l_buf[i, pl.ds(skip, MARGIN * by), :], channel)


def static_y(fr, info, contrast, channel, kappa, labels, forcing, coef, *rest):
    n = fr.sides[0]
    received, (k0, f0, w0, coef3), slabs = rest[:n], rest[n : n + 4], rest[n + 4 :]
    by, yf, w = fr.by, fr.yf, 2 * MARGIN + H
    c_in = w * by
    for ref in (k0, f0, w0, coef3):
        zero(ref)

    def core(x):
        for t in range(by // SUB):
            src = pl.ds(x * by + t * SUB, SUB)
            dst = pl.ds((x + H) * yf + TOP + t * SUB, SUB)
            label = labels[src, :]
            k0[dst, :] = kappa[src, :] * look_up(label, contrast)
            w0[dst, :] = look_up(label, channel)
            f0[dst, :] = forcing[src, :]

    loop(fr.bx, core, 4)
    coef3[SUB : SUB + coef.shape[0], 0 : coef.shape[1]] = coef[...]
    for i, buf in enumerate(received):
        lower = is_lower(info, 0, i)
        for frame, count, at, low in ((k0, H, 0, 0), (f0, MARGIN, H, 1), (w0, MARGIN, H + MARGIN, 1)):
            first = pick(lower, fr.bx + H, low)
            for j in range(count):
                for t in range(by // SUB):
                    row = (at + j) * by + t * SUB
                    frame[pl.ds(pl.multiple_of((first + j) * yf + TOP + t * SUB, SUB), SUB), :] = buf[row : row + SUB, :]
        coef3[pl.ds(pl.multiple_of(pick(lower, 2 * SUB, 0), SUB), SUB), :] = buf[c_in : c_in + SUB, :]

    def plane(x):
        r, o = x * yf, x * w
        for i, slab in enumerate(slabs):
            lower = is_lower(info, 1, i)
            for frame, count, at in ((k0, H, 0), (f0, MARGIN, H), (w0, MARGIN, H + MARGIN)):
                first = r + pick(lower, TOP + by - count, TOP)
                slab[pl.ds(o + at, count), :] = frame[pl.ds(first, count), :]

    loop(fr.xf, plane, 6)
    c_out = -(-fr.xf * w // SUB) * SUB
    for slab in slabs:
        slab[c_out : c_out + 3 * SUB, :] = coef3[...]


def static_z(fr, info, k_in, f_in, w_in, coef3, *rest):
    n = fr.sides[1]
    received, (k0, f0, w0, coef9), slabs = rest[:n], rest[n : n + 4], rest[n + 4 :]
    del k_in, f_in, w_in
    _, lane = iotas()
    by, yf, w = fr.by, fr.yf, 2 * MARGIN + H
    c_in = -(-fr.xf * w // SUB) * SUB

    def plane(x):
        r, o = x * yf, x * w
        for i, buf in enumerate(received):
            lower = is_lower(info, 1, i)
            for frame, count, at in ((k0, H, 0), (f0, MARGIN, H), (w0, MARGIN, H + MARGIN)):
                first = r + pick(lower, TOP + by, TOP - count)
                frame[pl.ds(first, count), :] = buf[pl.ds(o + at, count), :]

    loop(fr.xf, plane, 6)
    zero(coef9)
    for x in range(3):
        coef9[(x * 3 + 1) * SUB : (x * 3 + 2) * SUB, :] = coef3[x * SUB : (x + 1) * SUB, :]
        for i, buf in enumerate(received):
            to = pl.multiple_of((x * 3 + pick(is_lower(info, 1, i), 2, 0)) * SUB, SUB)
            coef9[pl.ds(to, SUB), :] = buf[c_in + x * SUB : c_in + (x + 1) * SUB, :]
    group = lane & (PIECE - 1)

    def block(b):
        for i, slab in enumerate(slabs):
            lower = is_lower(info, 2, i)
            packs = []
            for frame, high, low in ((k0, H, 0), (f0, WIDE, H), (w0, WIDE + MARGIN, WIDE)):
                tiles = [frame[pl.ds((b * GROUP + j) * SUB, SUB), :] for j in range(GROUP)]
                packs.append(pack_tiles(tiles, pick(lower, high, low), lane))
            mix = jnp.where(group < H, packs[0], jnp.where(group < WIDE, packs[1], packs[2]))
            slab[pl.ds(b * SUB, SUB), :] = mix

    loop(fr.blocks, block, 4)
    c_out = fr.blocks * SUB
    for slab in slabs:
        slab[c_out : c_out + 9 * SUB, :] = coef9[...]


def place_masks(z0, lane):
    main = (lane >= z0) & (lane < z0 + PIECE)
    beyond = jnp.where(lane < LANES // 2, lane + LANES, lane - LANES)
    return main, (beyond >= z0) & (beyond < z0 + PIECE)


def corner(off, p):
    return off[0, p] + 1, off[1, p] + TOP - MARGIN, off[2, p] - MARGIN


def add_piece(fr, off, p, valid, values, lane, main_ref, beyond_ref):
    x0, y0, z0 = corner(off, p)
    base = x0 * fr.yf + y0
    main, beyond = place_masks(z0, lane)
    places = [pl.ds(base + (c // HALVES) * fr.yf + (c % HALVES) * SUB, SUB) for c in range(CHUNKS)]
    main = main & valid
    new = [main_ref[a, :] + jnp.where(main, v, 0.0) for a, v in zip(places, values)]
    for a, v in zip(places, new):
        main_ref[a, :] = v

    @pl.when(valid & ((z0 < 0) | (z0 + PIECE > LANES)))
    def _():
        new = [beyond_ref[a, :] + jnp.where(beyond, v, 0.0) for a, v in zip(places, values)]
        for a, v in zip(places, new):
            beyond_ref[a, :] = v


def prolong(fr, shape, info, off, link, bases, coef9, *rest):
    slots, nb, together = shape
    n = fr.sides[2]
    received, (p0, p1), slabs, (table, buf, sem) = rest[:n], rest[n : n + 2], rest[n + 2 : 2 * n + 2], rest[2 * n + 2 :]
    sub, lane = iotas()
    live = info[0]

    def start(p, _):
        pltpu.make_async_copy(bases.at[p], buf.at[p], sem.at[p]).start()
        return 0

    lax.fori_loop(0, live, start, 0)
    zero(p0)
    zero(p1)
    for xy in range(9):
        table[xy * 3 + 1] = coef9[xy * SUB : (xy + 1) * SUB, :]
        for i, part in enumerate(received):
            at = (fr.blocks + xy) * SUB
            table[xy * 3 + pick(is_lower(info, 2, i), 2, 0)] = part[at : at + SUB, :]

    def some(step, _):
        numbers, valids, spread = [], [], []
        for i in range(together):
            p = step * together + i
            valids.append(p < live)
            numbers.append(p)

            @pl.when(p < live)
            def _():
                pltpu.make_async_copy(bases.at[p], buf.at[p], sem.at[p]).wait()

        for p in numbers:
            row = table[(link[0, p] * 3 + link[1, p]) * 3 + link[2, p]]
            coef = jnp.sum(jnp.where(lane == link[3, p], row, 0.0), axis=1, keepdims=True)
            coef = jnp.broadcast_to(coef, (SUB, LANES))[0:nb]
            for first in range(0, CHUNKS, SUB):
                parts = [buf[p, :, c * LANES : (c + 1) * LANES] * coef for c in range(first, first + SUB)]
                spread.append(sum_rows(parts, sub))
        spread = block_transpose(spread, sub, lane)
        per = CHUNKS // SUB
        for i, (p, valid) in enumerate(zip(numbers, valids)):
            z0 = off[2, p] - MARGIN
            values = [
                pltpu.roll(rows, (z0 - PIECE * j + 2 * LANES) % LANES, 1)
                for rows in spread[i * per : (i + 1) * per]
                for j in range(SUB)
            ]
            add_piece(fr, off, p, valid, values, lane, p0, p1)
        return 0

    lax.fori_loop(0, (live + together - 1) // together, some, 0)

    def block(b):
        tiles = []
        for j in range(GROUP):
            at = pl.ds(fr.yf + (b * GROUP + j) * SUB, SUB)
            tiles.append((p0[at, :], p1[at, :]))
        for i, slab in enumerate(slabs):
            lower = is_lower(info, 2, i)
            main = (lane >= LANES // 2) == lower
            near = [jnp.where(main, x, y) for x, y in tiles]
            slab[pl.ds(b * SUB, SUB), :] = pack_tiles(near, SUB, lane)

    loop(fr.live_blocks, block, 3)


def coarse_y(fr, info, p0_in, p1_in, *rest):
    n = fr.sides[2]
    received, (p0, p1), slabs = rest[:n], rest[n : n + 2], rest[n + 2 :]
    del p0_in, p1_in
    _, lane = iotas()
    packed = fr.live_x * WIDE

    def block(b):
        for i, buf in enumerate(received):
            lower = is_lower(info, 2, i)
            pack = buf[pl.ds(b * SUB, SUB), :]
            places = [pl.ds(fr.yf + (b * GROUP + j) * SUB, SUB) for j in range(GROUP)]
            values = [unpack_tile(pack, j, LANES - SUB) for j in range(GROUP)]
            to_main = ((lane >= LANES - SUB) & lower) | ((lane < SUB) & jnp.logical_not(lower))
            to_beyond = ((lane >= LANES - SUB) & jnp.logical_not(lower)) | ((lane < SUB) & lower)
            main = [p0[a, :] + jnp.where(to_main, v, 0.0) for a, v in zip(places, values)]
            beyond = [p1[a, :] + jnp.where(to_beyond, v, 0.0) for a, v in zip(places, values)]
            for a, v0, v1 in zip(places, main, beyond):
                p0[a, :] = v0
                p1[a, :] = v1

    loop(fr.live_blocks, block, 3)

    def plane(x):
        r = (x + 1) * fr.yf
        for i, slab in enumerate(slabs):
            first = r + pick(is_lower(info, 1, i), TOP + fr.by - H, TOP - MARGIN)
            slab[pl.ds(x * WIDE, WIDE), :] = p0[pl.ds(first, WIDE), :]

    loop(fr.live_x, plane, 8)

    def margin(b):
        for i, slab in enumerate(slabs):
            first = pick(is_lower(info, 1, i), fr.tiles - 2, 0)
            tiles = []
            for j in range(GROUP):
                row = (b * (GROUP // 2) + j // 2 + 1) * fr.yf + (first + j % 2) * SUB
                tiles.append(p1[pl.ds(row, SUB), :])
            slab[pl.ds(packed + b * SUB, SUB), :] = pack_tiles(tiles, SUB, lane)

    loop(fr.live_x * 2 // GROUP, margin, 5)


def coarse_x(fr, info, p0_in, p1_in, *rest):
    n = fr.sides[1]
    received, (p0, p1), slabs = rest[:n], rest[n : n + 2], rest[n + 2 :]
    del p0_in, p1_in
    _, lane = iotas()
    packed = fr.live_x * WIDE
    edge = (lane >= LANES - SUB) | (lane < SUB)

    def plane(x):
        r = (x + 1) * fr.yf
        for i, buf in enumerate(received):
            at = pl.ds(r + pick(is_lower(info, 1, i), TOP + fr.by - MARGIN, TOP - H), WIDE)
            p0[at, :] = p0[at, :] + buf[pl.ds(x * WIDE, WIDE), :]

    loop(fr.live_x, plane, 8)

    def margin(b):
        for i, buf in enumerate(received):
            first = pick(is_lower(info, 1, i), fr.tiles - 2, 0)
            pack = buf[pl.ds(packed + b * SUB, SUB), :]
            places = [
                pl.ds((b * (GROUP // 2) + j // 2 + 1) * fr.yf + (first + j % 2) * SUB, SUB) for j in range(GROUP)
            ]
            values = [jnp.where(edge, unpack_tile(pack, j, LANES - SUB), 0.0) for j in range(GROUP)]
            values = [p1[a, :] + v for a, v in zip(places, values)]
            for a, v in zip(places, values):
                p1[a, :] = v

    loop(fr.live_x * 2 // GROUP, margin, 5)
    main = WIDE * fr.yf
    for i, slab in enumerate(slabs):
        row = pl.multiple_of(pick(is_lower(info, 0, i), fr.xf - 1 - WIDE, 1) * fr.yf, SUB)
        slab[0:main, :] = p0[pl.ds(row, main), :]
        for b in range(-(-WIDE * fr.tiles // GROUP)):
            tiles = [p1[pl.ds(row + (b * GROUP + j) * SUB, SUB), :] for j in range(GROUP)]
            slab[main + b * SUB : main + (b + 1) * SUB, :] = pack_tiles(tiles, SUB, lane)


def enrich(fr, info, off, p0, p1, k0, f0, w0, *rest):
    n0, n2 = fr.sides[0], fr.sides[2]
    x_in, z_in, rest = rest[:n0], rest[n0 : n0 + n2], rest[n0 + n2 :]
    core, basis, y_edge, x_edge, slab = rest[:5]
    c0, c1, k1, r0, r1, w1, q0, q1, kb, rb, wb, wt, base, va, vb = rest[5:]
    sub, lane = iotas()
    yf, tiles = fr.yf, fr.tiles
    live = info[0]
    main_rows = WIDE * yf
    edge = (lane >= LANES - SUB) | (lane < SUB)

    c0[...] = p0[...]
    c1[...] = p1[...]
    for i, buf in enumerate(x_in):
        row = pl.multiple_of(pick(is_lower(info, 0, i), fr.xf - WIDE, 0) * yf, SUB)
        a = pl.ds(row, main_rows)
        c0[a, :] = c0[a, :] + buf[0:main_rows, :]
        for b in range(-(-WIDE * tiles // GROUP)):
            pack = buf[main_rows + b * SUB : main_rows + (b + 1) * SUB, :]
            count = min(GROUP, WIDE * tiles - b * GROUP)
            places = [pl.ds(row + (b * GROUP + j) * SUB, SUB) for j in range(count)]
            values = [jnp.where(edge, unpack_tile(pack, j, LANES - SUB), 0.0) for j in range(count)]
            for a, v in zip(places, [c1[a, :] + v for a, v in zip(places, values)]):
                c1[a, :] = v

    f1 = r1

    def beyond_z(b):
        sums = [[0.0] * GROUP for _ in range(3)]
        for i, buf in enumerate(z_in):
            lower = is_lower(info, 2, i)
            pack = buf[pl.ds(b * SUB, SUB), :]
            for m, (start, width) in enumerate(((0, H), (H, MARGIN), (H + MARGIN, MARGIN))):
                shift = pick(lower, LANES - start, LANES - width - start)
                low = pick(lower, 0, LANES - width)
                keep = (lane >= low) & (lane < low + width)
                for j in range(GROUP):
                    sums[m][j] = sums[m][j] + jnp.where(keep, unpack_tile(pack, j, shift), 0.0)
        for j in range(GROUP):
            at = pl.ds((b * GROUP + j) * SUB, SUB)
            k1[at, :] = sums[0][j]
            f1[at, :] = sums[1][j]
            w1[at, :] = sums[2][j]
            c0[at, :] = jnp.where(k0[at, :] > 0, c0[at, :], 0.0)
            c1[at, :] = jnp.where(sums[0][j] > 0, c1[at, :], 0.0)

    loop(fr.blocks, beyond_z, 2)

    def next_z(a, b):
        return pltpu.roll(jnp.where(lane == 0, b, a), LANES - 1, 1)

    def last_z(a, b):
        return pltpu.roll(jnp.where(lane == LANES - 1, b, a), 1, 1)

    def residual(x):
        r = (x + 1) * yf
        for t in range(tiles):
            at = pl.ds(r + t * SUB, SUB)
            for c, k, f, oc, ok, out in ((c0, k0, f0, c1, k1, r0), (c1, k1, f1, c0, k0, r1)):
                cc, kc = c[at, :], k[at, :]
                total = jnp.zeros((SUB, LANES), F32)
                beside = [
                    (c[pl.ds(r + t * SUB + d, SUB), :], k[pl.ds(r + t * SUB + d, SUB), :])
                    for d in (-yf, yf, -1, 1)
                ]
                beside += [(next_z(cc, oc[at, :]), next_z(kc, ok[at, :]))]
                beside += [(last_z(cc, oc[at, :]), last_z(kc, ok[at, :]))]
                for cn, kn in beside:
                    total = total + jnp.where(kn > 0, 0.5 * (kc + kn), kc) * (cc - cn)
                out[at, :] = jnp.where(kc > 0, f[at, :] - total, 0.0)

    loop(fr.live_x, residual, 1)

    zero(q0)
    zero(q1)
    for ref in (kb, va, vb):
        zero(ref)

    first_y, last_y = sub == 0, sub == SUB - 1
    z_cell = lane & (PIECE - 1)

    def tent(t):
        return (t + 0.5) * (PIECE - t - 0.5) * (4.0 / (PIECE * PIECE))

    def one_group(group, _):
        first = group * GROUP
        bases, shifts, spans, slots = [], [], [], []
        for g in range(GROUP):
            x0, y0, z0 = corner(off, first + g)
            bases.append(x0 * yf + y0)
            shifts.append((g * PIECE - z0 + LANES) % LANES)
            spans.append(z0)
            slots.append(jnp.where(first + g < live, g, -1))

        def gather(x):
            for h in range(HALVES):
                accs = [jnp.zeros((SUB, LANES), F32) for _ in range(3)]
                for g in range(GROUP):
                    at = pl.ds(bases[g] + x * yf + h * SUB, SUB)
                    main = (lane >= spans[g]) & (lane < spans[g] + PIECE)
                    keep = (lane >> 4) == slots[g]
                    for j, (a, b) in enumerate(((k0, k1), (r0, r1), (w0, w1))):
                        v = pltpu.roll(jnp.where(main, a[at, :], b[at, :]), shifts[g], 1)
                        accs[j] = jnp.where(keep, v, accs[j])
                r = x * PIECE + h * SUB
                kb[pl.ds(PIECE + r, SUB), :] = accs[0]
                rb[pl.ds(r, SUB), :] = accs[1]
                wb[pl.ds(r, SUB), :] = accs[2]

        loop(PIECE, gather, 4)

        def setup(x):
            for h in range(HALVES):
                r = x * PIECE + h * SUB
                kc = kb[pl.ds(PIECE + r, SUB), :]
                kn = [kb[pl.ds(PIECE + r + d, SUB), :] for d in (PIECE, -PIECE, 1, -1)]
                kn += [pltpu.roll(kc, LANES - 1, 1), pltpu.roll(kc, 1, 1)]
                if h == HALVES - 1:
                    kn[2] = jnp.where(last_y, 0.0, kn[2])
                if h == 0:
                    kn[3] = jnp.where(first_y, 0.0, kn[3])
                kn[4] = jnp.where(z_cell == PIECE - 1, 0.0, kn[4])
                kn[5] = jnp.where(z_cell == 0, 0.0, kn[5])
                faces, diag = [], jnp.zeros((SUB, LANES), F32)
                for k in kn:
                    there = k > 0
                    half = 0.5 * (kc + k)
                    faces.append(jnp.where(there, half, 0.0))
                    diag = diag + jnp.where(there, half, kc)
                inside = kc > 0
                scale = jnp.where(inside, DAMPING / jnp.where(inside, diag, 1.0), 0.0)
                for j, face in enumerate(faces):
                    wt[j, pl.ds(r, SUB), :] = face * scale
                s = rb[pl.ds(r, SUB), :] * scale
                s2 = s * wb[pl.ds(r, SUB), :]
                base[0, pl.ds(r, SUB), :] = s
                base[1, pl.ds(r, SUB), :] = s2
                va[0, pl.ds(PIECE + r, SUB), :] = s
                va[1, pl.ds(PIECE + r, SUB), :] = s2

        loop(PIECE, setup, 8)

        def sweep(src, dst):
            for x in range(PIECE):
                for h in range(HALVES):
                    r = x * PIECE + h * SUB
                    a = PIECE + r
                    w = [wt[j, r : r + SUB, :] for j in range(6)]
                    for s in range(2):
                        v = src[s, a : a + SUB, :]
                        total = base[s, r : r + SUB, :] + v * (1.0 - DAMPING)
                        if x < PIECE - 1:
                            total = total + w[0] * src[s, a + PIECE : a + PIECE + SUB, :]
                        if x > 0:
                            total = total + w[1] * src[s, a - PIECE : a - PIECE + SUB, :]
                        total = total + w[2] * src[s, a + 1 : a + 1 + SUB, :]
                        total = total + w[3] * src[s, a - 1 : a - 1 + SUB, :]
                        total = total + w[4] * pltpu.roll(v, LANES - 1, 1)
                        total = total + w[5] * pltpu.roll(v, 1, 1)
                        dst[s, a : a + SUB, :] = total

        def two(i, _):
            sweep(va, vb)
            sweep(vb, va)
            return 0

        lax.fori_loop(0, (SWEEPS - 1) // 2, two, 0)
        if (SWEEPS - 1) % 2:
            sweep(va, vb)
            done = vb
        else:
            done = va

        tz = tent(z_cell.astype(F32))
        ty = [tent(sub.astype(F32) + float(SUB * h)) * tz for h in range(HALVES)]
        for c in range(0, CHUNKS, SUB):
            values = []
            for i in range(SUB):
                r = (c + i) * SUB
                v0, v1 = done[0, PIECE + r : PIECE + r + SUB, :], done[1, PIECE + r : PIECE + r + SUB, :]
                rb[r : r + SUB, :] = (v0 + v1) * (ty[(c + i) % HALVES] * float(tent((c + i) // HALVES)))
                values += [v0, v1]
            for i, v in enumerate(block_transpose(values, sub, lane)):
                at = first * CHUNKS * 2 + c * 2 + i
                basis[pl.ds(at, GROUP, stride=CHUNKS * 2), :] = v

        for g in range(GROUP):
            z0 = off[2, first + g] - MARGIN
            shift = (z0 - g * PIECE + 2 * LANES) % LANES
            values = [pltpu.roll(rb[c * SUB : (c + 1) * SUB, :], shift, 1) for c in range(CHUNKS)]
            add_piece(fr, off, first + g, first + g < live, values, lane, q0, q1)
        return 0

    groups = (live + GROUP - 1) // GROUP
    lax.fori_loop(0, groups, one_group, 0)

    def clear(group, _):
        count = GROUP * CHUNKS * 2
        basis[pl.ds(pl.multiple_of(group * count, SUB), count), :] = jnp.zeros((count, LANES), F32)
        return 0

    lax.fori_loop(groups, basis.shape[0] // (GROUP * CHUNKS * 2), clear, 0)

    def block(b):
        part = [q1[pl.ds(yf + (b * GROUP + j) * SUB, SUB), :] for j in range(GROUP)]
        slab[pl.ds(b * SUB, SUB), :] = pack_tiles(part, SUB, lane)

    loop(fr.live_blocks, block, 5)

    def core_rows(x):
        for t in range(fr.by // SUB):
            at = pl.ds((x + H) * yf + TOP + t * SUB, SUB)
            core[pl.ds(x * fr.by + t * SUB, SUB), :] = c0[at, :] + q0[at, :]

    loop(fr.bx, core_rows, 4)

    def edge_rows(x):
        for j, t in enumerate((tiles - 1, 0)):
            y_edge[pl.ds((2 * x + j) * SUB, SUB), :] = q0[pl.ds((x + 1) * yf + t * SUB, SUB), :]

    loop(fr.live_x, edge_rows, 8)
    for i, x in enumerate(edge_planes(fr)):
        row = (x + 1) * yf + TOP
        x_edge[i * fr.by : (i + 1) * fr.by, :] = q0[row : row + fr.by, :]


def edge_planes(fr):
    return [*range(fr.live_x - MARGIN, fr.live_x), *range(MARGIN)]


def z_part(info, sides, received, pack, j, lane):
    total = 0.0
    for i, buf in enumerate(received):
        lower = is_lower(info, 2, i)
        keep = ((lane >= LANES - SUB) & lower) | ((lane < SUB) & jnp.logical_not(lower))
        v = unpack_tile(buf[pl.ds(pack * SUB, SUB), :], j, LANES - SUB)
        total = total + jnp.where(keep, v, 0.0)
    return total


def fold_y(fr, info, y_edge, *rest):
    n = fr.sides[2]
    received, slabs, tmp = rest[:n], rest[n:-1], rest[-1]
    _, lane = iotas()

    def planes(b):
        for i in range(4):
            for j, t in enumerate((fr.tiles - 1, 0)):
                m = i * fr.tiles + t
                at = pl.ds(((4 * b + i) * 2 + j) * SUB, SUB)
                part = z_part(info, n, received, b * (4 * fr.tiles // GROUP) + m // GROUP, m % GROUP, lane)
                tmp[at, :] = y_edge[at, :] + part

    loop(fr.live_x // 4, planes, 5)

    def plane(x):
        for i, slab in enumerate(slabs):
            first = x * 2 * SUB + pick(is_lower(info, 1, i), 0, SUB + MARGIN)
            slab[pl.ds(x * MARGIN, MARGIN), :] = tmp[pl.ds(first, MARGIN), :]

    loop(fr.live_x, plane, 8)


def fold_x(fr, info, x_edge, *rest):
    n1, n2 = fr.sides[1], fr.sides[2]
    z_in, y_in, slabs, tmp = rest[:n2], rest[n2 : n1 + n2], rest[n1 + n2 : -1], rest[-1]
    _, lane = iotas()
    by = fr.by
    for i, x in enumerate(edge_planes(fr)):
        for t in range(by // SUB):
            m = x * fr.tiles + t + 1
            a = slice(i * by + t * SUB, i * by + (t + 1) * SUB)
            tmp[a, :] = x_edge[a, :] + z_part(info, n2, z_in, m // GROUP, m % GROUP, lane)
        for k, buf in enumerate(y_in):
            a = pl.ds(i * by + pick(is_lower(info, 1, k), by - MARGIN, 0), MARGIN)
            tmp[a, :] = tmp[a, :] + buf[x * MARGIN : (x + 1) * MARGIN, :]
    count = MARGIN * by
    for i, slab in enumerate(slabs):
        slab[...] = tmp[pl.ds(pl.multiple_of(pick(is_lower(info, 0, i), 0, count), SUB), count), :]


def finish(fr, info, core, *rest):
    n0, n1, n2 = fr.sides
    z_in, y_in, x_in, out = rest[:n2], rest[n2 : n1 + n2], rest[n1 + n2 : -1], rest[-1]
    _, lane = iotas()
    by = fr.by

    def planes(b):
        for i in range(4):
            row = (4 * b + i) * by
            for t in range(by // SUB):
                m = i * fr.tiles + t + 1
                at = pl.ds(row + t * SUB, SUB)
                pack = (b + MARGIN // 4) * (4 * fr.tiles // GROUP) + m // GROUP
                out[at, :] = core[at, :] + z_part(info, n2, z_in, pack, m % GROUP, lane)
            for k, buf in enumerate(y_in):
                a = pl.ds(row + pick(is_lower(info, 1, k), by - MARGIN, 0), MARGIN)
                out[a, :] = out[a, :] + buf[pl.ds((4 * b + i + MARGIN) * MARGIN, MARGIN), :]

    loop(fr.bx // 4, planes, 4)
    count = MARGIN * by
    for i, buf in enumerate(x_in):
        a = pl.ds(pl.multiple_of(pick(is_lower(info, 0, i), (fr.bx - MARGIN) * by, 0), SUB), count)
        out[a, :] = out[a, :] + buf[...]


def local(
    forcing,
    kappa_base,
    labels,
    contrast,
    channel_weight,
    coarse_coef,
    source_link,
    offsets,
    live_pieces,
    resident_bases,
):
    bx, by, bz = forcing.shape
    axes = ("gx", "gy", "gz")
    fr = Frame(bx, by, bz, [lax.axis_size(a) for a in axes])
    slots, nb = resident_bases.shape[3], resident_bases.shape[4]
    nd = coarse_coef.shape[3]
    cells = PIECE**3
    part = functools.partial
    n0, n1, n2 = fr.sides
    live_rows = fr.live_blocks * SUB

    info = jnp.stack([live_pieces[0, 0, 0]] + [lax.axis_index(a).astype(jnp.int32) for a in axes])
    off = jnp.swapaxes(offsets.reshape(slots, 3), 0, 1)
    link = jnp.swapaxes(source_link.reshape(slots, 4), 0, 1)
    coef = jnp.swapaxes(coarse_coef.reshape(nd, nb), 0, 1)
    bases = resident_bases.reshape(slots, nb, cells)
    raw = [a.reshape(bx * by, bz) for a in (kappa_base, labels, forcing)]

    width = 2 * MARGIN + H
    slab = rows_of(width * by + SUB)
    slabs = call(
        part(static_x, fr),
        [slab] * n0,
        [info, contrast, channel_weight, *raw, coef],
        [SMEM] * 3 + [HBM] * 3,
        [
            pltpu.VMEM((n0, H * by, LANES), F32),
            pltpu.VMEM((n0, H * by, LANES), jnp.int32),
            pltpu.SemaphoreType.DMA((n0, 3)),
        ],
    )
    received = swap("gx", slabs)
    slab = rows_of(-(-fr.xf * width // SUB) * SUB + 3 * SUB)
    k0, f0, w0, coef3, *slabs = call(
        part(static_y, fr),
        [fr.frame] * 3 + [rows_of(3 * SUB)] + [slab] * n1,
        [info, contrast, channel_weight, *raw, coef, *received],
        [SMEM] * 3,
    )
    received = swap("gy", slabs)
    slab = rows_of((fr.blocks + 9) * SUB)
    k0, f0, w0, coef9, *slabs = call(
        part(static_z, fr),
        [fr.frame] * 3 + [rows_of(9 * SUB)] + [slab] * n2,
        [info, k0, f0, w0, coef3, *received],
        [SMEM],
        alias={1: 0, 2: 1, 3: 2},
    )
    static_z_in = swap("gz", slabs)

    p0, p1, *slabs = call(
        part(prolong, fr, (slots, nb, 4 if slots % 4 == 0 else 1)),
        [fr.frame] * 2 + [rows_of(live_rows)] * n2,
        [info, off, link, bases, coef9, *static_z_in],
        [SMEM] * 3 + [HBM],
        [
            pltpu.VMEM((27, SUB, LANES), F32),
            pltpu.VMEM((slots, nb, cells), F32),
            pltpu.SemaphoreType.DMA((slots,)),
        ],
        limit=16,
    )
    received = swap("gz", slabs)
    p0, p1, *slabs = call(
        part(coarse_y, fr),
        [fr.frame] * 2 + [rows_of(fr.live_x * (WIDE + 2))] * n1,
        [info, p0, p1, *received],
        [SMEM],
        alias={1: 0, 2: 1},
    )
    received = swap("gy", slabs)
    p0, p1, *slabs = call(
        part(coarse_x, fr),
        [fr.frame] * 2 + [rows_of(WIDE * fr.yf + -(-WIDE * fr.tiles // GROUP) * SUB)] * n0,
        [info, p0, p1, *received],
        [SMEM],
        alias={1: 0, 2: 1},
    )
    received = swap("gx", slabs)

    frame = pltpu.VMEM((fr.rows, LANES), F32)
    padded = PROWS + 2 * PIECE
    core, basis, y_edge, x_edge, slab = call(
        part(enrich, fr),
        [
            rows_of(bx * by),
            rows_of(slots * CHUNKS * 2),
            rows_of(fr.live_x * 2 * SUB),
            rows_of(2 * MARGIN * by),
            rows_of(live_rows),
        ],
        [info, off, p0, p1, k0, f0, w0, *received, *static_z_in],
        [SMEM] * 2,
        [frame] * 8
        + [
            pltpu.VMEM((padded, LANES), F32),
            pltpu.VMEM((PROWS, LANES), F32),
            pltpu.VMEM((PROWS, LANES), F32),
            pltpu.VMEM((6, PROWS, LANES), F32),
            pltpu.VMEM((2, PROWS, LANES), F32),
            pltpu.VMEM((2, padded, LANES), F32),
            pltpu.VMEM((2, padded, LANES), F32),
        ],
        limit=32,
    )

    z_in = swap("gz", [slab] * n2)
    slabs = call(
        part(fold_y, fr),
        [rows_of(fr.live_x * MARGIN)] * n1,
        [info, y_edge, *z_in],
        [SMEM],
        [pltpu.VMEM((fr.live_x * 2 * SUB, LANES), F32)],
    )
    y_in = swap("gy", slabs)
    slabs = call(
        part(fold_x, fr),
        [rows_of(MARGIN * by)] * n0,
        [info, x_edge, *z_in, *y_in],
        [SMEM],
        [pltpu.VMEM((2 * MARGIN * by, LANES), F32)],
    )
    x_in = swap("gx", slabs)
    update = call(part(finish, fr), rows_of(bx * by), [info, core, *z_in, *y_in, *x_in], [SMEM])
    new_basis = basis.reshape(slots, CHUNKS, 2, LANES).swapaxes(1, 2)
    return update.reshape(bx, by, bz), new_basis.reshape(1, 1, 1, slots, 2, cells)


def solution(mesh):
    brick = ("gx", "gy", "gz")
    return jax.shard_map(
        local,
        mesh=mesh,
        in_specs=(
            P(*brick),
            P(*brick),
            P(*brick),
            P(),
            P(),
            P(*brick, None, None),
            P(*brick, None, None),
            P(*brick, None, None),
            P(*brick),
            P(*brick, None, None, None),
        ),
        out_specs=(P(*brick), P(*brick, None, None, None)),
        check_vma=False,
    )
```

profile of v0, /device:TPU:10, one launch (start us, length us, event | category | flops | bytes accessed | tf_op | source)
XLA Modules:
  0.0 134.1 jit_solution(5194351194830398555)
XLA Ops:
  0.6 0.0 copy-start.8
  1.5 0.1 pad_add_fusion.info
  1.5 1.5 %copy-done.1 = f32[32,32,128]{2,1,0:T(8,128)S(1)} copy-done((f32[32,32,128]{2,1,0:T(8,128)S(1)}, f32[32,32,128]{2,1,0:T(8,128)}, u32[]{:S(2)}) %copy-start.1) | copy-done | bytes 524312
  3.0 1.0 copy-done.2
  4.1 1.0 copy-done.3
  5.1 0.7 copy-done.4
  5.8 0.7 copy-done.6
  6.4 0.7 copy-done.7
  7.1 1.3 shard_map.113
  8.4 0.5 collective-permute-start
  9.0 4.6 %collective-permute-start.1 = (f32[424,128]{1,0:T(8,128)S(1)}, f32[424,128]{1,0:T(8,128)S(1)}, u32[]{:S(2)}, u32[]{:S(2)}) collective-permute-start(f32[424,128]{1,0:T(8,128)S(1)} %get-tuple-element.36), channel_id=1, source_target_pairs={{8,16},{16,8},{9,17},{17,9},{10,18},{18,10},{11,19},{19,11},{12,20... | collective-permute-start | bytes 651272 | tf_op jit(solution)/shard_map/ppermute | solution.py:137
  13.6 2.0 %collective-permute-done.rest_0_ = f32[424,128]{1,0:T(8,128)S(1)} collective-permute-done((f32[424,128]{1,0:T(8,128)S(1)}, f32[424,128]{1,0:T(8,128)S(1)}, u32[]{:S(2)}, u32[]{:S(2)}) %collective-permute-start) | collective-permute-done | bytes 217120 | tf_op jit(solution)/shard_map/ppermute | solution.py:137
  15.6 3.0 %collective-permute-done.1.rest_1_ = f32[424,128]{1,0:T(8,128)S(1)} collective-permute-done((f32[424,128]{1,0:T(8,128)S(1)}, f32[424,128]{1,0:T(8,128)S(1)}, u32[]{:S(2)}, u32[]{:S(2)}) %collective-permute-start.1) | collective-permute-done | bytes 217120 | tf_op jit(solution)/shard_map/ppermute | solution.py:137
  18.6 1.3 shard_map.114
  19.9 0.1 collective-permute-start.2
  20.0 2.5 %collective-permute-start.3 = (f32[576,128]{1,0:T(8,128)S(1)}, f32[576,128]{1,0:T(8,128)S(1)}, u32[]{:S(2)}, u32[]{:S(2)}) collective-permute-start(f32[576,128]{1,0:T(8,128)S(1)} %get-tuple-element.42), channel_id=1, source_target_pairs={{2,4},{4,2},{3,5},{5,3},{10,12},{12,10},{11,13},{13,11},{18,20},{2... | collective-permute-start | bytes 884744 | tf_op jit(solution)/shard_map/ppermute | solution.py:137
  22.6 0.0 collective-permute-done.2.rest_0_
  22.6 5.5 %collective-permute-done.3.rest_1_ = f32[576,128]{1,0:T(8,128)S(1)} collective-permute-done((f32[576,128]{1,0:T(8,128)S(1)}, f32[576,128]{1,0:T(8,128)S(1)}, u32[]{:S(2)}, u32[]{:S(2)}) %collective-permute-start.3) | collective-permute-done | bytes 294944 | tf_op jit(solution)/shard_map/ppermute | solution.py:137
  28.1 2.3 %shard_map.115 = (f32[2048,128]{1,0:T(8,128)S(1)}, f32[2048,128]{1,0:T(8,128)S(1)}, f32[2048,128]{1,0:T(8,128)S(1)}, f32[72,128]{1,0:T(8,128)S(1)}, f32[328,128]{1,0:T(8,128)S(1)}) custom-call(s32[4]{0:T(128)S(1)} %pad_add_fusion.info, f32[2048,128]{1,0:T(8,128)S(1)} %get-tuple-element.37.k_in, ...), custom_call_target="tpu_custom_call", output_to_operand_aliasing={{0}: (1, {}), {1}: (2, {}), {2}: (3, {})} | custom-call | tf_op jit(solution)/shard_map/pallas_call | solution.py:117
  30.4 1.6 %collective-permute-start.4 = (f32[328,128]{1,0:T(8,128)S(1)}, f32[328,128]{1,0:T(8,128)S(1)}, u32[]{:S(2)}, u32[]{:S(2)}) collective-permute-start(f32[328,128]{1,0:T(8,128)S(1)} %get-tuple-element.44), channel_id=1, source_target_pairs={{0,1},{1,0},{2,3},{3,2},{4,5},{5,4},{6,7},{7,6},{8,9},{9,8},{10,11... | collective-permute-start | bytes 503816 | tf_op jit(solution)/shard_map/ppermute | solution.py:137
  32.0 3.8 %collective-permute-done.4.rest_0_.rest_2_ = f32[328,128]{1,0:T(8,128)S(1)} collective-permute-done((f32[328,128]{1,0:T(8,128)S(1)}, f32[328,128]{1,0:T(8,128)S(1)}, u32[]{:S(2)}, u32[]{:S(2)}) %collective-permute-start.4) | collective-permute-done | bytes 167968 | tf_op jit(solution)/shard_map/ppermute | solution.py:137
  35.8 9.1 %shard_map.116 = (f32[2048,128]{1,0:T(8,128)S(1)}, f32[2048,128]{1,0:T(8,128)S(1)}, f32[240,128]{1,0:T(8,128)S(1)}) custom-call(s32[4]{0:T(128)S(1)} %pad_add_fusion.info, s32[3,40]{1,0:T(4,128)S(1)} %bitcast.33, s32[4,40]{1,0:T(4,128)S(1)} %bitcast.37, f32[40,8,4096]{2,1,0:T(8,128)S(1)} %bitcast.26, f32[72,128]{1,0:T(8,128)S(1)} %get-tuple-element.43.coef9, ...), custom_call_target="tpu_custom_call" | custom-call | tf_op jit(solution)/shard_map/pallas_call | solution.py:117
  44.9 1.9 %collective-permute-start.5 = (f32[240,128]{1,0:T(8,128)S(1)}, f32[240,128]{1,0:T(8,128)S(1)}, u32[]{:S(2)}, u32[]{:S(2)}) collective-permute-start(f32[240,128]{1,0:T(8,128)S(1)} %get-tuple-element.47), channel_id=1, source_target_pairs={{0,1},{1,0},{2,3},{3,2},{4,5},{5,4},{6,7},{7,6},{8,9},{9,8},{10,11... | collective-permute-start | bytes 368648 | tf_op jit(solution)/shard_map/ppermute | solution.py:137
  46.8 3.0 %collective-permute-done.5.rest_0_ = f32[240,128]{1,0:T(8,128)S(1)} collective-permute-done((f32[240,128]{1,0:T(8,128)S(1)}, f32[240,128]{1,0:T(8,128)S(1)}, u32[]{:S(2)}, u32[]{:S(2)}) %collective-permute-start.5) | collective-permute-done | bytes 122912 | tf_op jit(solution)/shard_map/ppermute | solution.py:137
  49.9 1.9 %shard_map.117 = (f32[2048,128]{1,0:T(8,128)S(1)}, f32[2048,128]{1,0:T(8,128)S(1)}, f32[440,128]{1,0:T(8,128)S(1)}, f32[440,128]{1,0:T(8,128)S(1)}) custom-call(s32[4]{0:T(128)S(1)} %pad_add_fusion.info, f32[2048,128]{1,0:T(8,128)S(1)} %get-tuple-element.45.p0_in, ...), custom_call_target="tpu_custom_call", output_to_operand_aliasing={{0}: (1, {}), {1}: (2, {})} | custom-call | tf_op jit(solution)/shard_map/pallas_call | solution.py:117
  51.7 0.1 collective-permute-start.6
  51.8 1.9 %collective-permute-start.7 = (f32[440,128]{1,0:T(8,128)S(1)}, f32[440,128]{1,0:T(8,128)S(1)}, u32[]{:S(2)}, u32[]{:S(2)}) collective-permute-start(f32[440,128]{1,0:T(8,128)S(1)} %get-tuple-element.51), channel_id=1, source_target_pairs={{2,4},{4,2},{3,5},{5,3},{10,12},{12,10},{11,13},{13,11},{18,20},{2... | collective-permute-start | bytes 675848 | tf_op jit(solution)/shard_map/ppermute | solution.py:137
  53.7 0.0 collective-permute-done.6.rest_0_
  53.7 5.4 %collective-permute-done.7.rest_1_ = f32[440,128]{1,0:T(8,128)S(1)} collective-permute-done((f32[440,128]{1,0:T(8,128)S(1)}, f32[440,128]{1,0:T(8,128)S(1)}, u32[]{:S(2)}, u32[]{:S(2)}) %collective-permute-start.7) | collective-permute-done | bytes 225312 | tf_op jit(solution)/shard_map/ppermute | solution.py:137
  59.1 1.2 shard_map.118
  60.3 4.7 %collective-permute-start.8 = (f32[488,128]{1,0:T(8,128)S(1)}, f32[488,128]{1,0:T(8,128)S(1)}, u32[]{:S(2)}, u32[]{:S(2)}) collective-permute-start(f32[488,128]{1,0:T(8,128)S(1)} %get-tuple-element.57), channel_id=1, source_target_pairs={{0,8},{16,24},{8,0},{24,16},{1,9},{17,25},{9,1},{25,17},{2,10},{18... | collective-permute-start | bytes 749576 | tf_op jit(solution)/shard_map/ppermute | solution.py:137
  65.1 1.9 %collective-permute-start.9 = (f32[488,128]{1,0:T(8,128)S(1)}, f32[488,128]{1,0:T(8,128)S(1)}, u32[]{:S(2)}, u32[]{:S(2)}) collective-permute-start(f32[488,128]{1,0:T(8,128)S(1)} %get-tuple-element.58), channel_id=1, source_target_pairs={{8,16},{16,8},{9,17},{17,9},{10,18},{18,10},{11,19},{19,11},{12,20... | collective-permute-start | bytes 749576 | tf_op jit(solution)/shard_map/ppermute | solution.py:137
  67.0 2.3 %collective-permute-done.8.rest_0_ = f32[488,128]{1,0:T(8,128)S(1)} collective-permute-done((f32[488,128]{1,0:T(8,128)S(1)}, f32[488,128]{1,0:T(8,128)S(1)}, u32[]{:S(2)}, u32[]{:S(2)}) %collective-permute-start.8) | collective-permute-done | bytes 249888 | tf_op jit(solution)/shard_map/ppermute | solution.py:137
  69.3 3.9 %collective-permute-done.9.rest_1_ = f32[488,128]{1,0:T(8,128)S(1)} collective-permute-done((f32[488,128]{1,0:T(8,128)S(1)}, f32[488,128]{1,0:T(8,128)S(1)}, u32[]{:S(2)}, u32[]{:S(2)}) %collective-permute-start.9) | collective-permute-done | bytes 249888 | tf_op jit(solution)/shard_map/ppermute | solution.py:137
  73.2 29.6 %shard_map.119 = (f32[1024,128]{1,0:T(8,128)S(1)}, f32[2560,128]{1,0:T(8,128)}, f32[640,128]{1,0:T(8,128)S(1)}, f32[256,128]{1,0:T(8,128)S(1)}, f32[240,128]{1,0:T(8,128)S(1)}) custom-call(s32[4]{0:T(128)S(1)} %pad_add_fusion.info, s32[3,40]{1,0:T(4,128)S(1)} %bitcast.34, f32[2048,128]{1,0:T(8,128)S(1)} %get-tuple-element.52.p0, ...), custom_call_target="tpu_custom_call" | custom-call | tf_op jit(solution)/shard_map/pallas_call | solution.py:117
  102.8 2.0 %collective-permute-start.10 = (f32[240,128]{1,0:T(8,128)S(1)}, f32[240,128]{1,0:T(8,128)S(1)}, u32[]{:S(2)}, u32[]{:S(2)}) collective-permute-start(f32[240,128]{1,0:T(8,128)S(1)} %get-tuple-element.60), channel_id=1, source_target_pairs={{0,1},{1,0},{2,3},{3,2},{4,5},{5,4},{6,7},{7,6},{8,9},{9,8},{10,11... | collective-permute-start | bytes 368648 | tf_op jit(solution)/shard_map/ppermute | solution.py:137
  104.8 2.9 %collective-permute-done.10.rest_0_ = f32[240,128]{1,0:T(8,128)S(1)} collective-permute-done((f32[240,128]{1,0:T(8,128)S(1)}, f32[240,128]{1,0:T(8,128)S(1)}, u32[]{:S(2)}, u32[]{:S(2)}) %collective-permute-start.10) | collective-permute-done | bytes 122912 | tf_op jit(solution)/shard_map/ppermute | solution.py:137
  107.7 0.8 shard_map.120
  108.5 0.1 collective-permute-start.11
  108.6 1.9 %collective-permute-start.12 = (f32[160,128]{1,0:T(8,128)S(1)}, f32[160,128]{1,0:T(8,128)S(1)}, u32[]{:S(2)}, u32[]{:S(2)}) collective-permute-start(f32[160,128]{1,0:T(8,128)S(1)} %get-tuple-element.63), channel_id=1, source_target_pairs={{2,4},{4,2},{3,5},{5,3},{10,12},{12,10},{11,13},{13,11},{18,20},{2... | collective-permute-start | bytes 245768 | tf_op jit(solution)/shard_map/ppermute | solution.py:137
  110.5 0.0 collective-permute-done.11.rest_1_
  110.6 3.8 %collective-permute-done.12.rest_2_ = f32[160,128]{1,0:T(8,128)S(1)} collective-permute-done((f32[160,128]{1,0:T(8,128)S(1)}, f32[160,128]{1,0:T(8,128)S(1)}, u32[]{:S(2)}, u32[]{:S(2)}) %collective-permute-start.12) | collective-permute-done | bytes 81952 | tf_op jit(solution)/shard_map/ppermute | solution.py:137
  114.4 0.7 shard_map.121
  115.1 11.0 %collective-permute-start.13 = (f32[128,128]{1,0:T(8,128)S(1)}, f32[128,128]{1,0:T(8,128)S(1)}, u32[]{:S(2)}, u32[]{:S(2)}) collective-permute-start(f32[128,128]{1,0:T(8,128)S(1)} %get-tuple-element.65), channel_id=1, source_target_pairs={{0,8},{16,24},{8,0},{24,16},{1,9},{17,25},{9,1},{25,17},{2,10},{18... | collective-permute-start | bytes 196616 | tf_op jit(solution)/shard_map/ppermute | solution.py:137
  126.1 1.9 %collective-permute-start.14 = (f32[128,128]{1,0:T(8,128)S(1)}, f32[128,128]{1,0:T(8,128)S(1)}, u32[]{:S(2)}, u32[]{:S(2)}) collective-permute-start(f32[128,128]{1,0:T(8,128)S(1)} %get-tuple-element.66), channel_id=1, source_target_pairs={{8,16},{16,8},{9,17},{17,9},{10,18},{18,10},{11,19},{19,11},{12,20... | collective-permute-start | bytes 196616 | tf_op jit(solution)/shard_map/ppermute | solution.py:137
  128.0 0.3 collective-permute-done.13.rest_3_
  128.3 3.9 %collective-permute-done.14.rest_4_ = f32[128,128]{1,0:T(8,128)S(1)} collective-permute-done((f32[128,128]{1,0:T(8,128)S(1)}, f32[128,128]{1,0:T(8,128)S(1)}, u32[]{:S(2)}, u32[]{:S(2)}) %collective-permute-start.14) | collective-permute-done | bytes 65568 | tf_op jit(solution)/shard_map/ppermute | solution.py:137
  132.2 1.8 %shard_map.122 = f32[1024,128]{1,0:T(8,128)} custom-call(s32[4]{0:T(128)S(1)} %pad_add_fusion.info, f32[1024,128]{1,0:T(8,128)S(1)} %get-tuple-element.59.core, f32[240,128]{1,0:T(8,128)S(1)} %collective-permute-done.10.rest_0_, f32[160,128]{1,0:T(8,128)S(1)} %collective-permute-done.11.rest_1_, f32[160,128]{1,0:T(8,128)S(1)} %collective-permute-done.12.rest_2_, ...), custom_call_target="tpu_custom_call" | custom-call | tf_op jit(solution)/shard_map/pallas_call | solution.py:117
  (12 shorter events, 0.0 us)
Async XLA Ops:
  0.6 31.3 %copy-start.8 = (s32[1,1,1,40,3]{3,2,4,1,0:T(1,128)S(1)}, s32[1,1,1,40,3]{3,2,4,1,0:T(1,128)}, u32[]{:S(2)}) copy-start(s32[1,1,1,40,3]{3,2,4,1,0:T(1,128)} %param.17) | copy-start | bytes 1444
  0.6 35.2 %copy-start.5 = (s32[1,1,1,40,4]{3,4,2,1,0:T(4,128)S(1)}, s32[1,1,1,40,4]{3,4,2,1,0:T(4,128)}, u32[]{:S(2)}) copy-start(s32[1,1,1,40,4]{3,4,2,1,0:T(4,128)} %param.16) | copy-start | bytes 1924
  0.7 35.1 %copy-start = (f32[1,1,1,40,8,4096]{5,4,3,2,1,0:T(8,128)S(1)}, f32[1,1,1,40,8,4096]{5,4,3,2,1,0:T(8,128)}, u32[]{:S(2)}) copy-start(f32[1,1,1,40,8,4096]{5,4,3,2,1,0:T(8,128)} %param.19) | copy-start | bytes 15728644
  1.5 1.5 %copy-start.1 = (f32[32,32,128]{2,1,0:T(8,128)S(1)}, f32[32,32,128]{2,1,0:T(8,128)}, u32[]{:S(2)}) copy-start(f32[32,32,128]{2,1,0:T(8,128)} %param.11) | copy-start | bytes 1572868
  3.0 1.0 copy-start.2
  4.1 1.0 copy-start.3
  5.1 0.7 copy-start.4
  5.8 0.7 copy-start.6
  6.4 0.7 copy-start.7
  8.4 7.1 %collective-permute-start = (f32[424,128]{1,0:T(8,128)S(1)}, f32[424,128]{1,0:T(8,128)S(1)}, u32[]{:S(2)}, u32[]{:S(2)}) collective-permute-start(f32[424,128]{1,0:T(8,128)S(1)} %get-tuple-element.35), channel_id=1, source_target_pairs={{0,8},{16,24},{8,0},{24,16},{1,9},{17,25},{9,1},{25,17},{2,10},{18... | collective-permute-start | bytes 651272 | tf_op jit(solution)/shard_map/ppermute | solution.py:137
  9.0 9.7 %collective-permute-start.1 = (f32[424,128]{1,0:T(8,128)S(1)}, f32[424,128]{1,0:T(8,128)S(1)}, u32[]{:S(2)}, u32[]{:S(2)}) collective-permute-start(f32[424,128]{1,0:T(8,128)S(1)} %get-tuple-element.36), channel_id=1, source_target_pairs={{8,16},{16,8},{9,17},{17,9},{10,18},{18,10},{11,19},{19,11},{12,20... | collective-permute-start | bytes 651272 | tf_op jit(solution)/shard_map/ppermute | solution.py:137
  19.9 2.6 %collective-permute-start.2 = (f32[576,128]{1,0:T(8,128)S(1)}, f32[576,128]{1,0:T(8,128)S(1)}, u32[]{:S(2)}, u32[]{:S(2)}) collective-permute-start(f32[576,128]{1,0:T(8,128)S(1)} %get-tuple-element.41), channel_id=1, source_target_pairs={{0,2},{4,6},{2,0},{6,4},{1,3},{5,7},{3,1},{7,5},{8,10},{12,14},{10... | collective-permute-start | bytes 884744 | tf_op jit(solution)/shard_map/ppermute | solution.py:137
  20.0 8.0 %collective-permute-start.3 = (f32[576,128]{1,0:T(8,128)S(1)}, f32[576,128]{1,0:T(8,128)S(1)}, u32[]{:S(2)}, u32[]{:S(2)}) collective-permute-start(f32[576,128]{1,0:T(8,128)S(1)} %get-tuple-element.42), channel_id=1, source_target_pairs={{2,4},{4,2},{3,5},{5,3},{10,12},{12,10},{11,13},{13,11},{18,20},{2... | collective-permute-start | bytes 884744 | tf_op jit(solution)/shard_map/ppermute | solution.py:137
  30.4 5.4 %collective-permute-start.4 = (f32[328,128]{1,0:T(8,128)S(1)}, f32[328,128]{1,0:T(8,128)S(1)}, u32[]{:S(2)}, u32[]{:S(2)}) collective-permute-start(f32[328,128]{1,0:T(8,128)S(1)} %get-tuple-element.44), channel_id=1, source_target_pairs={{0,1},{1,0},{2,3},{3,2},{4,5},{5,4},{6,7},{7,6},{8,9},{9,8},{10,11... | collective-permute-start | bytes 503816 | tf_op jit(solution)/shard_map/ppermute | solution.py:137
  44.9 4.9 %collective-permute-start.5 = (f32[240,128]{1,0:T(8,128)S(1)}, f32[240,128]{1,0:T(8,128)S(1)}, u32[]{:S(2)}, u32[]{:S(2)}) collective-permute-start(f32[240,128]{1,0:T(8,128)S(1)} %get-tuple-element.47), channel_id=1, source_target_pairs={{0,1},{1,0},{2,3},{3,2},{4,5},{5,4},{6,7},{7,6},{8,9},{9,8},{10,11... | collective-permute-start | bytes 368648 | tf_op jit(solution)/shard_map/ppermute | solution.py:137
  51.7 2.0 %collective-permute-start.6 = (f32[440,128]{1,0:T(8,128)S(1)}, f32[440,128]{1,0:T(8,128)S(1)}, u32[]{:S(2)}, u32[]{:S(2)}) collective-permute-start(f32[440,128]{1,0:T(8,128)S(1)} %get-tuple-element.50), channel_id=1, source_target_pairs={{0,2},{4,6},{2,0},{6,4},{1,3},{5,7},{3,1},{7,5},{8,10},{12,14},{10... | collective-permute-start | bytes 675848 | tf_op jit(solution)/shard_map/ppermute | solution.py:137
  51.8 7.3 %collective-permute-start.7 = (f32[440,128]{1,0:T(8,128)S(1)}, f32[440,128]{1,0:T(8,128)S(1)}, u32[]{:S(2)}, u32[]{:S(2)}) collective-permute-start(f32[440,128]{1,0:T(8,128)S(1)} %get-tuple-element.51), channel_id=1, source_target_pairs={{2,4},{4,2},{3,5},{5,3},{10,12},{12,10},{11,13},{13,11},{18,20},{2... | collective-permute-start | bytes 675848 | tf_op jit(solution)/shard_map/ppermute | solution.py:137
  60.3 8.9 %collective-permute-start.8 = (f32[488,128]{1,0:T(8,128)S(1)}, f32[488,128]{1,0:T(8,128)S(1)}, u32[]{:S(2)}, u32[]{:S(2)}) collective-permute-start(f32[488,128]{1,0:T(8,128)S(1)} %get-tuple-element.57), channel_id=1, source_target_pairs={{0,8},{16,24},{8,0},{24,16},{1,9},{17,25},{9,1},{25,17},{2,10},{18... | collective-permute-start | bytes 749576 | tf_op jit(solution)/shard_map/ppermute | solution.py:137
  65.1 8.1 %collective-permute-start.9 = (f32[488,128]{1,0:T(8,128)S(1)}, f32[488,128]{1,0:T(8,128)S(1)}, u32[]{:S(2)}, u32[]{:S(2)}) collective-permute-start(f32[488,128]{1,0:T(8,128)S(1)} %get-tuple-element.58), channel_id=1, source_target_pairs={{8,16},{16,8},{9,17},{17,9},{10,18},{18,10},{11,19},{19,11},{12,20... | collective-permute-start | bytes 749576 | tf_op jit(solution)/shard_map/ppermute | solution.py:137
  102.8 4.9 %collective-permute-start.10 = (f32[240,128]{1,0:T(8,128)S(1)}, f32[240,128]{1,0:T(8,128)S(1)}, u32[]{:S(2)}, u32[]{:S(2)}) collective-permute-start(f32[240,128]{1,0:T(8,128)S(1)} %get-tuple-element.60), channel_id=1, source_target_pairs={{0,1},{1,0},{2,3},{3,2},{4,5},{5,4},{6,7},{7,6},{8,9},{9,8},{10,11... | collective-permute-start | bytes 368648 | tf_op jit(solution)/shard_map/ppermute | solution.py:137
  108.5 2.0 %collective-permute-start.11 = (f32[160,128]{1,0:T(8,128)S(1)}, f32[160,128]{1,0:T(8,128)S(1)}, u32[]{:S(2)}, u32[]{:S(2)}) collective-permute-start(f32[160,128]{1,0:T(8,128)S(1)} %get-tuple-element.62), channel_id=1, source_target_pairs={{0,2},{4,6},{2,0},{6,4},{1,3},{5,7},{3,1},{7,5},{8,10},{12,14},{10... | collective-permute-start | bytes 245768 | tf_op jit(solution)/shard_map/ppermute | solution.py:137
  108.6 5.8 %collective-permute-start.12 = (f32[160,128]{1,0:T(8,128)S(1)}, f32[160,128]{1,0:T(8,128)S(1)}, u32[]{:S(2)}, u32[]{:S(2)}) collective-permute-start(f32[160,128]{1,0:T(8,128)S(1)} %get-tuple-element.63), channel_id=1, source_target_pairs={{2,4},{4,2},{3,5},{5,3},{10,12},{12,10},{11,13},{13,11},{18,20},{2... | collective-permute-start | bytes 245768 | tf_op jit(solution)/shard_map/ppermute | solution.py:137
  115.1 13.3 %collective-permute-start.13 = (f32[128,128]{1,0:T(8,128)S(1)}, f32[128,128]{1,0:T(8,128)S(1)}, u32[]{:S(2)}, u32[]{:S(2)}) collective-permute-start(f32[128,128]{1,0:T(8,128)S(1)} %get-tuple-element.65), channel_id=1, source_target_pairs={{0,8},{16,24},{8,0},{24,16},{1,9},{17,25},{9,1},{25,17},{2,10},{18... | collective-permute-start | bytes 196616 | tf_op jit(solution)/shard_map/ppermute | solution.py:137
  126.1 6.1 %collective-permute-start.14 = (f32[128,128]{1,0:T(8,128)S(1)}, f32[128,128]{1,0:T(8,128)S(1)}, u32[]{:S(2)}, u32[]{:S(2)}) collective-permute-start(f32[128,128]{1,0:T(8,128)S(1)} %get-tuple-element.66), channel_id=1, source_target_pairs={{8,16},{16,8},{9,17},{17,9},{10,18},{18,10},{11,19},{19,11},{12,20... | collective-permute-start | bytes 196616 | tf_op jit(solution)/shard_map/ppermute | solution.py:137
where the time goes:
time: 135 us; the launch traced here: 134 us
  Pallas kernels  50.1 us (37%)
  waiting for transfers between devices  39.9 us (30%)
  starting transfers between devices  36.8 us (27%)
  local copies, waits for them, and re-layouts  5.57 us (4%)
  between operations  1.62 us (1%)
    pallas_call x10, Pallas kernels, call(): pl.pallas_call(kernel, out_shape=outs, in_specs=specs, out_specs=jax.tree...  50.1 us
    ppermute x15, waiting for transfers between devices, swap(): lax.ppermute(slab, axis, pairs + [(j, i) for i, j in pairs])  39.9 us
    ppermute x15, starting transfers between devices, swap(): lax.ppermute(slab, axis, pairs + [(j, i) for i, j in pairs])  36.8 us
    unnamed x19, local copies, waits for them, and re-layouts  5.57 us
  transfers between devices with their start and end apart: 15, of which 12 were waited for; matrix products, arithmetic and copies ran while one was open for 0% of the time, Pallas kernels for 0%

commit v1 on v0

--- a/solution.py
+++ b/solution.py
@@ -92,6 +92,7 @@
         self.rows = self.blocks * GROUP * SUB
         self.live_x = bx + 2 * MARGIN
         self.live_blocks = self.live_x * self.tiles // GROUP
+        self.counts = counts
         self.sides = [1 if n == 2 else 2 for n in counts]
 
     @property
@@ -109,7 +110,7 @@
 
 VMEM = pl.BlockSpec(memory_space=pltpu.VMEM)
 SMEM = pl.BlockSpec(memory_space=pltpu.SMEM)
-HBM = pl.BlockSpec(memory_space=pl.ANY)
+HBM = pl.BlockSpec(memory_space=pltpu.HBM)
 
 
 def call(kernel, outs, ins, specs=(), scratch=(), alias=None, limit=12):
@@ -138,19 +139,22 @@
     return received
 
 
-def look_up(labels, values):
+def look_up(labels, values, which):
     out = jnp.zeros(labels.shape, F32)
-    for c in range(values.shape[0]):
-        out = out + jnp.where(labels == c, values[c], 0.0)
+    for c in range(values.shape[1]):
+        out = out + jnp.where(labels == c, values[which, c], 0.0)
     return out
 
 
-def static_x(fr, info, contrast, channel, kappa, labels, forcing, coef, *rest):
+def static_x(fr, info, contrast, channel, kappa, labels, forcing, *rest):
     n = fr.sides[0]
-    slabs, (k_buf, l_buf, sem) = rest[:n], rest[n:]
+    slabs, (k_buf, l_buf, t_buf, sem, t_sem) = rest[:n], rest[n:]
     by = fr.by
     f_row, w_row, c_row = H * by, (H + MARGIN) * by, (H + 2 * MARGIN) * by
-    copies = []
+    copies = [
+        pltpu.make_async_copy(contrast, t_buf.at[0], t_sem.at[0]),
+        pltpu.make_async_copy(channel, t_buf.at[1], t_sem.at[1]),
+    ]
     for i, slab in enumerate(slabs):
         lower = is_lower(info, 0, i)
         first = pl.multiple_of(pick(lower, (fr.bx - H) * by, 0), SUB)
@@ -165,23 +169,19 @@
             copies.append(pltpu.make_async_copy(src, dst, sem.at[i, j]))
     for copy in copies:
         copy.start()
-    for slab in slabs:
-        slab[c_row : c_row + SUB, :] = jnp.zeros((SUB, LANES), F32)
-        slab[c_row : c_row + coef.shape[0], 0 : coef.shape[1]] = coef[...]
     for copy in copies:
         copy.wait()
     for i, slab in enumerate(slabs):
         skip = pl.multiple_of(pick(is_lower(info, 0, i), by, 0), SUB)
-        slab[0:f_row, :] = k_buf[i] * look_up(l_buf[i], contrast)
-        slab[w_row:c_row, :] = look_up(l_buf[i, pl.ds(skip, MARGIN * by), :], channel)
-
-
-def static_y(fr, info, contrast, channel, kappa, labels, forcing, coef, *rest):
+        slab[0:f_row, :] = k_buf[i] * look_up(l_buf[i], t_buf, 0)
+        slab[w_row:c_row, :] = look_up(l_buf[i, pl.ds(skip, MARGIN * by), :], t_buf, 1)
+
+
+def static_y(fr, info, tables, kappa, labels, forcing, *rest):
     n = fr.sides[0]
-    received, (k0, f0, w0, coef3), slabs = rest[:n], rest[n : n + 4], rest[n + 4 :]
+    received, (k0, f0, w0), slabs = rest[:n], rest[n : n + 3], rest[n + 3 :]
     by, yf, w = fr.by, fr.yf, 2 * MARGIN + H
-    c_in = w * by
-    for ref in (k0, f0, w0, coef3):
+    for ref in (k0, f0, w0):
         zero(ref)
 
     def core(x):
@@ -189,12 +189,11 @@
             src = pl.ds(x * by + t * SUB, SUB)
             dst = pl.ds((x + H) * yf + TOP + t * SUB, SUB)
             label = labels[src, :]
-            k0[dst, :] = kappa[src, :] * look_up(label, contrast)
-            w0[dst, :] = look_up(label, channel)
+            k0[dst, :] = kappa[src, :] * look_up(label, tables, 0)
+            w0[dst, :] = look_up(label, tables, 1)
             f0[dst, :] = forcing[src, :]
 
     loop(fr.bx, core, 4)
-    coef3[SUB : SUB + coef.shape[0], 0 : coef.shape[1]] = coef[...]
     for i, buf in enumerate(received):
         lower = is_lower(info, 0, i)
         for frame, count, at, low in ((k0, H, 0, 0), (f0, MARGIN, H, 1), (w0, MARGIN, H + MARGIN, 1)):
@@ -203,7 +202,6 @@
                 for t in range(by // SUB):
                     row = (at + j) * by + t * SUB
                     frame[pl.ds(pl.multiple_of((first + j) * yf + TOP + t * SUB, SUB), SUB), :] = buf[row : row + SUB, :]
-        coef3[pl.ds(pl.multiple_of(pick(lower, 2 * SUB, 0), SUB), SUB), :] = buf[c_in : c_in + SUB, :]
 
     def plane(x):
         r, o = x * yf, x * w
@@ -214,18 +212,14 @@
                 slab[pl.ds(o + at, count), :] = frame[pl.ds(first, count), :]
 
     loop(fr.xf, plane, 6)
-    c_out = -(-fr.xf * w // SUB) * SUB
-    for slab in slabs:
-        slab[c_out : c_out + 3 * SUB, :] = coef3[...]
-
-
-def static_z(fr, info, k_in, f_in, w_in, coef3, *rest):
+
+
+def static_z(fr, info, k_in, f_in, w_in, *rest):
     n = fr.sides[1]
-    received, (k0, f0, w0, coef9), slabs = rest[:n], rest[n : n + 4], rest[n + 4 :]
+    received, (k0, f0, w0), slabs = rest[:n], rest[n : n + 3], rest[n + 3 :]
     del k_in, f_in, w_in
     _, lane = iotas()
     by, yf, w = fr.by, fr.yf, 2 * MARGIN + H
-    c_in = -(-fr.xf * w // SUB) * SUB
 
     def plane(x):
         r, o = x * yf, x * w
@@ -236,12 +230,6 @@
                 frame[pl.ds(first, count), :] = buf[pl.ds(o + at, count), :]
 
     loop(fr.xf, plane, 6)
-    zero(coef9)
-    for x in range(3):
-        coef9[(x * 3 + 1) * SUB : (x * 3 + 2) * SUB, :] = coef3[x * SUB : (x + 1) * SUB, :]
-        for i, buf in enumerate(received):
-            to = pl.multiple_of((x * 3 + pick(is_lower(info, 1, i), 2, 0)) * SUB, SUB)
-            coef9[pl.ds(to, SUB), :] = buf[c_in + x * SUB : c_in + (x + 1) * SUB, :]
     group = lane & (PIECE - 1)
 
     def block(b):
@@ -255,9 +243,6 @@
             slab[pl.ds(b * SUB, SUB), :] = mix
 
     loop(fr.blocks, block, 4)
-    c_out = fr.blocks * SUB
-    for slab in slabs:
-        slab[c_out : c_out + 9 * SUB, :] = coef9[...]
 
 
 def place_masks(z0, lane):
@@ -270,71 +255,85 @@
     return off[0, p] + 1, off[1, p] + TOP - MARGIN, off[2, p] - MARGIN
 
 
-def add_piece(fr, off, p, valid, values, lane, main_ref, beyond_ref):
-    x0, y0, z0 = corner(off, p)
+def piece_rows(fr, off, p):
+    x0, y0, _ = corner(off, p)
     base = x0 * fr.yf + y0
-    main, beyond = place_masks(z0, lane)
-    places = [pl.ds(base + (c // HALVES) * fr.yf + (c % HALVES) * SUB, SUB) for c in range(CHUNKS)]
+    return [pl.ds(base + (c // HALVES) * fr.yf + (c % HALVES) * SUB, SUB) for c in range(CHUNKS)]
+
+
+def add_main(fr, off, p, valid, values, lane, ref):
+    main, _ = place_masks(off[2, p] - MARGIN, lane)
     main = main & valid
-    new = [main_ref[a, :] + jnp.where(main, v, 0.0) for a, v in zip(places, values)]
+    places = piece_rows(fr, off, p)
+    new = [ref[a, :] + jnp.where(main, v, 0.0) for a, v in zip(places, values)]
     for a, v in zip(places, new):
-        main_ref[a, :] = v
+        ref[a, :] = v
+
+
+def add_beyond(fr, off, p, valid, get_values, lane, ref):
+    z0 = off[2, p] - MARGIN
 
     @pl.when(valid & ((z0 < 0) | (z0 + PIECE > LANES)))
     def _():
-        new = [beyond_ref[a, :] + jnp.where(beyond, v, 0.0) for a, v in zip(places, values)]
+        _, beyond = place_masks(z0, lane)
+        places = piece_rows(fr, off, p)
+        new = [ref[a, :] + jnp.where(beyond, v, 0.0) for a, v in zip(places, get_values())]
         for a, v in zip(places, new):
-            beyond_ref[a, :] = v
-
-
-def prolong(fr, shape, info, off, link, bases, coef9, *rest):
-    slots, nb, together = shape
-    n = fr.sides[2]
-    received, (p0, p1), slabs, (table, buf, sem) = rest[:n], rest[n : n + 2], rest[n + 2 : 2 * n + 2], rest[2 * n + 2 :]
+            ref[a, :] = v
+
+
+def stack(own, *rest):
+    received, out = rest[:-1], rest[-1]
+    zero(out)
+    count = own.shape[0]
+    for i, ref in enumerate((own, *received)):
+        out[i * count : (i + 1) * count, 0 : ref.shape[1]] = ref[...]
+
+
+def prolong(fr, shape, info, off, link, bases, own, *rest):
+    nb, together = shape
+    n, m = fr.sides[0], fr.sides[2]
+    received, (p0, p1), slabs, (table, keep) = rest[:n], rest[n : n + 2], rest[n + 2 : n + m + 2], rest[n + m + 2 :]
     sub, lane = iotas()
     live = info[0]
-
-    def start(p, _):
-        pltpu.make_async_copy(bases.at[p], buf.at[p], sem.at[p]).start()
-        return 0
-
-    lax.fori_loop(0, live, start, 0)
     zero(p0)
     zero(p1)
-    for xy in range(9):
-        table[xy * 3 + 1] = coef9[xy * SUB : (xy + 1) * SUB, :]
-        for i, part in enumerate(received):
-            at = (fr.blocks + xy) * SUB
-            table[xy * 3 + pick(is_lower(info, 2, i), 2, 0)] = part[at : at + SUB, :]
+    each = (1 + fr.sides[1]) * (1 + m)
+    for i, ref in enumerate((own, *received)):
+        for j in range(each):
+            table[i * each + j] = ref[j * SUB : (j + 1) * SUB, :]
+
+    def position(axis, step):
+        came = 1 + ((info[1 + axis] + jnp.where(step == 0, 1, 0)) & 1)
+        return jnp.where(step == 1, 0, came)
 
     def some(step, _):
-        numbers, valids, spread = [], [], []
-        for i in range(together):
-            p = step * together + i
-            valids.append(p < live)
-            numbers.append(p)
-
-            @pl.when(p < live)
-            def _():
-                pltpu.make_async_copy(bases.at[p], buf.at[p], sem.at[p]).wait()
-
+        numbers = [step * together + i for i in range(together)]
+        per = CHUNKS // SUB
+        rows = []
         for p in numbers:
-            row = table[(link[0, p] * 3 + link[1, p]) * 3 + link[2, p]]
+            at = [position(axis, link[axis, p]) for axis in range(3)]
+            row = table[(at[0] * (1 + fr.sides[1]) + at[1]) * (1 + m) + at[2]]
             coef = jnp.sum(jnp.where(lane == link[3, p], row, 0.0), axis=1, keepdims=True)
             coef = jnp.broadcast_to(coef, (SUB, LANES))[0:nb]
             for first in range(0, CHUNKS, SUB):
-                parts = [buf[p, :, c * LANES : (c + 1) * LANES] * coef for c in range(first, first + SUB)]
-                spread.append(sum_rows(parts, sub))
-        spread = block_transpose(spread, sub, lane)
-        per = CHUNKS // SUB
-        for i, (p, valid) in enumerate(zip(numbers, valids)):
+                parts = [bases[p, :, c * LANES : (c + 1) * LANES] * coef for c in range(first, first + SUB)]
+                rows.append(sum_rows(parts, sub))
+        rows = block_transpose(rows, sub, lane)
+        for i, v in enumerate(rows):
+            keep[i] = v
+
+        def placed(i, p):
             z0 = off[2, p] - MARGIN
-            values = [
-                pltpu.roll(rows, (z0 - PIECE * j + 2 * LANES) % LANES, 1)
-                for rows in spread[i * per : (i + 1) * per]
-                for j in range(SUB)
+            return [
+                pltpu.roll(keep[i * per + c // SUB], (z0 - PIECE * (c % SUB) + 2 * LANES) % LANES, 1)
+                for c in range(CHUNKS)
             ]
-            add_piece(fr, off, p, valid, values, lane, p0, p1)
+
+        for i, p in enumerate(numbers):
+            add_main(fr, off, p, p < live, placed(i, p), lane, p0)
+        for i, p in enumerate(numbers):
+            add_beyond(fr, off, p, p < live, functools.partial(placed, i, p), lane, p1)
         return 0
 
     lax.fori_loop(0, (live + together - 1) // together, some, 0)
@@ -434,34 +433,12 @@
             slab[main + b * SUB : main + (b + 1) * SUB, :] = pack_tiles(tiles, SUB, lane)
 
 
-def enrich(fr, info, off, p0, p1, k0, f0, w0, *rest):
-    n0, n2 = fr.sides[0], fr.sides[2]
-    x_in, z_in, rest = rest[:n0], rest[n0 : n0 + n2], rest[n0 + n2 :]
-    core, basis, y_edge, x_edge, slab = rest[:5]
-    c0, c1, k1, r0, r1, w1, q0, q1, kb, rb, wb, wt, base, va, vb = rest[5:]
-    sub, lane = iotas()
-    yf, tiles = fr.yf, fr.tiles
-    live = info[0]
-    main_rows = WIDE * yf
-    edge = (lane >= LANES - SUB) | (lane < SUB)
-
-    c0[...] = p0[...]
-    c1[...] = p1[...]
-    for i, buf in enumerate(x_in):
-        row = pl.multiple_of(pick(is_lower(info, 0, i), fr.xf - WIDE, 0) * yf, SUB)
-        a = pl.ds(row, main_rows)
-        c0[a, :] = c0[a, :] + buf[0:main_rows, :]
-        for b in range(-(-WIDE * tiles // GROUP)):
-            pack = buf[main_rows + b * SUB : main_rows + (b + 1) * SUB, :]
-            count = min(GROUP, WIDE * tiles - b * GROUP)
-            places = [pl.ds(row + (b * GROUP + j) * SUB, SUB) for j in range(count)]
-            values = [jnp.where(edge, unpack_tile(pack, j, LANES - SUB), 0.0) for j in range(count)]
-            for a, v in zip(places, [c1[a, :] + v for a, v in zip(places, values)]):
-                c1[a, :] = v
-
-    f1 = r1
-
-    def beyond_z(b):
+def beyond(fr, info, *rest):
+    n2 = fr.sides[2]
+    z_in, outs = rest[:n2], rest[n2:]
+    _, lane = iotas()
+
+    def block(b):
         sums = [[0.0] * GROUP for _ in range(3)]
         for i, buf in enumerate(z_in):
             lower = is_lower(info, 2, i)
@@ -472,76 +449,48 @@
                 keep = (lane >= low) & (lane < low + width)
                 for j in range(GROUP):
                     sums[m][j] = sums[m][j] + jnp.where(keep, unpack_tile(pack, j, shift), 0.0)
-        for j in range(GROUP):
-            at = pl.ds((b * GROUP + j) * SUB, SUB)
-            k1[at, :] = sums[0][j]
-            f1[at, :] = sums[1][j]
-            w1[at, :] = sums[2][j]
-            c0[at, :] = jnp.where(k0[at, :] > 0, c0[at, :], 0.0)
-            c1[at, :] = jnp.where(sums[0][j] > 0, c1[at, :], 0.0)
-
-    loop(fr.blocks, beyond_z, 2)
-
-    def next_z(a, b):
-        return pltpu.roll(jnp.where(lane == 0, b, a), LANES - 1, 1)
-
-    def last_z(a, b):
-        return pltpu.roll(jnp.where(lane == LANES - 1, b, a), 1, 1)
-
-    def residual(x):
-        r = (x + 1) * yf
-        for t in range(tiles):
-            at = pl.ds(r + t * SUB, SUB)
-            for c, k, f, oc, ok, out in ((c0, k0, f0, c1, k1, r0), (c1, k1, f1, c0, k0, r1)):
-                cc, kc = c[at, :], k[at, :]
-                total = jnp.zeros((SUB, LANES), F32)
-                beside = [
-                    (c[pl.ds(r + t * SUB + d, SUB), :], k[pl.ds(r + t * SUB + d, SUB), :])
-                    for d in (-yf, yf, -1, 1)
-                ]
-                beside += [(next_z(cc, oc[at, :]), next_z(kc, ok[at, :]))]
-                beside += [(last_z(cc, oc[at, :]), last_z(kc, ok[at, :]))]
-                for cn, kn in beside:
-                    total = total + jnp.where(kn > 0, 0.5 * (kc + kn), kc) * (cc - cn)
-                out[at, :] = jnp.where(kc > 0, f[at, :] - total, 0.0)
-
-    loop(fr.live_x, residual, 1)
-
-    zero(q0)
-    zero(q1)
-    for ref in (kb, va, vb):
-        zero(ref)
-
+        for m, out in enumerate(outs):
+            for j in range(GROUP):
+                out[pl.ds((b * GROUP + j) * SUB, SUB), :] = sums[m][j]
+
+    loop(fr.blocks, block, 4)
+
+
+def gather_group(fr, off, first, live, fields, lane):
+    places = []
+    for g in range(GROUP):
+        x0, y0, z0 = corner(off, first + g)
+        slot = jnp.where(first + g < live, g, -1)
+        places.append((x0 * fr.yf + y0, z0, (g * PIECE - z0 + LANES) % LANES, slot))
+
+    def tiles_at(x, h):
+        accs = [jnp.zeros((SUB, LANES), F32) for _ in fields]
+        for base, z0, shift, slot in places:
+            at = pl.ds(base + x * fr.yf + h * SUB, SUB)
+            main = (lane >= z0) & (lane < z0 + PIECE)
+            keep = (lane >> 4) == slot
+            for j, (a, b) in enumerate(fields):
+                v = pltpu.roll(jnp.where(main, a[at, :], b[at, :]), shift, 1)
+                accs[j] = jnp.where(keep, v, accs[j])
+        return accs
+
+    return tiles_at
+
+
+def couple(fr, info, off, k0, k1, w0, w1, wt, scales, weights, kb):
+    sub, lane = iotas()
+    live = info[0]
     first_y, last_y = sub == 0, sub == SUB - 1
     z_cell = lane & (PIECE - 1)
-
-    def tent(t):
-        return (t + 0.5) * (PIECE - t - 0.5) * (4.0 / (PIECE * PIECE))
+    zero(kb)
 
     def one_group(group, _):
-        first = group * GROUP
-        bases, shifts, spans, slots = [], [], [], []
-        for g in range(GROUP):
-            x0, y0, z0 = corner(off, first + g)
-            bases.append(x0 * yf + y0)
-            shifts.append((g * PIECE - z0 + LANES) % LANES)
-            spans.append(z0)
-            slots.append(jnp.where(first + g < live, g, -1))
+        tiles_at = gather_group(fr, off, group * GROUP, live, ((k0, k1), (w0, w1)), lane)
 
         def gather(x):
             for h in range(HALVES):
-                accs = [jnp.zeros((SUB, LANES), F32) for _ in range(3)]
-                for g in range(GROUP):
-                    at = pl.ds(bases[g] + x * yf + h * SUB, SUB)
-                    main = (lane >= spans[g]) & (lane < spans[g] + PIECE)
-                    keep = (lane >> 4) == slots[g]
-                    for j, (a, b) in enumerate(((k0, k1), (r0, r1), (w0, w1))):
-                        v = pltpu.roll(jnp.where(main, a[at, :], b[at, :]), shifts[g], 1)
-                        accs[j] = jnp.where(keep, v, accs[j])
                 r = x * PIECE + h * SUB
-                kb[pl.ds(PIECE + r, SUB), :] = accs[0]
-                rb[pl.ds(r, SUB), :] = accs[1]
-                wb[pl.ds(r, SUB), :] = accs[2]
+                kb[pl.ds(PIECE + r, SUB), :], weights[group, pl.ds(r, SUB), :] = tiles_at(x, h)
 
         loop(PIECE, gather, 4)
 
@@ -566,22 +515,131 @@
                 inside = kc > 0
                 scale = jnp.where(inside, DAMPING / jnp.where(inside, diag, 1.0), 0.0)
                 for j, face in enumerate(faces):
-                    wt[j, pl.ds(r, SUB), :] = face * scale
-                s = rb[pl.ds(r, SUB), :] * scale
-                s2 = s * wb[pl.ds(r, SUB), :]
-                base[0, pl.ds(r, SUB), :] = s
-                base[1, pl.ds(r, SUB), :] = s2
-                va[0, pl.ds(PIECE + r, SUB), :] = s
-                va[1, pl.ds(PIECE + r, SUB), :] = s2
+                    wt[group, j, pl.ds(r, SUB), :] = face * scale
+                scales[group, pl.ds(r, SUB), :] = scale
 
         loop(PIECE, setup, 8)
-
-        def sweep(src, dst):
+        return 0
+
+    lax.fori_loop(0, (live + GROUP - 1) // GROUP, one_group, 0)
+
+
+def enrich(fr, info, off, p0, p1, k0, f0, k1, f1, wt, scales, weights, *rest):
+    n0 = fr.sides[0]
+    x_in, rest = rest[:n0], rest[n0:]
+    core, solved, y_edge, x_edge, slab = rest[:5]
+    c0, c1, r0, r1, q0, q1, rb, base, va, vb, here = rest[5:]
+    sub, lane = iotas()
+    yf, tiles = fr.yf, fr.tiles
+    live = info[0]
+    main_rows = WIDE * yf
+    edge = (lane >= LANES - SUB) | (lane < SUB)
+
+    c0[...] = p0[...]
+    c1[...] = p1[...]
+    for i, buf in enumerate(x_in):
+        row = pl.multiple_of(pick(is_lower(info, 0, i), fr.xf - WIDE, 0) * yf, SUB)
+        a = pl.ds(row, main_rows)
+        c0[a, :] = c0[a, :] + buf[0:main_rows, :]
+        for b in range(-(-WIDE * tiles // GROUP)):
+            pack = buf[main_rows + b * SUB : main_rows + (b + 1) * SUB, :]
+            count = min(GROUP, WIDE * tiles - b * GROUP)
+            places = [pl.ds(row + (b * GROUP + j) * SUB, SUB) for j in range(count)]
+            values = [jnp.where(edge, unpack_tile(pack, j, LANES - SUB), 0.0) for j in range(count)]
+            for a, v in zip(places, [c1[a, :] + v for a, v in zip(places, values)]):
+                c1[a, :] = v
+
+    def mask(b):
+        for j in range(GROUP):
+            at = pl.ds((b * GROUP + j) * SUB, SUB)
+            c0[at, :] = jnp.where(k0[at, :] > 0, c0[at, :], 0.0)
+            c1[at, :] = jnp.where(k1[at, :] > 0, c1[at, :], 0.0)
+
+    loop(fr.blocks, mask, 4)
+
+    def next_z(a, b):
+        return pltpu.roll(jnp.where(lane == 0, b, a), LANES - 1, 1)
+
+    def last_z(a, b):
+        return pltpu.roll(jnp.where(lane == LANES - 1, b, a), 1, 1)
+
+    def at_edge(axis, count, first, last, position):
+        low = (position == first) & (info[1 + axis] == 0)
+        high = (position == last) & (info[1 + axis] == count - 1)
+        return jnp.where(low, 1.0, 0.0) + jnp.where(high, 1.0, 0.0)
+
+    out_y = [at_edge(1, fr.counts[1], TOP, TOP + fr.by - 1, sub + t * SUB) for t in range(tiles)]
+    out_z = at_edge(2, fr.counts[2], 0, LANES - 1, lane)
+
+    def flux_x(x):
+        fluxes = []
+        for t in range(tiles):
+            at, to = pl.ds(x * yf + t * SUB, SUB), pl.ds((x + 1) * yf + t * SUB, SUB)
+            fluxes += [(k[at, :] + k[to, :]) * (c[at, :] - c[to, :]) for c, k in ((c0, k0), (c1, k1))]
+        return fluxes
+
+    def residual(x, before):
+        r = x * yf
+        after = flux_x(x)
+        out_x = at_edge(0, fr.counts[0], H, H + fr.bx - 1, x)
+        last_y = [jnp.zeros((SUB, LANES), F32)] * 2
+        for t in range(tiles):
+            at, to = pl.ds(r + t * SUB, SUB), pl.ds(r + t * SUB + 1, SUB)
+            cs, ks = (c0[at, :], c1[at, :]), (k0[at, :], k1[at, :])
+            fz = []
+            for i in range(2):
+                cn, kn = next_z(cs[i], cs[1 - i]), next_z(ks[i], ks[1 - i])
+                fz.append((ks[i] + kn) * (cs[i] - cn))
+            for i, (c, k, f, out) in enumerate(((c0, k0, f0, r0), (c1, k1, f1, r1))):
+                fy = pltpu.roll((ks[i] + k[to, :]) * (cs[i] - c[to, :]), 1, 0)
+                fy_next = (ks[i] + k[to, :]) * (cs[i] - c[to, :])
+                fy_last = jnp.where(sub == 0, last_y[i], fy)
+                last_y[i] = fy
+                outside = out_x + out_y[t] + (out_z if i == 0 else 0.0)
+                total = (after[2 * t + i] - before[2 * t + i]) + (fy_next - fy_last)
+                total = total + (fz[i] - last_z(fz[i], fz[1 - i])) + outside * (ks[i] * cs[i])
+                out[at, :] = jnp.where(ks[i] > 0, f[at, :] - 0.5 * total, 0.0)
+        return tuple(after)
+
+    def residuals(i, before):
+        for j in range(4):
+            before = residual(4 * i + j + 1, before)
+        return before
+
+    lax.fori_loop(0, fr.live_x // 4, residuals, tuple(flux_x(0)))
+
+    zero(q0)
+    zero(q1)
+    for ref in (va, vb):
+        zero(ref)
+
+    z_cell = lane & (PIECE - 1)
+    tz = tent(z_cell.astype(F32))
+    ty = [tent(sub.astype(F32) + float(SUB * h)) * tz for h in range(HALVES)]
+
+    def one_group(group, _):
+        first = group * GROUP
+        tiles_at = gather_group(fr, off, first, live, ((r0, r1),), lane)
+
+        def gather(x):
+            for h in range(HALVES):
+                r = x * PIECE + h * SUB
+                at = pl.ds(r, SUB)
+                s = tiles_at(x, h)[0] * scales[group, at, :]
+                s2 = s * weights[group, at, :]
+                for i, v in enumerate((s, s2)):
+                    base[i, at, :] = v
+                    va[i, pl.ds(PIECE + r, SUB), :] = v
+
+        loop(PIECE, gather, 8)
+        here[...] = wt[group]
+
+        def sweep(src, dst, out=None):
             for x in range(PIECE):
                 for h in range(HALVES):
                     r = x * PIECE + h * SUB
                     a = PIECE + r
-                    w = [wt[j, r : r + SUB, :] for j in range(6)]
+                    w = [here[j, r : r + SUB, :] for j in range(6)]
                     for s in range(2):
                         v = src[s, a : a + SUB, :]
                         total = base[s, r : r + SUB, :] + v * (1.0 - DAMPING)
@@ -593,49 +651,39 @@
                         total = total + w[3] * src[s, a - 1 : a - 1 + SUB, :]
                         total = total + w[4] * pltpu.roll(v, LANES - 1, 1)
                         total = total + w[5] * pltpu.roll(v, 1, 1)
-                        dst[s, a : a + SUB, :] = total
+                        if out is None:
+                            dst[s, a : a + SUB, :] = total
+                        else:
+                            out[group, s, r : r + SUB, :] = total
 
         def two(i, _):
             sweep(va, vb)
             sweep(vb, va)
             return 0
 
-        lax.fori_loop(0, (SWEEPS - 1) // 2, two, 0)
-        if (SWEEPS - 1) % 2:
+        lax.fori_loop(0, (SWEEPS - 2) // 2, two, 0)
+        if SWEEPS % 2:
             sweep(va, vb)
-            done = vb
+            sweep(vb, None, solved)
         else:
-            done = va
-
-        tz = tent(z_cell.astype(F32))
-        ty = [tent(sub.astype(F32) + float(SUB * h)) * tz for h in range(HALVES)]
-        for c in range(0, CHUNKS, SUB):
-            values = []
-            for i in range(SUB):
-                r = (c + i) * SUB
-                v0, v1 = done[0, PIECE + r : PIECE + r + SUB, :], done[1, PIECE + r : PIECE + r + SUB, :]
-                rb[r : r + SUB, :] = (v0 + v1) * (ty[(c + i) % HALVES] * float(tent((c + i) // HALVES)))
-                values += [v0, v1]
-            for i, v in enumerate(block_transpose(values, sub, lane)):
-                at = first * CHUNKS * 2 + c * 2 + i
-                basis[pl.ds(at, GROUP, stride=CHUNKS * 2), :] = v
+            sweep(va, None, solved)
+
+        for c in range(CHUNKS):
+            a = slice(c * SUB, (c + 1) * SUB)
+            weight = ty[c % HALVES] * float(tent(c // HALVES))
+            rb[a, :] = (solved[group, 0, a, :] + solved[group, 1, a, :]) * weight
+
+        def placed(g):
+            shift = (off[2, first + g] - MARGIN - g * PIECE + 2 * LANES) % LANES
+            return [pltpu.roll(rb[c * SUB : (c + 1) * SUB, :], shift, 1) for c in range(CHUNKS)]
 
         for g in range(GROUP):
-            z0 = off[2, first + g] - MARGIN
-            shift = (z0 - g * PIECE + 2 * LANES) % LANES
-            values = [pltpu.roll(rb[c * SUB : (c + 1) * SUB, :], shift, 1) for c in range(CHUNKS)]
-            add_piece(fr, off, first + g, first + g < live, values, lane, q0, q1)
+            add_main(fr, off, first + g, first + g < live, placed(g), lane, q0)
+        for g in range(GROUP):
+            add_beyond(fr, off, first + g, first + g < live, functools.partial(placed, g), lane, q1)
         return 0
 
-    groups = (live + GROUP - 1) // GROUP
-    lax.fori_loop(0, groups, one_group, 0)
-
-    def clear(group, _):
-        count = GROUP * CHUNKS * 2
-        basis[pl.ds(pl.multiple_of(group * count, SUB), count), :] = jnp.zeros((count, LANES), F32)
-        return 0
-
-    lax.fori_loop(groups, basis.shape[0] // (GROUP * CHUNKS * 2), clear, 0)
+    lax.fori_loop(0, (live + GROUP - 1) // GROUP, one_group, 0)
 
     def block(b):
         part = [q1[pl.ds(yf + (b * GROUP + j) * SUB, SUB), :] for j in range(GROUP)]
@@ -658,6 +706,33 @@
     for i, x in enumerate(edge_planes(fr)):
         row = (x + 1) * yf + TOP
         x_edge[i * fr.by : (i + 1) * fr.by, :] = q0[row : row + fr.by, :]
+
+
+def tent(t):
+    return (t + 0.5) * (PIECE - t - 0.5) * (4.0 / (PIECE * PIECE))
+
+
+def lay_out(info, solved, basis):
+    sub, lane = iotas()
+    groups = (info[0] + GROUP - 1) // GROUP
+    count = GROUP * CHUNKS * 2
+
+    def one_group(group, _):
+        for c in range(0, CHUNKS, SUB):
+            values = []
+            for i in range(c, c + SUB):
+                values += [solved[group, s, i * SUB : (i + 1) * SUB, :] for s in range(2)]
+            for i, v in enumerate(block_transpose(values, sub, lane)):
+                basis[pl.ds(group * count + c * 2 + i, GROUP, stride=CHUNKS * 2), :] = v
+        return 0
+
+    lax.fori_loop(0, groups, one_group, 0)
+
+    def clear(group, _):
+        basis[pl.ds(pl.multiple_of(group * count, SUB), count), :] = jnp.zeros((count, LANES), F32)
+        return 0
+
+    lax.fori_loop(groups, basis.shape[0] // count, clear, 0)
 
 
 def edge_planes(fr):
@@ -769,51 +844,61 @@
     bases = resident_bases.reshape(slots, nb, cells)
     raw = [a.reshape(bx * by, bz) for a in (kappa_base, labels, forcing)]
 
+    def stacked(own, received):
+        return call(stack, rows_of(own.shape[0] * (1 + len(received))), [own, *received], limit=4)
+
+    after_z = swap("gz", [coef] * n2)
     width = 2 * MARGIN + H
-    slab = rows_of(width * by + SUB)
+    slab = rows_of(width * by)
     slabs = call(
         part(static_x, fr),
         [slab] * n0,
-        [info, contrast, channel_weight, *raw, coef],
-        [SMEM] * 3 + [HBM] * 3,
+        [info, contrast, channel_weight, *raw],
+        [SMEM] + [HBM] * 5,
         [
             pltpu.VMEM((n0, H * by, LANES), F32),
             pltpu.VMEM((n0, H * by, LANES), jnp.int32),
+            pltpu.SMEM((2, contrast.shape[0]), F32),
             pltpu.SemaphoreType.DMA((n0, 3)),
+            pltpu.SemaphoreType.DMA((2,)),
         ],
     )
-    received = swap("gx", slabs)
-    slab = rows_of(-(-fr.xf * width // SUB) * SUB + 3 * SUB)
-    k0, f0, w0, coef3, *slabs = call(
+    after_z, slabs = lax.optimization_barrier((after_z, slabs))
+    coef = stacked(coef, after_z)
+    after_y = swap("gy", [coef] * n1)
+    static_x_in = swap("gx", slabs)
+    coef = stacked(coef, after_y)
+    after_x = swap("gx", [coef] * n0)
+    tables, raw, _ = lax.optimization_barrier((jnp.stack([contrast, channel_weight]), raw, slabs))
+    slab = rows_of(fr.xf * width)
+    k0, f0, w0, *slabs = call(
         part(static_y, fr),
-        [fr.frame] * 3 + [rows_of(3 * SUB)] + [slab] * n1,
-        [info, contrast, channel_weight, *raw, coef, *received],
+        [fr.frame] * 3 + [slab] * n1,
+        [info, tables, *raw, *static_x_in],
+        [SMEM] * 2,
+    )
+    after_x, slabs = lax.optimization_barrier((after_x, slabs))
+    static_y_in = swap("gy", slabs)
+
+    together = 4 if slots % 4 == 0 else 1
+    p0, p1, *slabs = call(
+        part(prolong, fr, (nb, together)),
+        [fr.frame] * 2 + [rows_of(live_rows)] * n2,
+        [info, off, link, bases, coef, *after_x],
         [SMEM] * 3,
-    )
-    received = swap("gy", slabs)
-    slab = rows_of((fr.blocks + 9) * SUB)
-    k0, f0, w0, coef9, *slabs = call(
+        [pltpu.VMEM((27, SUB, LANES), F32), pltpu.VMEM((together * CHUNKS // SUB, SUB, LANES), F32)],
+        limit=16,
+    )
+    received = swap("gz", slabs)
+    k0, f0, w0, *slabs = call(
         part(static_z, fr),
-        [fr.frame] * 3 + [rows_of(9 * SUB)] + [slab] * n2,
-        [info, k0, f0, w0, coef3, *received],
+        [fr.frame] * 3 + [rows_of(fr.blocks * SUB)] * n2,
+        [info, k0, f0, w0, *static_y_in],
         [SMEM],
         alias={1: 0, 2: 1, 3: 2},
     )
+    received, slabs = lax.optimization_barrier((received, slabs))
     static_z_in = swap("gz", slabs)
-
-    p0, p1, *slabs = call(
-        part(prolong, fr, (slots, nb, 4 if slots % 4 == 0 else 1)),
-        [fr.frame] * 2 + [rows_of(live_rows)] * n2,
-        [info, off, link, bases, coef9, *static_z_in],
-        [SMEM] * 3 + [HBM],
-        [
-            pltpu.VMEM((27, SUB, LANES), F32),
-            pltpu.VMEM((slots, nb, cells), F32),
-            pltpu.SemaphoreType.DMA((slots,)),
-        ],
-        limit=16,
-    )
-    received = swap("gz", slabs)
     p0, p1, *slabs = call(
         part(coarse_y, fr),
         [fr.frame] * 2 + [rows_of(fr.live_x * (WIDE + 2))] * n1,
@@ -822,6 +907,8 @@
         alias={1: 0, 2: 1},
     )
     received = swap("gy", slabs)
+    k1, f1, w1 = call(part(beyond, fr), [fr.frame] * 3, [info, *static_z_in], [SMEM])
+    received, k1 = lax.optimization_barrier((received, k1))
     p0, p1, *slabs = call(
         part(coarse_x, fr),
         [fr.frame] * 2 + [rows_of(WIDE * fr.yf + -(-WIDE * fr.tiles // GROUP) * SUB)] * n0,
@@ -830,34 +917,40 @@
         alias={1: 0, 2: 1},
     )
     received = swap("gx", slabs)
-
-    frame = pltpu.VMEM((fr.rows, LANES), F32)
-    padded = PROWS + 2 * PIECE
-    core, basis, y_edge, x_edge, slab = call(
+    groups = slots // GROUP
+    wt, scales, weights = call(
+        part(couple, fr),
+        [
+            jax.ShapeDtypeStruct((groups, 6, PROWS, LANES), F32),
+            jax.ShapeDtypeStruct((groups, PROWS, LANES), F32),
+            jax.ShapeDtypeStruct((groups, PROWS, LANES), F32),
+        ],
+        [info, off, k0, k1, w0, w1],
+        [SMEM] * 2,
+        [pltpu.VMEM((PROWS + 2 * PIECE, LANES), F32)],
+        limit=16,
+    )
+
+    solve = pltpu.VMEM((2, PROWS, LANES), F32)
+    padded = pltpu.VMEM((2, PROWS + 2 * PIECE, LANES), F32)
+    core, solved, y_edge, x_edge, slab = call(
         part(enrich, fr),
         [
             rows_of(bx * by),
-            rows_of(slots * CHUNKS * 2),
+            jax.ShapeDtypeStruct((groups, 2, PROWS, LANES), F32),
             rows_of(fr.live_x * 2 * SUB),
             rows_of(2 * MARGIN * by),
             rows_of(live_rows),
         ],
-        [info, off, p0, p1, k0, f0, w0, *received, *static_z_in],
+        [info, off, p0, p1, k0, f0, k1, f1, wt, scales, weights, *received],
         [SMEM] * 2,
-        [frame] * 8
-        + [
-            pltpu.VMEM((padded, LANES), F32),
-            pltpu.VMEM((PROWS, LANES), F32),
-            pltpu.VMEM((PROWS, LANES), F32),
-            pltpu.VMEM((6, PROWS, LANES), F32),
-            pltpu.VMEM((2, PROWS, LANES), F32),
-            pltpu.VMEM((2, padded, LANES), F32),
-            pltpu.VMEM((2, padded, LANES), F32),
-        ],
+        [pltpu.VMEM((fr.rows, LANES), F32)] * 6 + [pltpu.VMEM((PROWS, LANES), F32), solve, padded, padded, pltpu.VMEM((6, PROWS, LANES), F32)],
         limit=32,
     )
 
     z_in = swap("gz", [slab] * n2)
+    basis = call(lay_out, rows_of(slots * CHUNKS * 2), [info, solved], [SMEM])
+    z_in, basis = lax.optimization_barrier((z_in, basis))
     slabs = call(
         part(fold_y, fr),
         [rows_of(fr.live_x * MARGIN)] * n1,

time: 135 us -> 114 us (0.84)
  waiting for transfers between devices: 39.9 us -> 17.5 us
  Pallas kernels: 50.1 us -> 38.4 us
  local copies, waits for them, and re-layouts: 5.57 us -> 12.1 us
  starting transfers between devices: 36.8 us -> 42.1 us
    ppermute x15 -> x20, waiting for transfers between devices: 39.9 us -> 17.5 us  [swap(): lax.ppermute(slab, axis, pairs + [(j, i) for i, j in pairs])]
    pallas_call x10 -> x15, Pallas kernels: 50.1 us -> 38.4 us  [call(): pl.pallas_call(kernel, out_shape=outs, in_specs=specs, out_specs=jax.tree...]
    unnamed x19 -> x23, local copies, waits for them, and re-layouts: 5.57 us -> 12.1 us
    ppermute x15 -> x20, starting transfers between devices: 36.8 us -> 42.1 us  [swap(): lax.ppermute(slab, axis, pairs + [(j, i) for i, j in pairs])]
  transfers between devices with their start and end apart: 15 -> 20, of which waited for: 12 -> 7; matrix products, arithmetic and copies ran while one was open for 0% -> 1% of each run, Pallas kernels for 0% -> 16%
where the time goes in v1:
time: 114 us; the launch traced here: 112 us
  starting transfers between devices  42.1 us (37%)
  Pallas kernels  38.4 us (34%)
  waiting for transfers between devices  17.5 us (15%)
  local copies, waits for them, and re-layouts  12.1 us (11%)
  between operations  1.61 us (1%)
    ppermute x20, starting transfers between devices, swap(): lax.ppermute(slab, axis, pairs + [(j, i) for i, j in pairs])  42.1 us
    pallas_call x15, Pallas kernels, call(): pl.pallas_call(kernel, out_shape=outs, in_specs=specs, out_specs=jax.tree...  38.4 us
    ppermute x20, waiting for transfers between devices, swap(): lax.ppermute(slab, axis, pairs + [(j, i) for i, j in pairs])  17.5 us
    unnamed x23, local copies, waits for them, and re-layouts  12.1 us
  transfers between devices with their start and end apart: 20, of which 7 were waited for; matrix products, arithmetic and copies ran while one was open for 1% of the time, Pallas kernels for 16%

profile of v1, /device:TPU:10, one launch (start us, length us, event | category | flops | bytes accessed | tf_op | source)
XLA Modules:
  0.0 111.8 jit_solution(11984957938111155105)
XLA Ops:
  0.6 1.6 %collective-permute-start = (f32[8,64]{1,0:T(8,128)}, f32[8,64]{1,0:T(8,128)S(1)}, u32[]{:S(2)}, u32[]{:S(2)}) collective-permute-start(f32[8,64]{1,0:T(8,128)} %bitcast.38), channel_id=1, source_target_pairs={{0,1},{1,0},{2,3},{3,2},{4,5},{5,4},{6,7},{7,6},{8,9},{9,8},{10,11... | collective-permute-start | bytes 6152 | tf_op jit(solution)/shard_map/ppermute | solution.py:138
  2.9 0.1 pad_add_fusion.info
  2.9 1.0 copy-done.1
  4.0 1.0 copy-done.3
  5.0 1.0 copy-done.5
  6.1 0.7 copy-done.8
  6.7 0.7 copy-done.9
  7.4 1.4 %shard_map.113 = (f32[416,128]{1,0:T(8,128)S(1)}, f32[416,128]{1,0:T(8,128)S(1)}) custom-call(s32[4]{0:T(128)S(1)} %pad_add_fusion.info, f32[4]{0:T(128)S(1)} %copy-done.9, f32[4]{0:T(128)S(1)} %copy-done.8, f32[1024,128]{1,0:T(8,128)S(1)} %bitcast.29, s32[1024,128]{1,0:T(8,128)S(1)} %bitcast.31, f32[1024,128]{1,0:T(8,128)S(1)} %bitcast.33), custom_call_target="tpu_custom_call" | custom-call | tf_op jit(solution)/shard_map/pallas_call | solution.py:118
  8.8 0.5 collective-permute-start.5
  9.3 4.6 %collective-permute-start.6 = (f32[416,128]{1,0:T(8,128)S(1)}, f32[416,128]{1,0:T(8,128)S(1)}, u32[]{:S(2)}, u32[]{:S(2)}) collective-permute-start(f32[416,128]{1,0:T(8,128)S(1)} %get-tuple-element.61), channel_id=1, source_target_pairs={{8,16},{16,8},{9,17},{17,9},{10,18},{18,10},{11,19},{19,11},{12,20... | collective-permute-start | bytes 638984 | tf_op jit(solution)/shard_map/ppermute | solution.py:138
  13.9 0.7 copy-done.7
  14.6 1.9 %collective-permute-start.2 = (f32[16,128]{1,0:T(8,128)S(1)}, f32[16,128]{1,0:T(8,128)S(1)}, u32[]{:S(2)}, u32[]{:S(2)}) collective-permute-start(f32[16,128]{1,0:T(8,128)S(1)} %shard_map.114.own), channel_id=1, source_target_pairs={{2,4},{4,2},{3,5},{5,3},{10,12},{12,10},{11,13},{13,11},{18,20},{2... | collective-permute-start | bytes 24584 | tf_op jit(solution)/shard_map/ppermute | solution.py:138
  16.5 0.1 collective-permute-start.1
  16.6 3.0 %collective-permute-done.2.rest_1_ = f32[16,128]{1,0:T(8,128)S(1)} collective-permute-done((f32[16,128]{1,0:T(8,128)S(1)}, f32[16,128]{1,0:T(8,128)S(1)}, u32[]{:S(2)}, u32[]{:S(2)}) %collective-permute-start.2) | collective-permute-done | bytes 8224 | tf_op jit(solution)/shard_map/ppermute | solution.py:138
  19.5 1.9 %collective-permute-start.4 = (f32[48,128]{1,0:T(8,128)S(1)}, f32[48,128]{1,0:T(8,128)S(1)}, u32[]{:S(2)}, u32[]{:S(2)}) collective-permute-start(f32[48,128]{1,0:T(8,128)S(1)} %shard_map.115.own), channel_id=1, source_target_pairs={{8,16},{16,8},{9,17},{17,9},{10,18},{18,10},{11,19},{19,11},{12,20... | collective-permute-start | bytes 73736 | tf_op jit(solution)/shard_map/ppermute | solution.py:138
  21.5 0.1 collective-permute-start.3
  21.6 1.0 copy-done.2
  22.6 1.0 copy-done.4
  23.7 1.0 copy-done.6
  24.7 1.3 %shard_map.116 = (f32[2048,128]{1,0:T(8,128)S(1)}, f32[2048,128]{1,0:T(8,128)S(1)}, f32[2048,128]{1,0:T(8,128)S(1)}, f32[552,128]{1,0:T(8,128)S(1)}, f32[552,128]{1,0:T(8,128)S(1)}) custom-call(s32[4]{0:T(128)S(1)} %pad_add_fusion.info, f32[2,4]{1,0:T(2,128)S(1)} %pad_maximum_fusion.tables, f32[1024,128]{1,0:T(8,128)S(1)} %bitcast.30, ...), custom_call_target="tpu_custom_call" | custom-call | tf_op jit(solution)/shard_map/pallas_call | solution.py:118
  26.0 0.1 collective-permute-start.8
  26.1 2.0 %collective-permute-start.9 = (f32[552,128]{1,0:T(8,128)S(1)}, f32[552,128]{1,0:T(8,128)S(1)}, u32[]{:S(2)}, u32[]{:S(2)}) collective-permute-start(f32[552,128]{1,0:T(8,128)S(1)} %get-tuple-element.77), channel_id=1, source_target_pairs={{2,4},{4,2},{3,5},{5,3},{10,12},{12,10},{11,13},{13,11},{18,20},{2... | collective-permute-start | bytes 847880 | tf_op jit(solution)/shard_map/ppermute | solution.py:138
  28.1 0.7 copy.22
  28.8 2.5 %copy-done = f32[1,1,1,40,8,4096]{5,4,3,2,1,0:T(8,128)S(1)} copy-done((f32[1,1,1,40,8,4096]{5,4,3,2,1,0:T(8,128)S(1)}, f32[1,1,1,40,8,4096]{5,4,3,2,1,0:T(8,128)}, u32[]{:S(2)}) %copy-start) | copy-done | bytes 5242904
  31.3 0.7 copy-done.10
  32.0 4.2 %shard_map.117 = (f32[2048,128]{1,0:T(8,128)S(1)}, f32[2048,128]{1,0:T(8,128)S(1)}, f32[240,128]{1,0:T(8,128)S(1)}) custom-call(s32[4]{0:T(128)S(1)} %pad_add_fusion.info, s32[3,40]{1,0:T(4,128)S(1)} %bitcast.35, s32[4,40]{1,0:T(4,128)S(1)} %bitcast.42, f32[40,8,4096]{2,1,0:T(8,128)S(1)} %bitcast.28, f32[48,128]{1,0:T(8,128)S(1)} %shard_map.115.own, ...), custom_call_target="tpu_custom_call" | custom-call | tf_op jit(solution)/shard_map/pallas_call | solution.py:118
  36.2 2.3 %shard_map.118 = (f32[2048,128]{1,0:T(8,128)S(1)}, f32[2048,128]{1,0:T(8,128)S(1)}, f32[2048,128]{1,0:T(8,128)S(1)}, f32[256,128]{1,0:T(8,128)S(1)}) custom-call(s32[4]{0:T(128)S(1)} %pad_add_fusion.info, f32[2048,128]{1,0:T(8,128)S(1)} %get-tuple-element.73.k_in, ...), custom_call_target="tpu_custom_call", output_to_operand_aliasing={{0}: (1, {}), {1}: (2, {}), {2}: (3, {})} | custom-call | tf_op jit(solution)/shard_map/pallas_call | solution.py:118
  38.5 2.5 %collective-permute-done.7.rest_0_ = f32[240,128]{1,0:T(8,128)S(1)} collective-permute-done((f32[240,128]{1,0:T(8,128)S(1)}, f32[240,128]{1,0:T(8,128)S(1)}, u32[]{:S(2)}, u32[]{:S(2)}) %collective-permute-start.7) | collective-permute-done | bytes 122912 | tf_op jit(solution)/shard_map/ppermute | solution.py:138
  41.1 1.9 %shard_map.119 = (f32[2048,128]{1,0:T(8,128)S(1)}, f32[2048,128]{1,0:T(8,128)S(1)}, f32[440,128]{1,0:T(8,128)S(1)}, f32[440,128]{1,0:T(8,128)S(1)}) custom-call(s32[4]{0:T(128)S(1)} %pad_add_fusion.info, f32[2048,128]{1,0:T(8,128)S(1)} %get-tuple-element.70.p0_in, ...), custom_call_target="tpu_custom_call", output_to_operand_aliasing={{0}: (1, {}), {1}: (2, {})} | custom-call | tf_op jit(solution)/shard_map/pallas_call | solution.py:118
  43.0 3.0 %collective-permute-start.11 = (f32[440,128]{1,0:T(8,128)S(1)}, f32[440,128]{1,0:T(8,128)S(1)}, u32[]{:S(2)}, u32[]{:S(2)}) collective-permute-start(f32[440,128]{1,0:T(8,128)S(1)} %get-tuple-element.83), channel_id=1, source_target_pairs={{2,4},{4,2},{3,5},{5,3},{10,12},{12,10},{11,13},{13,11},{18,20},{2... | collective-permute-start | bytes 675848 | tf_op jit(solution)/shard_map/ppermute | solution.py:138
  46.1 0.4 collective-permute-start.12
  46.4 4.6 %collective-permute-done.12.rest_0_ = f32[256,128]{1,0:T(8,128)S(1)} collective-permute-done((f32[256,128]{1,0:T(8,128)S(1)}, f32[256,128]{1,0:T(8,128)S(1)}, u32[]{:S(2)}, u32[]{:S(2)}) %collective-permute-start.12) | collective-permute-done | bytes 131104 | tf_op jit(solution)/shard_map/ppermute | solution.py:138
  51.1 2.3 %shard_map.120 = (f32[2048,128]{1,0:T(8,128)S(1)}, f32[2048,128]{1,0:T(8,128)S(1)}, f32[2048,128]{1,0:T(8,128)S(1)}) custom-call(s32[4]{0:T(128)S(1)} %pad_add_fusion.info, f32[256,128]{1,0:T(8,128)S(1)} %collective-permute-done.12.rest_0_), custom_call_target="tpu_custom_call" | custom-call | tf_op jit(solution)/shard_map/pallas_call | solution.py:118
  53.4 1.2 %shard_map.121 = (f32[2048,128]{1,0:T(8,128)S(1)}, f32[2048,128]{1,0:T(8,128)S(1)}, f32[488,128]{1,0:T(8,128)S(1)}, f32[488,128]{1,0:T(8,128)S(1)}) custom-call(s32[4]{0:T(128)S(1)} %pad_add_fusion.info, f32[2048,128]{1,0:T(8,128)S(1)} %get-tuple-element.80.p0_in, ...), custom_call_target="tpu_custom_call", output_to_operand_aliasing={{0}: (1, {}), {1}: (2, {})} | custom-call | tf_op jit(solution)/shard_map/pallas_call | solution.py:118
  54.6 1.8 %collective-permute-start.13 = (f32[488,128]{1,0:T(8,128)S(1)}, f32[488,128]{1,0:T(8,128)S(1)}, u32[]{:S(2)}, u32[]{:S(2)}) collective-permute-start(f32[488,128]{1,0:T(8,128)S(1)} %get-tuple-element.99), channel_id=1, source_target_pairs={{0,8},{16,24},{8,0},{24,16},{1,9},{17,25},{9,1},{25,17},{2,10},{18... | collective-permute-start | bytes 749576 | tf_op jit(solution)/shard_map/ppermute | solution.py:138
  56.5 3.9 %collective-permute-start.14 = (f32[488,128]{1,0:T(8,128)S(1)}, f32[488,128]{1,0:T(8,128)S(1)}, u32[]{:S(2)}, u32[]{:S(2)}) collective-permute-start(f32[488,128]{1,0:T(8,128)S(1)} %get-tuple-element.100), channel_id=1, source_target_pairs={{8,16},{16,8},{9,17},{17,9},{10,18},{18,10},{11,19},{19,11},{12,20... | collective-permute-start | bytes 749576 | tf_op jit(solution)/shard_map/ppermute | solution.py:138
  60.4 3.1 %shard_map.122 = (f32[5,6,256,128]{3,2,1,0:T(8,128)S(1)}, f32[5,256,128]{2,1,0:T(8,128)S(1)}, f32[5,256,128]{2,1,0:T(8,128)S(1)}) custom-call(s32[4]{0:T(128)S(1)} %pad_add_fusion.info, s32[3,40]{1,0:T(4,128)S(1)} %bitcast.36, f32[2048,128]{1,0:T(8,128)S(1)} %get-tuple-element.90.k0, f32[2048,128]{1,0:T(8,128)S(1)} %get-tuple-element.92.k1, ...), custom_call_target="tpu_custom_call" | custom-call | tf_op jit(solution)/shard_map/pallas_call | solution.py:118
  63.5 1.0 collective-permute-done.14.rest_1_
  64.6 14.4 %shard_map.123 = (f32[1024,128]{1,0:T(8,128)S(1)}, f32[5,2,256,128]{3,2,1,0:T(8,128)S(1)}, f32[640,128]{1,0:T(8,128)S(1)}, f32[256,128]{1,0:T(8,128)S(1)}, f32[240,128]{1,0:T(8,128)S(1)}) custom-call(s32[4]{0:T(128)S(1)} %pad_add_fusion.info, s32[3,40]{1,0:T(4,128)S(1)} %bitcast.37, f32[2048,128]{1,0:T(8,128)S(1)} %get-tuple-element.88.p0, ...), custom_call_target="tpu_custom_call" | custom-call | tf_op jit(solution)/shard_map/pallas_call | solution.py:118
  79.1 2.9 %shard_map.124 = f32[2560,128]{1,0:T(8,128)} custom-call(s32[4]{0:T(128)S(1)} %pad_add_fusion.info, f32[5,2,256,128]{3,2,1,0:T(8,128)S(1)} %get-tuple-element.103.solved), custom_call_target="tpu_custom_call" | custom-call | tf_op jit(solution)/shard_map/pallas_call | solution.py:118
  82.0 1.9 %collective-permute-done.15.rest_0_ = f32[240,128]{1,0:T(8,128)S(1)} collective-permute-done((f32[240,128]{1,0:T(8,128)S(1)}, f32[240,128]{1,0:T(8,128)S(1)}, u32[]{:S(2)}, u32[]{:S(2)}) %collective-permute-start.15) | collective-permute-done | bytes 122912 | tf_op jit(solution)/shard_map/ppermute | solution.py:138
  83.9 0.8 shard_map.125
  84.9 6.2 %collective-permute-start.17 = (f32[160,128]{1,0:T(8,128)S(1)}, f32[160,128]{1,0:T(8,128)S(1)}, u32[]{:S(2)}, u32[]{:S(2)}) collective-permute-start(f32[160,128]{1,0:T(8,128)S(1)} %get-tuple-element.107), channel_id=1, source_target_pairs={{2,4},{4,2},{3,5},{5,3},{10,12},{12,10},{11,13},{13,11},{18,20},{2... | collective-permute-start | bytes 245768 | tf_op jit(solution)/shard_map/ppermute | solution.py:138
  91.1 2.1 %collective-permute-done.17.rest_2_ = f32[160,128]{1,0:T(8,128)S(1)} collective-permute-done((f32[160,128]{1,0:T(8,128)S(1)}, f32[160,128]{1,0:T(8,128)S(1)}, u32[]{:S(2)}, u32[]{:S(2)}) %collective-permute-start.17) | collective-permute-done | bytes 81952 | tf_op jit(solution)/shard_map/ppermute | solution.py:138
  93.2 0.7 shard_map.126
  94.0 13.7 %collective-permute-start.19 = (f32[128,128]{1,0:T(8,128)S(1)}, f32[128,128]{1,0:T(8,128)S(1)}, u32[]{:S(2)}, u32[]{:S(2)}) collective-permute-start(f32[128,128]{1,0:T(8,128)S(1)} %get-tuple-element.110), channel_id=1, source_target_pairs={{8,16},{16,8},{9,17},{17,9},{10,18},{18,10},{11,19},{19,11},{12,20... | collective-permute-start | bytes 196616 | tf_op jit(solution)/shard_map/ppermute | solution.py:138
  107.7 2.2 %collective-permute-done.19.rest_4_ = f32[128,128]{1,0:T(8,128)S(1)} collective-permute-done((f32[128,128]{1,0:T(8,128)S(1)}, f32[128,128]{1,0:T(8,128)S(1)}, u32[]{:S(2)}, u32[]{:S(2)}) %collective-permute-start.19) | collective-permute-done | bytes 65568 | tf_op jit(solution)/shard_map/ppermute | solution.py:138
  109.9 1.8 %shard_map.127 = f32[1024,128]{1,0:T(8,128)} custom-call(s32[4]{0:T(128)S(1)} %pad_add_fusion.info, f32[1024,128]{1,0:T(8,128)S(1)} %get-tuple-element.101.core, f32[240,128]{1,0:T(8,128)S(1)} %collective-permute-done.15.rest_0_, f32[160,128]{1,0:T(8,128)S(1)} %collective-permute-done.16.rest_1_, f32[160,128]{1,0:T(8,128)S(1)} %collective-permute-done.17.rest_2_, ...), custom_call_target="tpu_custom_call" | custom-call | tf_op jit(solution)/shard_map/pallas_call | solution.py:118
  (32 shorter events, 0.4 us)
Async XLA Ops:
  0.6 8.1 %collective-permute-start = (f32[8,64]{1,0:T(8,128)}, f32[8,64]{1,0:T(8,128)S(1)}, u32[]{:S(2)}, u32[]{:S(2)}) collective-permute-start(f32[8,64]{1,0:T(8,128)} %bitcast.38), channel_id=1, source_target_pairs={{0,1},{1,0},{2,3},{3,2},{4,5},{5,4},{6,7},{7,6},{8,9},{9,8},{10,11... | collective-permute-start | bytes 6152 | tf_op jit(solution)/shard_map/ppermute | solution.py:138
  2.9 1.0 copy-start.1
  4.0 1.0 copy-start.3
  5.0 1.0 copy-start.5
  6.1 0.7 copy-start.8
  6.7 0.7 copy-start.9
  8.8 12.8 %collective-permute-start.5 = (f32[416,128]{1,0:T(8,128)S(1)}, f32[416,128]{1,0:T(8,128)S(1)}, u32[]{:S(2)}, u32[]{:S(2)}) collective-permute-start(f32[416,128]{1,0:T(8,128)S(1)} %get-tuple-element.60), channel_id=1, source_target_pairs={{0,8},{16,24},{8,0},{24,16},{1,9},{17,25},{9,1},{25,17},{2,10},{18... | collective-permute-start | bytes 638984 | tf_op jit(solution)/shard_map/ppermute | solution.py:138
  9.3 12.3 %collective-permute-start.6 = (f32[416,128]{1,0:T(8,128)S(1)}, f32[416,128]{1,0:T(8,128)S(1)}, u32[]{:S(2)}, u32[]{:S(2)}) collective-permute-start(f32[416,128]{1,0:T(8,128)S(1)} %get-tuple-element.61), channel_id=1, source_target_pairs={{8,16},{16,8},{9,17},{17,9},{10,18},{18,10},{11,19},{19,11},{12,20... | collective-permute-start | bytes 638984 | tf_op jit(solution)/shard_map/ppermute | solution.py:138
  13.9 0.7 copy-start.7
  14.6 5.0 %collective-permute-start.2 = (f32[16,128]{1,0:T(8,128)S(1)}, f32[16,128]{1,0:T(8,128)S(1)}, u32[]{:S(2)}, u32[]{:S(2)}) collective-permute-start(f32[16,128]{1,0:T(8,128)S(1)} %shard_map.114.own), channel_id=1, source_target_pairs={{2,4},{4,2},{3,5},{5,3},{10,12},{12,10},{11,13},{13,11},{18,20},{2... | collective-permute-start | bytes 24584 | tf_op jit(solution)/shard_map/ppermute | solution.py:138
  16.5 3.0 %collective-permute-start.1 = (f32[16,128]{1,0:T(8,128)S(1)}, f32[16,128]{1,0:T(8,128)S(1)}, u32[]{:S(2)}, u32[]{:S(2)}) collective-permute-start(f32[16,128]{1,0:T(8,128)S(1)} %shard_map.114.own), channel_id=1, source_target_pairs={{0,2},{4,6},{2,0},{6,4},{1,3},{5,7},{3,1},{7,5},{8,10},{12,14},{10... | collective-permute-start | bytes 24584 | tf_op jit(solution)/shard_map/ppermute | solution.py:138
  19.5 6.5 %collective-permute-start.4 = (f32[48,128]{1,0:T(8,128)S(1)}, f32[48,128]{1,0:T(8,128)S(1)}, u32[]{:S(2)}, u32[]{:S(2)}) collective-permute-start(f32[48,128]{1,0:T(8,128)S(1)} %shard_map.115.own), channel_id=1, source_target_pairs={{8,16},{16,8},{9,17},{17,9},{10,18},{18,10},{11,19},{19,11},{12,20... | collective-permute-start | bytes 73736 | tf_op jit(solution)/shard_map/ppermute | solution.py:138
  21.5 4.6 %collective-permute-start.3 = (f32[48,128]{1,0:T(8,128)S(1)}, f32[48,128]{1,0:T(8,128)S(1)}, u32[]{:S(2)}, u32[]{:S(2)}) collective-permute-start(f32[48,128]{1,0:T(8,128)S(1)} %shard_map.115.own), channel_id=1, source_target_pairs={{0,8},{16,24},{8,0},{24,16},{1,9},{17,25},{9,1},{25,17},{2,10},{18... | collective-permute-start | bytes 73736 | tf_op jit(solution)/shard_map/ppermute | solution.py:138
  21.6 1.0 copy-start.2
  22.6 1.0 copy-start.4
  23.7 1.0 copy-start.6
  26.0 10.2 %collective-permute-start.8 = (f32[552,128]{1,0:T(8,128)S(1)}, f32[552,128]{1,0:T(8,128)S(1)}, u32[]{:S(2)}, u32[]{:S(2)}) collective-permute-start(f32[552,128]{1,0:T(8,128)S(1)} %get-tuple-element.76), channel_id=1, source_target_pairs={{0,2},{4,6},{2,0},{6,4},{1,3},{5,7},{3,1},{7,5},{8,10},{12,14},{10... | collective-permute-start | bytes 847880 | tf_op jit(solution)/shard_map/ppermute | solution.py:138
  26.1 10.1 %collective-permute-start.9 = (f32[552,128]{1,0:T(8,128)S(1)}, f32[552,128]{1,0:T(8,128)S(1)}, u32[]{:S(2)}, u32[]{:S(2)}) collective-permute-start(f32[552,128]{1,0:T(8,128)S(1)} %get-tuple-element.77), channel_id=1, source_target_pairs={{2,4},{4,2},{3,5},{5,3},{10,12},{12,10},{11,13},{13,11},{18,20},{2... | collective-permute-start | bytes 847880 | tf_op jit(solution)/shard_map/ppermute | solution.py:138
  28.8 2.5 %copy-start = (f32[1,1,1,40,8,4096]{5,4,3,2,1,0:T(8,128)S(1)}, f32[1,1,1,40,8,4096]{5,4,3,2,1,0:T(8,128)}, u32[]{:S(2)}) copy-start(f32[1,1,1,40,8,4096]{5,4,3,2,1,0:T(8,128)} %param.19) | copy-start | bytes 15728644
  31.3 0.7 copy-start.10
  36.1 4.9 %collective-permute-start.7 = (f32[240,128]{1,0:T(8,128)S(1)}, f32[240,128]{1,0:T(8,128)S(1)}, u32[]{:S(2)}, u32[]{:S(2)}) collective-permute-start(f32[240,128]{1,0:T(8,128)S(1)} %get-tuple-element.72), channel_id=1, source_target_pairs={{0,1},{1,0},{2,3},{3,2},{4,5},{5,4},{6,7},{7,6},{8,9},{9,8},{10,11... | collective-permute-start | bytes 368648 | tf_op jit(solution)/shard_map/ppermute | solution.py:138
  43.0 10.4 %collective-permute-start.10 = (f32[440,128]{1,0:T(8,128)S(1)}, f32[440,128]{1,0:T(8,128)S(1)}, u32[]{:S(2)}, u32[]{:S(2)}) collective-permute-start(f32[440,128]{1,0:T(8,128)S(1)} %get-tuple-element.82), channel_id=1, source_target_pairs={{0,2},{4,6},{2,0},{6,4},{1,3},{5,7},{3,1},{7,5},{8,10},{12,14},{10... | collective-permute-start | bytes 675848 | tf_op jit(solution)/shard_map/ppermute | solution.py:138
  43.0 10.3 %collective-permute-start.11 = (f32[440,128]{1,0:T(8,128)S(1)}, f32[440,128]{1,0:T(8,128)S(1)}, u32[]{:S(2)}, u32[]{:S(2)}) collective-permute-start(f32[440,128]{1,0:T(8,128)S(1)} %get-tuple-element.83), channel_id=1, source_target_pairs={{2,4},{4,2},{3,5},{5,3},{10,12},{12,10},{11,13},{13,11},{18,20},{2... | collective-permute-start | bytes 675848 | tf_op jit(solution)/shard_map/ppermute | solution.py:138
  46.1 5.0 %collective-permute-start.12 = (f32[256,128]{1,0:T(8,128)S(1)}, f32[256,128]{1,0:T(8,128)S(1)}, u32[]{:S(2)}, u32[]{:S(2)}) collective-permute-start(f32[256,128]{1,0:T(8,128)S(1)} %get-tuple-element.84), channel_id=1, source_target_pairs={{0,1},{1,0},{2,3},{3,2},{4,5},{5,4},{6,7},{7,6},{8,9},{9,8},{10,11... | collective-permute-start | bytes 393224 | tf_op jit(solution)/shard_map/ppermute | solution.py:138
  54.6 8.9 %collective-permute-start.13 = (f32[488,128]{1,0:T(8,128)S(1)}, f32[488,128]{1,0:T(8,128)S(1)}, u32[]{:S(2)}, u32[]{:S(2)}) collective-permute-start(f32[488,128]{1,0:T(8,128)S(1)} %get-tuple-element.99), channel_id=1, source_target_pairs={{0,8},{16,24},{8,0},{24,16},{1,9},{17,25},{9,1},{25,17},{2,10},{18... | collective-permute-start | bytes 749576 | tf_op jit(solution)/shard_map/ppermute | solution.py:138
  56.5 8.1 %collective-permute-start.14 = (f32[488,128]{1,0:T(8,128)S(1)}, f32[488,128]{1,0:T(8,128)S(1)}, u32[]{:S(2)}, u32[]{:S(2)}) collective-permute-start(f32[488,128]{1,0:T(8,128)S(1)} %get-tuple-element.100), channel_id=1, source_target_pairs={{8,16},{16,8},{9,17},{17,9},{10,18},{18,10},{11,19},{19,11},{12,20... | collective-permute-start | bytes 749576 | tf_op jit(solution)/shard_map/ppermute | solution.py:138
  79.0 4.9 %collective-permute-start.15 = (f32[240,128]{1,0:T(8,128)S(1)}, f32[240,128]{1,0:T(8,128)S(1)}, u32[]{:S(2)}, u32[]{:S(2)}) collective-permute-start(f32[240,128]{1,0:T(8,128)S(1)} %get-tuple-element.102), channel_id=1, source_target_pairs={{0,1},{1,0},{2,3},{3,2},{4,5},{5,4},{6,7},{7,6},{8,9},{9,8},{10,11... | collective-permute-start | bytes 368648 | tf_op jit(solution)/shard_map/ppermute | solution.py:138
  84.8 6.3 %collective-permute-start.16 = (f32[160,128]{1,0:T(8,128)S(1)}, f32[160,128]{1,0:T(8,128)S(1)}, u32[]{:S(2)}, u32[]{:S(2)}) collective-permute-start(f32[160,128]{1,0:T(8,128)S(1)} %get-tuple-element.106), channel_id=1, source_target_pairs={{0,2},{4,6},{2,0},{6,4},{1,3},{5,7},{3,1},{7,5},{8,10},{12,14},{10... | collective-permute-start | bytes 245768 | tf_op jit(solution)/shard_map/ppermute | solution.py:138
  84.9 8.4 %collective-permute-start.17 = (f32[160,128]{1,0:T(8,128)S(1)}, f32[160,128]{1,0:T(8,128)S(1)}, u32[]{:S(2)}, u32[]{:S(2)}) collective-permute-start(f32[160,128]{1,0:T(8,128)S(1)} %get-tuple-element.107), channel_id=1, source_target_pairs={{2,4},{4,2},{3,5},{5,3},{10,12},{12,10},{11,13},{13,11},{18,20},{2... | collective-permute-start | bytes 245768 | tf_op jit(solution)/shard_map/ppermute | solution.py:138
  93.9 13.8 %collective-permute-start.18 = (f32[128,128]{1,0:T(8,128)S(1)}, f32[128,128]{1,0:T(8,128)S(1)}, u32[]{:S(2)}, u32[]{:S(2)}) collective-permute-start(f32[128,128]{1,0:T(8,128)S(1)} %get-tuple-element.109), channel_id=1, source_target_pairs={{0,8},{16,24},{8,0},{24,16},{1,9},{17,25},{9,1},{25,17},{2,10},{18... | collective-permute-start | bytes 196616 | tf_op jit(solution)/shard_map/ppermute | solution.py:138
  94.0 15.9 %collective-permute-start.19 = (f32[128,128]{1,0:T(8,128)S(1)}, f32[128,128]{1,0:T(8,128)S(1)}, u32[]{:S(2)}, u32[]{:S(2)}) collective-permute-start(f32[128,128]{1,0:T(8,128)S(1)} %get-tuple-element.110), channel_id=1, source_target_pairs={{8,16},{16,8},{9,17},{17,9},{10,18},{18,10},{11,19},{19,11},{12,20... | collective-permute-start | bytes 196616 | tf_op jit(solution)/shard_map/ppermute | solution.py:138

commit v2 on v1

--- a/solution.py
+++ b/solution.py
@@ -95,6 +95,12 @@
         self.counts = counts
         self.sides = [1 if n == 2 else 2 for n in counts]
 
+        per = by // SUB
+        self.z_rows = bx * per // GROUP * SUB
+        self.x_pack = (H + 1) * per // GROUP * SUB
+        self.y_rows = -(-self.xf * (2 * MARGIN + H) // SUB) * SUB
+        self.y_pack = -(-self.xf // GROUP) * SUB
+
     @property
     def frame(self):
         return rows_of(self.rows)
@@ -111,15 +117,16 @@
 VMEM = pl.BlockSpec(memory_space=pltpu.VMEM)
 SMEM = pl.BlockSpec(memory_space=pltpu.SMEM)
 HBM = pl.BlockSpec(memory_space=pltpu.HBM)
-
-
-def call(kernel, outs, ins, specs=(), scratch=(), alias=None, limit=12):
+ANY = pl.BlockSpec(memory_space=pl.ANY)
+
+
+def call(kernel, outs, ins, specs=(), scratch=(), alias=None, limit=12, out_spec=VMEM):
     specs = list(specs) + [VMEM] * (len(ins) - len(specs))
     return pl.pallas_call(
         kernel,
         out_shape=outs,
         in_specs=specs,
-        out_specs=jax.tree.map(lambda _: VMEM, outs),
+        out_specs=jax.tree.map(lambda _: out_spec, outs),
         scratch_shapes=list(scratch),
         input_output_aliases=alias or {},
         compiler_params=pltpu.CompilerParams(vmem_limit_bytes=limit * 1024 * 1024),
@@ -146,103 +153,206 @@
     return out
 
 
-def static_x(fr, info, contrast, channel, kappa, labels, forcing, *rest):
-    n = fr.sides[0]
-    slabs, (k_buf, l_buf, t_buf, sem, t_sem) = rest[:n], rest[n:]
+FIELDS = ((0, H, H, 0), (1, MARGIN, WIDE, H), (2, MARGIN, WIDE + MARGIN, WIDE))
+FIRST = (0, H, H + MARGIN)
+DEPTH = (H, MARGIN, MARGIN)
+WIDTH = H + 2 * MARGIN
+
+
+def static_first(fr, info, contrast, channel, kappa, labels, forcing, coef, offsets, links, *rest):
+    n = fr.sides[2]
+    (kap, frc, wgt, own, table), slabs = rest[:5], rest[5 : 5 + n]
+    k_buf, l_buf, c_buf, o_buf, i_buf, t_buf, sem = rest[5 + n :]
+    _, lane = iotas()
+    moves = (
+        (contrast, t_buf.at[0]),
+        (channel, t_buf.at[1]),
+        (labels, l_buf),
+        (kappa, k_buf),
+        (forcing, frc),
+        (coef, c_buf),
+        (offsets, o_buf),
+        (links, i_buf),
+    )
+    copies = [pltpu.make_async_copy(src, dst, sem.at[i]) for i, (src, dst) in enumerate(moves)]
+    for copy in copies:
+        copy.start()
+    zero(own)
+    zero(table)
+    for copy in copies:
+        copy.wait()
+    own[0 : coef.shape[0], 0 : coef.shape[1]] = c_buf[...]
+    for i in range(3):
+        table[i : i + 1, 0 : offsets.shape[2]] = o_buf[i]
+    table[4:8, 0 : links.shape[1]] = i_buf[...]
+    group = lane & (PIECE - 1)
+
+    def block(b):
+        tiles = [[], [], []]
+        for j in range(GROUP):
+            at = pl.ds((b * GROUP + j) * SUB, SUB)
+            label = l_buf[at, :]
+            k, w = k_buf[at, :] * look_up(label, t_buf, 0), look_up(label, t_buf, 1)
+            kap[at, :] = k
+            wgt[at, :] = w
+            for some, v in zip(tiles, (k, frc[at, :], w)):
+                some.append(v)
+        for i, slab in enumerate(slabs):
+            lower = is_lower(info, 2, i)
+            packs = [pack_tiles(tiles[m], pick(lower, high, low), lane) for m, _, high, low in FIELDS]
+            mix = jnp.where(group < H, packs[0], jnp.where(group < WIDE, packs[1], packs[2]))
+            slab[pl.ds(b * SUB, SUB), :] = mix
+
+    count = fr.bx * fr.by // (GROUP * SUB)
+    loop(count, block, 2)
+    for slab in slabs:
+        slab[count * SUB : (count + 1) * SUB, :] = own[...]
+
+
+def static_x(fr, info, kap, frc, wgt, own, *rest):
+    n0, n2 = fr.sides[0], fr.sides[2]
+    z_in, coefs, slabs = rest[:n2], rest[n2], rest[n2 + 1 :]
     by = fr.by
-    f_row, w_row, c_row = H * by, (H + MARGIN) * by, (H + 2 * MARGIN) * by
-    copies = [
-        pltpu.make_async_copy(contrast, t_buf.at[0], t_sem.at[0]),
-        pltpu.make_async_copy(channel, t_buf.at[1], t_sem.at[1]),
-    ]
+    coefs[0:SUB, :] = own[...]
+    for s, buf in enumerate(z_in):
+        coefs[(1 + s) * SUB : (2 + s) * SUB, :] = buf[fr.z_rows : fr.z_rows + SUB, :]
     for i, slab in enumerate(slabs):
         lower = is_lower(info, 0, i)
-        first = pl.multiple_of(pick(lower, (fr.bx - H) * by, 0), SUB)
-        four = pl.multiple_of(pick(lower, (fr.bx - MARGIN) * by, 0), SUB)
-        for j, (src, dst) in enumerate(
-            (
-                (kappa.at[pl.ds(first, H * by)], k_buf.at[i]),
-                (labels.at[pl.ds(first, H * by)], l_buf.at[i]),
-                (forcing.at[pl.ds(four, MARGIN * by)], slab.at[pl.ds(f_row, MARGIN * by)]),
-            )
-        ):
-            copies.append(pltpu.make_async_copy(src, dst, sem.at[i, j]))
-    for copy in copies:
-        copy.start()
-    for copy in copies:
-        copy.wait()
-    for i, slab in enumerate(slabs):
-        skip = pl.multiple_of(pick(is_lower(info, 0, i), by, 0), SUB)
-        slab[0:f_row, :] = k_buf[i] * look_up(l_buf[i], t_buf, 0)
-        slab[w_row:c_row, :] = look_up(l_buf[i, pl.ds(skip, MARGIN * by), :], t_buf, 1)
-
-
-def static_y(fr, info, tables, kappa, labels, forcing, *rest):
-    n = fr.sides[0]
-    received, (k0, f0, w0), slabs = rest[:n], rest[n : n + 3], rest[n + 3 :]
-    by, yf, w = fr.by, fr.yf, 2 * MARGIN + H
+        for ref, at, count in zip((kap, frc, wgt), FIRST, DEPTH):
+            first = pl.multiple_of(pick(lower, (fr.bx - count) * by, 0), SUB)
+            slab[at * by : (at + count) * by, :] = ref[pl.ds(first, count * by), :]
+        first = pl.multiple_of(pick(lower, fr.z_rows - fr.x_pack, 0), SUB)
+        row = WIDTH * by
+        for buf in z_in:
+            slab[row : row + fr.x_pack, :] = buf[pl.ds(first, fr.x_pack), :]
+            row += fr.x_pack
+        slab[row : row + coefs.shape[0], :] = coefs[...]
+
+
+def x_margin(fr, info, phase):
+    lower = is_lower(info, 0, phase)
+    return pick(lower, fr.bx + H, 0), pick(lower, 0, 1)
+
+
+def static_y(fr, info, kap, frc, wgt, coefs_in, *rest):
+    n0, n1, n2 = fr.sides
+    z_in, x_in, (k0, f0, w0, coefs), rest = rest[:n2], rest[n2 : n0 + n2], rest[n0 + n2 : n0 + n2 + 4], rest[n0 + n2 + 4 :]
+    slabs, tall = rest[:n1], rest[n1]
+    _, lane = iotas()
+    by, yf, per = fr.by, fr.yf, fr.by // SUB
     for ref in (k0, f0, w0):
         zero(ref)
 
     def core(x):
-        for t in range(by // SUB):
+        for t in range(per):
             src = pl.ds(x * by + t * SUB, SUB)
             dst = pl.ds((x + H) * yf + TOP + t * SUB, SUB)
-            label = labels[src, :]
-            k0[dst, :] = kappa[src, :] * look_up(label, tables, 0)
-            w0[dst, :] = look_up(label, tables, 1)
-            f0[dst, :] = forcing[src, :]
+            for frame, ref in ((k0, kap), (f0, frc), (w0, wgt)):
+                frame[dst, :] = ref[src, :]
 
     loop(fr.bx, core, 4)
-    for i, buf in enumerate(received):
+    each = coefs_in.shape[0]
+    coefs[0:each, :] = coefs_in[...]
+    c_in = WIDTH * by + n2 * fr.x_pack
+    for i, buf in enumerate(x_in):
+        coefs[(1 + i) * each : (2 + i) * each, :] = buf[c_in : c_in + each, :]
         lower = is_lower(info, 0, i)
-        for frame, count, at, low in ((k0, H, 0, 0), (f0, MARGIN, H, 1), (w0, MARGIN, H + MARGIN, 1)):
-            first = pick(lower, fr.bx + H, low)
+        for frame, count, at in zip((k0, f0, w0), DEPTH, FIRST):
+            first = pick(lower, fr.bx + H, H - count)
             for j in range(count):
-                for t in range(by // SUB):
+                for t in range(per):
                     row = (at + j) * by + t * SUB
                     frame[pl.ds(pl.multiple_of((first + j) * yf + TOP + t * SUB, SUB), SUB), :] = buf[row : row + SUB, :]
 
     def plane(x):
-        r, o = x * yf, x * w
+        r, o = x * yf, x * WIDTH
         for i, slab in enumerate(slabs):
             lower = is_lower(info, 1, i)
-            for frame, count, at in ((k0, H, 0), (f0, MARGIN, H), (w0, MARGIN, H + MARGIN)):
+            for frame, count, at in zip((k0, f0, w0), DEPTH, FIRST):
                 first = r + pick(lower, TOP + by - count, TOP)
                 slab[pl.ds(o + at, count), :] = frame[pl.ds(first, count), :]
 
     loop(fr.xf, plane, 6)
 
-
-def static_z(fr, info, k_in, f_in, w_in, *rest):
-    n = fr.sides[1]
-    received, (k0, f0, w0), slabs = rest[:n], rest[n : n + 3], rest[n + 3 :]
+    narrow = lane < PIECE
+    for i, slab in enumerate(slabs):
+        t = pick(is_lower(info, 1, i), per - 1, 0)
+        row = fr.y_rows
+        for s, buf in enumerate(z_in):
+            zero(tall)
+            for x in range(fr.bx):
+                pack, group = x * per // GROUP, x * per % GROUP + t
+                v = unpack_tile(buf[pack * SUB : (pack + 1) * SUB, :], group, 0)
+                tall[(x + H) * SUB : (x + H + 1) * SUB, :] = jnp.where(narrow, v, 0.0)
+            for k, part in enumerate(x_in):
+                first, skip = x_margin(fr, info, k)
+                for j in range(H):
+                    at = (j + skip) * per
+                    start = WIDTH * by + s * fr.x_pack + (at // GROUP) * SUB
+                    v = unpack_tile(part[pl.ds(pl.multiple_of(start, SUB), SUB), :], at % GROUP + t, 0)
+                    to = pl.multiple_of((first + j) * SUB, SUB)
+                    tall[pl.ds(to, SUB), :] = jnp.where(narrow, v, 0.0)
+            for b in range(fr.y_pack // SUB):
+                tiles = [tall[(b * GROUP + j) * SUB : (b * GROUP + j + 1) * SUB, :] for j in range(GROUP)]
+                slab[row : row + SUB, :] = pack_tiles(tiles, 0, lane)
+                row += SUB
+        slab[row : row + coefs.shape[0], :] = coefs[...]
+
+
+def static_end(fr, info, k_in, f_in, w_in, *rest):
+    n0, n1, n2 = fr.sides
+    z_in, x_in, y_in = rest[:n2], rest[n2 : n0 + n2], rest[n0 + n2 : n0 + n1 + n2]
+    k0, f0, w0, k1, f1, w1 = rest[n0 + n1 + n2 :]
     del k_in, f_in, w_in
     _, lane = iotas()
-    by, yf, w = fr.by, fr.yf, 2 * MARGIN + H
+    by, yf, per = fr.by, fr.yf, fr.by // SUB
 
     def plane(x):
-        r, o = x * yf, x * w
-        for i, buf in enumerate(received):
+        r, o = x * yf, x * WIDTH
+        for i, buf in enumerate(y_in):
             lower = is_lower(info, 1, i)
-            for frame, count, at in ((k0, H, 0), (f0, MARGIN, H), (w0, MARGIN, H + MARGIN)):
+            for frame, count, at in zip((k0, f0, w0), DEPTH, FIRST):
                 first = r + pick(lower, TOP + by, TOP - count)
                 frame[pl.ds(first, count), :] = buf[pl.ds(o + at, count), :]
 
     loop(fr.xf, plane, 6)
-    group = lane & (PIECE - 1)
-
-    def block(b):
-        for i, slab in enumerate(slabs):
-            lower = is_lower(info, 2, i)
-            packs = []
-            for frame, high, low in ((k0, H, 0), (f0, WIDE, H), (w0, WIDE + MARGIN, WIDE)):
-                tiles = [frame[pl.ds((b * GROUP + j) * SUB, SUB), :] for j in range(GROUP)]
-                packs.append(pack_tiles(tiles, pick(lower, high, low), lane))
-            mix = jnp.where(group < H, packs[0], jnp.where(group < WIDE, packs[1], packs[2]))
-            slab[pl.ds(b * SUB, SUB), :] = mix
-
-    loop(fr.blocks, block, 4)
+    for ref in (k1, f1, w1):
+        zero(ref)
+    keeps, shifts = [], []
+    for s in range(n2):
+        lower = is_lower(info, 2, s)
+        lows = [pick(lower, 0, LANES - width) for width in DEPTH]
+        keeps.append([(lane >= low) & (lane < low + width) for low, width in zip(lows, DEPTH)])
+        shifts.append([pick(lower, LANES - at, LANES - width - at) for at, width in zip(FIRST, DEPTH)])
+
+    def put(row, packs, group):
+        for m, ref in enumerate((k1, f1, w1)):
+            value = 0.0
+            for s, pack in enumerate(packs):
+                value = value + jnp.where(keeps[s][m], unpack_tile(pack, group, shifts[s][m]), 0.0)
+            ref[pl.ds(pl.multiple_of(row, SUB), SUB), :] = value
+
+    def core(b):
+        for i in range(4):
+            at = i * per
+            packs = [buf[pl.ds((b * 4 * per // GROUP + at // GROUP) * SUB, SUB), :] for buf in z_in]
+            for t in range(per):
+                put((4 * b + i + H) * yf + TOP + t * SUB, packs, at % GROUP + t)
+
+    loop(fr.bx // 4, core, 2)
+    for k, part in enumerate(x_in):
+        first, skip = x_margin(fr, info, k)
+        for j in range(H):
+            at = (j + skip) * per
+            starts = [WIDTH * by + s * fr.x_pack + (at // GROUP) * SUB for s in range(n2)]
+            packs = [part[pl.ds(pl.multiple_of(start, SUB), SUB), :] for start in starts]
+            for t in range(per):
+                put((first + j) * yf + TOP + t * SUB, packs, at % GROUP + t)
+    for i, part in enumerate(y_in):
+        t = pick(is_lower(info, 1, i), fr.tiles - 1, 0)
+        for x in range(fr.xf):
+            starts = [fr.y_rows + s * fr.y_pack + x // GROUP * SUB for s in range(n2)]
+            put(x * yf + t * SUB, [part[start : start + SUB, :] for start in starts], x % GROUP)
 
 
 def place_masks(z0, lane):
@@ -282,26 +392,29 @@
             ref[a, :] = v
 
 
-def stack(own, *rest):
-    received, out = rest[:-1], rest[-1]
-    zero(out)
-    count = own.shape[0]
-    for i, ref in enumerate((own, *received)):
-        out[i * count : (i + 1) * count, 0 : ref.shape[1]] = ref[...]
-
-
-def prolong(fr, shape, info, off, link, bases, own, *rest):
+def prolong(fr, shape, info, off, bases, own, *rest):
     nb, together = shape
-    n, m = fr.sides[0], fr.sides[2]
-    received, (p0, p1), slabs, (table, keep) = rest[:n], rest[n : n + 2], rest[n + 2 : n + m + 2], rest[n + m + 2 :]
+    n, m = fr.sides[1], fr.sides[2]
+    received, (p0, p1), slabs = rest[:n], rest[n : n + 2], rest[n + 2 : n + m + 2]
+    table, keep, buf, sem = rest[n + m + 2 :]
     sub, lane = iotas()
     live = info[0]
+
+    def copy(p):
+        return pltpu.make_async_copy(bases.at[p], buf.at[p], sem.at[p])
+
+    def start(p, _):
+        copy(p).start()
+        return 0
+
+    lax.fori_loop(0, live, start, 0)
     zero(p0)
     zero(p1)
-    each = (1 + fr.sides[1]) * (1 + m)
+    each = (1 + fr.sides[0]) * (1 + m)
     for i, ref in enumerate((own, *received)):
         for j in range(each):
-            table[i * each + j] = ref[j * SUB : (j + 1) * SUB, :]
+            row = j * SUB + (fr.y_rows + m * fr.y_pack if i else 0)
+            table[i * each + j] = ref[row : row + SUB, :]
 
     def position(axis, step):
         came = 1 + ((info[1 + axis] + jnp.where(step == 0, 1, 0)) & 1)
@@ -310,14 +423,20 @@
     def some(step, _):
         numbers = [step * together + i for i in range(together)]
         per = CHUNKS // SUB
+        for p in numbers:
+
+            @pl.when(p < live)
+            def _():
+                copy(p).wait()
+
         rows = []
         for p in numbers:
-            at = [position(axis, link[axis, p]) for axis in range(3)]
-            row = table[(at[0] * (1 + fr.sides[1]) + at[1]) * (1 + m) + at[2]]
-            coef = jnp.sum(jnp.where(lane == link[3, p], row, 0.0), axis=1, keepdims=True)
+            at = [position(axis, off[4 + axis, p]) for axis in range(3)]
+            row = table[(at[1] * (1 + fr.sides[0]) + at[0]) * (1 + m) + at[2]]
+            coef = jnp.sum(jnp.where(lane == off[7, p], row, 0.0), axis=1, keepdims=True)
             coef = jnp.broadcast_to(coef, (SUB, LANES))[0:nb]
             for first in range(0, CHUNKS, SUB):
-                parts = [bases[p, :, c * LANES : (c + 1) * LANES] * coef for c in range(first, first + SUB)]
+                parts = [buf[p, :, c * LANES : (c + 1) * LANES] * coef for c in range(first, first + SUB)]
                 rows.append(sum_rows(parts, sub))
         rows = block_transpose(rows, sub, lane)
         for i, v in enumerate(rows):
@@ -431,29 +550,6 @@
         for b in range(-(-WIDE * fr.tiles // GROUP)):
             tiles = [p1[pl.ds(row + (b * GROUP + j) * SUB, SUB), :] for j in range(GROUP)]
             slab[main + b * SUB : main + (b + 1) * SUB, :] = pack_tiles(tiles, SUB, lane)
-
-
-def beyond(fr, info, *rest):
-    n2 = fr.sides[2]
-    z_in, outs = rest[:n2], rest[n2:]
-    _, lane = iotas()
-
-    def block(b):
-        sums = [[0.0] * GROUP for _ in range(3)]
-        for i, buf in enumerate(z_in):
-            lower = is_lower(info, 2, i)
-            pack = buf[pl.ds(b * SUB, SUB), :]
-            for m, (start, width) in enumerate(((0, H), (H, MARGIN), (H + MARGIN, MARGIN))):
-                shift = pick(lower, LANES - start, LANES - width - start)
-                low = pick(lower, 0, LANES - width)
-                keep = (lane >= low) & (lane < low + width)
-                for j in range(GROUP):
-                    sums[m][j] = sums[m][j] + jnp.where(keep, unpack_tile(pack, j, shift), 0.0)
-        for m, out in enumerate(outs):
-            for j in range(GROUP):
-                out[pl.ds((b * GROUP + j) * SUB, SUB), :] = sums[m][j]
-
-    loop(fr.blocks, block, 4)
 
 
 def gather_group(fr, off, first, live, fields, lane):
@@ -712,27 +808,30 @@
     return (t + 0.5) * (PIECE - t - 0.5) * (4.0 / (PIECE * PIECE))
 
 
-def lay_out(info, solved, basis):
+def lay_out(info, solved, basis, buf, sem):
     sub, lane = iotas()
-    groups = (info[0] + GROUP - 1) // GROUP
     count = GROUP * CHUNKS * 2
-
-    def one_group(group, _):
-        for c in range(0, CHUNKS, SUB):
-            values = []
-            for i in range(c, c + SUB):
-                values += [solved[group, s, i * SUB : (i + 1) * SUB, :] for s in range(2)]
-            for i, v in enumerate(block_transpose(values, sub, lane)):
-                basis[pl.ds(group * count + c * 2 + i, GROUP, stride=CHUNKS * 2), :] = v
-        return 0
-
-    lax.fori_loop(0, groups, one_group, 0)
-
-    def clear(group, _):
-        basis[pl.ds(pl.multiple_of(group * count, SUB), count), :] = jnp.zeros((count, LANES), F32)
-        return 0
-
-    lax.fori_loop(groups, basis.shape[0] // count, clear, 0)
+    copies = []
+    for group in range(solved.shape[0]):
+        some = group * GROUP < info[0]
+
+        @pl.when(some)
+        def _():
+            for c in range(0, CHUNKS, SUB):
+                values = []
+                for i in range(c, c + SUB):
+                    values += [solved[group, s, i * SUB : (i + 1) * SUB, :] for s in range(2)]
+                for i, v in enumerate(block_transpose(values, sub, lane)):
+                    buf[group, pl.ds(c * 2 + i, GROUP, stride=CHUNKS * 2), :] = v
+
+        @pl.when(jnp.logical_not(some))
+        def _():
+            buf[group] = jnp.zeros((count, LANES), F32)
+
+        copies.append(pltpu.make_async_copy(buf.at[group], basis.at[pl.ds(group * count, count)], sem.at[group]))
+        copies[-1].start()
+    for copy in copies:
+        copy.wait()
 
 
 def edge_planes(fr):
@@ -838,67 +937,77 @@
     live_rows = fr.live_blocks * SUB
 
     info = jnp.stack([live_pieces[0, 0, 0]] + [lax.axis_index(a).astype(jnp.int32) for a in axes])
-    off = jnp.swapaxes(offsets.reshape(slots, 3), 0, 1)
-    link = jnp.swapaxes(source_link.reshape(slots, 4), 0, 1)
-    coef = jnp.swapaxes(coarse_coef.reshape(nd, nb), 0, 1)
-    bases = resident_bases.reshape(slots, nb, cells)
-    raw = [a.reshape(bx * by, bz) for a in (kappa_base, labels, forcing)]
-
-    def stacked(own, received):
-        return call(stack, rows_of(own.shape[0] * (1 + len(received))), [own, *received], limit=4)
-
-    after_z = swap("gz", [coef] * n2)
-    width = 2 * MARGIN + H
-    slab = rows_of(width * by)
-    slabs = call(
+
+    def stays(a):
+        return pltpu.with_memory_space_constraint(a, pltpu.HBM)
+
+    raw = [stays(a.reshape(bx * by, bz)) for a in (kappa_base, labels, forcing)]
+    raw += [
+        stays(jnp.swapaxes(coarse_coef.reshape(nd, nb), 0, 1)),
+        stays(jnp.swapaxes(offsets.reshape(slots, 1, 3), 0, 2).reshape(3, 1, slots)),
+        stays(jnp.swapaxes(source_link.reshape(slots, 4), 0, 1)),
+    ]
+    bases = stays(resident_bases.reshape(slots, nb, cells))
+
+    core = rows_of(bx * by)
+    kap, frc, wgt, coefs, off, *slabs = call(
+        part(static_first, fr),
+        [core] * 3 + [rows_of(SUB), jax.ShapeDtypeStruct((SUB, LANES), jnp.int32)] + [rows_of(fr.z_rows + SUB)] * n2,
+        [info, stays(contrast), stays(channel_weight), *raw],
+        [SMEM] + [HBM] * 8,
+        [
+            pltpu.VMEM((bx * by, LANES), F32),
+            pltpu.VMEM((bx * by, LANES), jnp.int32),
+            pltpu.VMEM((nb, nd), F32),
+            pltpu.VMEM((3, 1, slots), jnp.int32),
+            pltpu.VMEM((4, slots), jnp.int32),
+            pltpu.SMEM((2, contrast.shape[0]), F32),
+            pltpu.SemaphoreType.DMA((8,)),
+        ],
+    )
+    z_static = swap("gz", slabs)
+    each = (1 + n2) * SUB
+    coefs, *slabs = call(
         part(static_x, fr),
-        [slab] * n0,
-        [info, contrast, channel_weight, *raw],
-        [SMEM] + [HBM] * 5,
-        [
-            pltpu.VMEM((n0, H * by, LANES), F32),
-            pltpu.VMEM((n0, H * by, LANES), jnp.int32),
-            pltpu.SMEM((2, contrast.shape[0]), F32),
-            pltpu.SemaphoreType.DMA((n0, 3)),
-            pltpu.SemaphoreType.DMA((2,)),
-        ],
-    )
-    after_z, slabs = lax.optimization_barrier((after_z, slabs))
-    coef = stacked(coef, after_z)
-    after_y = swap("gy", [coef] * n1)
-    static_x_in = swap("gx", slabs)
-    coef = stacked(coef, after_y)
-    after_x = swap("gx", [coef] * n0)
-    tables, raw, _ = lax.optimization_barrier((jnp.stack([contrast, channel_weight]), raw, slabs))
-    slab = rows_of(fr.xf * width)
-    k0, f0, w0, *slabs = call(
+        [rows_of(each)] + [rows_of(WIDTH * by + n2 * fr.x_pack + each)] * n0,
+        [info, kap, frc, wgt, coefs, *z_static],
+        [SMEM],
+    )
+    x_static = swap("gx", slabs)
+    each *= 1 + n0
+    k0, f0, w0, coefs, *slabs = call(
         part(static_y, fr),
-        [fr.frame] * 3 + [slab] * n1,
-        [info, tables, *raw, *static_x_in],
-        [SMEM] * 2,
-    )
-    after_x, slabs = lax.optimization_barrier((after_x, slabs))
-    static_y_in = swap("gy", slabs)
+        [fr.frame] * 3 + [rows_of(each)] + [rows_of(fr.y_rows + n2 * fr.y_pack + each)] * n1,
+        [info, kap, frc, wgt, coefs, *z_static, *x_static],
+        [SMEM],
+        [pltpu.VMEM((fr.y_pack * GROUP, LANES), F32)],
+    )
+    y_static = swap("gy", slabs)
 
     together = 4 if slots % 4 == 0 else 1
     p0, p1, *slabs = call(
         part(prolong, fr, (nb, together)),
         [fr.frame] * 2 + [rows_of(live_rows)] * n2,
-        [info, off, link, bases, coef, *after_x],
-        [SMEM] * 3,
-        [pltpu.VMEM((27, SUB, LANES), F32), pltpu.VMEM((together * CHUNKS // SUB, SUB, LANES), F32)],
+        [info, off, bases, coefs, *y_static],
+        [SMEM] * 2 + [HBM],
+        [
+            pltpu.VMEM((27, SUB, LANES), F32),
+            pltpu.VMEM((together * CHUNKS // SUB, SUB, LANES), F32),
+            pltpu.VMEM((slots, nb, cells), F32),
+            pltpu.SemaphoreType.DMA((slots,)),
+        ],
         limit=16,
     )
     received = swap("gz", slabs)
-    k0, f0, w0, *slabs = call(
-        part(static_z, fr),
-        [fr.frame] * 3 + [rows_of(fr.blocks * SUB)] * n2,
-        [info, k0, f0, w0, *static_y_in],
+    k0, f0, w0, k1, f1, w1 = call(
+        part(static_end, fr),
+        [fr.frame] * 6,
+        [info, k0, f0, w0, *z_static, *x_static, *y_static],
         [SMEM],
         alias={1: 0, 2: 1, 3: 2},
-    )
-    received, slabs = lax.optimization_barrier((received, slabs))
-    static_z_in = swap("gz", slabs)
+        limit=16,
+    )
+    received, k1 = lax.optimization_barrier((received, k1))
     p0, p1, *slabs = call(
         part(coarse_y, fr),
         [fr.frame] * 2 + [rows_of(fr.live_x * (WIDE + 2))] * n1,
@@ -907,16 +1016,6 @@
         alias={1: 0, 2: 1},
     )
     received = swap("gy", slabs)
-    k1, f1, w1 = call(part(beyond, fr), [fr.frame] * 3, [info, *static_z_in], [SMEM])
-    received, k1 = lax.optimization_barrier((received, k1))
-    p0, p1, *slabs = call(
-        part(coarse_x, fr),
-        [fr.frame] * 2 + [rows_of(WIDE * fr.yf + -(-WIDE * fr.tiles // GROUP) * SUB)] * n0,
-        [info, p0, p1, *received],
-        [SMEM],
-        alias={1: 0, 2: 1},
-    )
-    received = swap("gx", slabs)
     groups = slots // GROUP
     wt, scales, weights = call(
         part(couple, fr),
@@ -930,6 +1029,15 @@
         [pltpu.VMEM((PROWS + 2 * PIECE, LANES), F32)],
         limit=16,
     )
+    received, wt = lax.optimization_barrier((received, wt))
+    p0, p1, *slabs = call(
+        part(coarse_x, fr),
+        [fr.frame] * 2 + [rows_of(WIDE * fr.yf + -(-WIDE * fr.tiles // GROUP) * SUB)] * n0,
+        [info, p0, p1, *received],
+        [SMEM],
+        alias={1: 0, 2: 1},
+    )
+    received = swap("gx", slabs)
 
     solve = pltpu.VMEM((2, PROWS, LANES), F32)
     padded = pltpu.VMEM((2, PROWS + 2 * PIECE, LANES), F32)
@@ -949,7 +1057,14 @@
     )
 
     z_in = swap("gz", [slab] * n2)
-    basis = call(lay_out, rows_of(slots * CHUNKS * 2), [info, solved], [SMEM])
+    basis = call(
+        lay_out,
+        rows_of(slots * CHUNKS * 2),
+        [info, solved],
+        [SMEM],
+        [pltpu.VMEM((groups, GROUP * CHUNKS * 2, LANES), F32), pltpu.SemaphoreType.DMA((groups,))],
+        out_spec=ANY,
+    )
     z_in, basis = lax.optimization_barrier((z_in, basis))
     slabs = call(
         part(fold_y, fr),

time: 114 us -> 107 us (0.939)
  starting transfers between devices: 42.1 us -> 27.4 us
  waiting for transfers between devices: 17.5 us -> 30 us
  local copies, waits for them, and re-layouts: 12.1 us -> 0 us
  Pallas kernels: 38.4 us -> 46 us
    ppermute x20 -> x15, starting transfers between devices: 42.1 us -> 27.4 us  [swap(): lax.ppermute(slab, axis, pairs + [(j, i) for i, j in pairs])]
    ppermute x20 -> x15, waiting for transfers between devices: 17.5 us -> 30 us  [swap(): lax.ppermute(slab, axis, pairs + [(j, i) for i, j in pairs])]
    unnamed x23 -> x0, local copies, waits for them, and re-layouts: 12.1 us -> none
    pallas_call x15 -> x13, Pallas kernels: 38.4 us -> 46 us  [call(): pl.pallas_call(kernel, out_shape=outs, in_specs=specs, out_specs=jax.tree...]
  transfers between devices with their start and end apart: 20 -> 15, of which waited for: 7 -> 12; matrix products, arithmetic and copies ran while one was open for 1% -> 0% of each run, Pallas kernels for 16% -> 10%
where the time goes in v2:
time: 107 us; the launch traced here: 105 us
  Pallas kernels  46 us (43%)
  waiting for transfers between devices  30 us (28%)
  starting transfers between devices  27.4 us (26%)
  between operations  1.49 us (1%)
    pallas_call x13, Pallas kernels, call(): pl.pallas_call(kernel, out_shape=outs, in_specs=specs, out_specs=jax.tree...  46 us
    ppermute x15, waiting for transfers between devices, swap(): lax.ppermute(slab, axis, pairs + [(j, i) for i, j in pairs])  30 us
    ppermute x15, starting transfers between devices, swap(): lax.ppermute(slab, axis, pairs + [(j, i) for i, j in pairs])  27.4 us
  transfers between devices with their start and end apart: 15, of which 12 were waited for; matrix products, arithmetic and copies ran while one was open for 0% of the time, Pallas kernels for 10%

profile of v2, /device:TPU:10, one launch (start us, length us, event | category | flops | bytes accessed | tf_op | source)
XLA Modules:
  0.0 105.0 jit_solution(17203683312053724967)
XLA Ops:
  1.3 0.1 pad_add_fusion.info
  1.4 3.1 %shard_map.113 = (f32[1024,128]{1,0:T(8,128)S(1)}, f32[1024,128]{1,0:T(8,128)S(1)}, f32[1024,128]{1,0:T(8,128)S(1)}, f32[8,128]{1,0:T(8,128)S(1)}, s32[8,128]{1,0:T(8,128)S(1)}, /*index=5*/f32[136,128]{1,0:T(8,128)S(1)}) custom-call(s32[4]{0:T(128)S(1)} %pad_add_fusion.info, f32[4]{0:T(128)} %contrast.1, f32[4]{0:T(128)} %channel.1, f32[1024,128]{1,0:T(8,128)} %bitcast.27, ...), custom_call_target="tpu_custom_call" | custom-call | tf_op jit(solution)/shard_map/pallas_call | solution.py:125
  4.5 1.6 %collective-permute-start = (f32[136,128]{1,0:T(8,128)S(1)}, f32[136,128]{1,0:T(8,128)S(1)}, u32[]{:S(2)}, u32[]{:S(2)}) collective-permute-start(f32[136,128]{1,0:T(8,128)S(1)} %get-tuple-element.58), channel_id=1, source_target_pairs={{0,1},{1,0},{2,3},{3,2},{4,5},{5,4},{6,7},{7,6},{8,9},{9,8},{10,11... | collective-permute-start | bytes 208904 | tf_op jit(solution)/shard_map/ppermute | solution.py:145
  6.1 2.8 %collective-permute-done.rest_0_ = f32[136,128]{1,0:T(8,128)S(1)} collective-permute-done((f32[136,128]{1,0:T(8,128)S(1)}, f32[136,128]{1,0:T(8,128)S(1)}, u32[]{:S(2)}, u32[]{:S(2)}) %collective-permute-start) | collective-permute-done | bytes 69664 | tf_op jit(solution)/shard_map/ppermute | solution.py:145
  8.9 0.6 shard_map.114
  9.4 0.5 collective-permute-start.1
  10.0 4.6 %collective-permute-start.2 = (f32[456,128]{1,0:T(8,128)S(1)}, f32[456,128]{1,0:T(8,128)S(1)}, u32[]{:S(2)}, u32[]{:S(2)}) collective-permute-start(f32[456,128]{1,0:T(8,128)S(1)} %get-tuple-element.61), channel_id=1, source_target_pairs={{8,16},{16,8},{9,17},{17,9},{10,18},{18,10},{11,19},{19,11},{12,20... | collective-permute-start | bytes 700424 | tf_op jit(solution)/shard_map/ppermute | solution.py:145
  14.6 1.2 %collective-permute-done.1.rest_1_ = f32[456,128]{1,0:T(8,128)S(1)} collective-permute-done((f32[456,128]{1,0:T(8,128)S(1)}, f32[456,128]{1,0:T(8,128)S(1)}, u32[]{:S(2)}, u32[]{:S(2)}) %collective-permute-start.1) | collective-permute-done | bytes 233504 | tf_op jit(solution)/shard_map/ppermute | solution.py:145
  15.8 3.0 %collective-permute-done.2.rest_2_ = f32[456,128]{1,0:T(8,128)S(1)} collective-permute-done((f32[456,128]{1,0:T(8,128)S(1)}, f32[456,128]{1,0:T(8,128)S(1)}, u32[]{:S(2)}, u32[]{:S(2)}) %collective-permute-start.2) | collective-permute-done | bytes 233504 | tf_op jit(solution)/shard_map/ppermute | solution.py:145
  18.8 1.4 %shard_map.115 = (f32[2048,128]{1,0:T(8,128)S(1)}, f32[2048,128]{1,0:T(8,128)S(1)}, f32[2048,128]{1,0:T(8,128)S(1)}, f32[48,128]{1,0:T(8,128)S(1)}, f32[648,128]{1,0:T(8,128)S(1)}, /*index=5*/f32[648,128]{1,0:T(8,128)S(1)}) custom-call(s32[4]{0:T(128)S(1)} %pad_add_fusion.info, f32[1024,128]{1,0:T(8,128)S(1)} %get-tuple-element.54.kap, ...), custom_call_target="tpu_custom_call" | custom-call | tf_op jit(solution)/shard_map/pallas_call | solution.py:125
  20.2 0.1 collective-permute-start.3
  20.3 2.5 %collective-permute-start.4 = (f32[648,128]{1,0:T(8,128)S(1)}, f32[648,128]{1,0:T(8,128)S(1)}, u32[]{:S(2)}, u32[]{:S(2)}) collective-permute-start(f32[648,128]{1,0:T(8,128)S(1)} %get-tuple-element.64), channel_id=1, source_target_pairs={{2,4},{4,2},{3,5},{5,3},{10,12},{12,10},{11,13},{13,11},{18,20},{2... | collective-permute-start | bytes 995336 | tf_op jit(solution)/shard_map/ppermute | solution.py:145
  22.9 0.0 collective-permute-done.3.rest_0_.rest_3_
  22.9 5.9 %collective-permute-done.4.rest_1_.rest_4_ = f32[648,128]{1,0:T(8,128)S(1)} collective-permute-done((f32[648,128]{1,0:T(8,128)S(1)}, f32[648,128]{1,0:T(8,128)S(1)}, u32[]{:S(2)}, u32[]{:S(2)}) %collective-permute-start.4) | collective-permute-done | bytes 331808 | tf_op jit(solution)/shard_map/ppermute | solution.py:145
  28.8 5.9 %shard_map.116 = (f32[2048,128]{1,0:T(8,128)S(1)}, f32[2048,128]{1,0:T(8,128)S(1)}, f32[240,128]{1,0:T(8,128)S(1)}) custom-call(s32[4]{0:T(128)S(1)} %pad_add_fusion.info, s32[8,128]{1,0:T(8,128)S(1)} %get-tuple-element.53.off, f32[40,8,4096]{2,1,0:T(8,128)} %bitcast.24, f32[48,128]{1,0:T(8,128)S(1)} %get-tuple-element.62.own, ...), custom_call_target="tpu_custom_call" | custom-call | tf_op jit(solution)/shard_map/pallas_call | solution.py:125
  34.6 0.1 collective-permute-start.5
  34.7 2.5 %shard_map.117 = (f32[2048,128]{1,0:T(8,128)S(1)}, f32[2048,128]{1,0:T(8,128)S(1)}, f32[2048,128]{1,0:T(8,128)S(1)}, f32[2048,128]{1,0:T(8,128)S(1)}, f32[2048,128]{1,0:T(8,128)S(1)}, /*index=5*/f32[2048,128]{1,0:T(8,128)S(1)}) custom-call(s32[4]{0:T(128)S(1)} %pad_add_fusion.info, ...), custom_call_target="tpu_custom_call", output_to_operand_aliasing={{0}: (1, {}), {1}: (2, {}), {2}: (3, {})} | custom-call | tf_op jit(solution)/shard_map/pallas_call | solution.py:125
  37.2 2.4 %collective-permute-done.5.rest_0_ = f32[240,128]{1,0:T(8,128)S(1)} collective-permute-done((f32[240,128]{1,0:T(8,128)S(1)}, f32[240,128]{1,0:T(8,128)S(1)}, u32[]{:S(2)}, u32[]{:S(2)}) %collective-permute-start.5) | collective-permute-done | bytes 122912 | tf_op jit(solution)/shard_map/ppermute | solution.py:145
  39.6 1.9 %shard_map.118 = (f32[2048,128]{1,0:T(8,128)S(1)}, f32[2048,128]{1,0:T(8,128)S(1)}, f32[440,128]{1,0:T(8,128)S(1)}, f32[440,128]{1,0:T(8,128)S(1)}) custom-call(s32[4]{0:T(128)S(1)} %pad_add_fusion.info, f32[2048,128]{1,0:T(8,128)S(1)} %get-tuple-element.65.p0_in, ...), custom_call_target="tpu_custom_call", output_to_operand_aliasing={{0}: (1, {}), {1}: (2, {})} | custom-call | tf_op jit(solution)/shard_map/pallas_call | solution.py:125
  41.5 0.1 collective-permute-start.6
  41.5 1.9 %collective-permute-start.7 = (f32[440,128]{1,0:T(8,128)S(1)}, f32[440,128]{1,0:T(8,128)S(1)}, u32[]{:S(2)}, u32[]{:S(2)}) collective-permute-start(f32[440,128]{1,0:T(8,128)S(1)} %get-tuple-element.76), channel_id=1, source_target_pairs={{2,4},{4,2},{3,5},{5,3},{10,12},{12,10},{11,13},{13,11},{18,20},{2... | collective-permute-start | bytes 675848 | tf_op jit(solution)/shard_map/ppermute | solution.py:145
  43.5 4.4 %shard_map.119 = (f32[5,6,256,128]{3,2,1,0:T(8,128)S(1)}, f32[5,256,128]{2,1,0:T(8,128)S(1)}, f32[5,256,128]{2,1,0:T(8,128)S(1)}) custom-call(s32[4]{0:T(128)S(1)} %pad_add_fusion.info, s32[8,128]{1,0:T(8,128)S(1)} %get-tuple-element.53.off, f32[2048,128]{1,0:T(8,128)S(1)} %get-tuple-element.77.k0, f32[2048,128]{1,0:T(8,128)S(1)} %get-tuple-element.78.k1, ...), custom_call_target="tpu_custom_call" | custom-call | tf_op jit(solution)/shard_map/pallas_call | solution.py:125
  47.9 0.0 collective-permute-done.6.rest_0_
  47.9 0.9 collective-permute-done.7.rest_1_
  48.8 1.2 %shard_map.120 = (f32[2048,128]{1,0:T(8,128)S(1)}, f32[2048,128]{1,0:T(8,128)S(1)}, f32[488,128]{1,0:T(8,128)S(1)}, f32[488,128]{1,0:T(8,128)S(1)}) custom-call(s32[4]{0:T(128)S(1)} %pad_add_fusion.info, f32[2048,128]{1,0:T(8,128)S(1)} %get-tuple-element.73.p0_in, ...), custom_call_target="tpu_custom_call", output_to_operand_aliasing={{0}: (1, {}), {1}: (2, {})} | custom-call | tf_op jit(solution)/shard_map/pallas_call | solution.py:125
  50.1 0.1 collective-permute-start.8
  50.2 4.0 %collective-permute-start.9 = (f32[488,128]{1,0:T(8,128)S(1)}, f32[488,128]{1,0:T(8,128)S(1)}, u32[]{:S(2)}, u32[]{:S(2)}) collective-permute-start(f32[488,128]{1,0:T(8,128)S(1)} %get-tuple-element.92), channel_id=1, source_target_pairs={{8,16},{16,8},{9,17},{17,9},{10,18},{18,10},{11,19},{19,11},{12,20... | collective-permute-start | bytes 749576 | tf_op jit(solution)/shard_map/ppermute | solution.py:145
  54.2 2.2 %collective-permute-done.8.rest_0_ = f32[488,128]{1,0:T(8,128)S(1)} collective-permute-done((f32[488,128]{1,0:T(8,128)S(1)}, f32[488,128]{1,0:T(8,128)S(1)}, u32[]{:S(2)}, u32[]{:S(2)}) %collective-permute-start.8) | collective-permute-done | bytes 249888 | tf_op jit(solution)/shard_map/ppermute | solution.py:145
  56.4 2.0 %collective-permute-done.9.rest_1_ = f32[488,128]{1,0:T(8,128)S(1)} collective-permute-done((f32[488,128]{1,0:T(8,128)S(1)}, f32[488,128]{1,0:T(8,128)S(1)}, u32[]{:S(2)}, u32[]{:S(2)}) %collective-permute-start.9) | collective-permute-done | bytes 249888 | tf_op jit(solution)/shard_map/ppermute | solution.py:145
  58.4 18.3 %shard_map.121 = (f32[1024,128]{1,0:T(8,128)S(1)}, f32[5,2,256,128]{3,2,1,0:T(8,128)S(1)}, f32[640,128]{1,0:T(8,128)S(1)}, f32[256,128]{1,0:T(8,128)S(1)}, f32[240,128]{1,0:T(8,128)S(1)}) custom-call(s32[4]{0:T(128)S(1)} %pad_add_fusion.info, s32[8,128]{1,0:T(8,128)S(1)} %get-tuple-element.53.off, f32[2048,128]{1,0:T(8,128)S(1)} %get-tuple-element.84.p0, ...), custom_call_target="tpu_custom_call" | custom-call | tf_op jit(solution)/shard_map/pallas_call | solution.py:125
  76.8 0.1 collective-permute-start.10
  76.8 3.4 %shard_map.122 = f32[2560,128]{1,0:T(8,128)} custom-call(s32[4]{0:T(128)S(1)} %pad_add_fusion.info, f32[5,2,256,128]{3,2,1,0:T(8,128)S(1)} %get-tuple-element.95.solved), custom_call_target="tpu_custom_call" | custom-call | tf_op jit(solution)/shard_map/pallas_call | solution.py:125
  80.2 1.5 %collective-permute-done.10.rest_0_ = f32[240,128]{1,0:T(8,128)S(1)} collective-permute-done((f32[240,128]{1,0:T(8,128)S(1)}, f32[240,128]{1,0:T(8,128)S(1)}, u32[]{:S(2)}, u32[]{:S(2)}) %collective-permute-start.10) | collective-permute-done | bytes 122912 | tf_op jit(solution)/shard_map/ppermute | solution.py:145
  81.7 0.8 shard_map.123
  82.6 0.1 collective-permute-start.11
  82.6 1.9 %collective-permute-start.12 = (f32[160,128]{1,0:T(8,128)S(1)}, f32[160,128]{1,0:T(8,128)S(1)}, u32[]{:S(2)}, u32[]{:S(2)}) collective-permute-start(f32[160,128]{1,0:T(8,128)S(1)} %get-tuple-element.99), channel_id=1, source_target_pairs={{2,4},{4,2},{3,5},{5,3},{10,12},{12,10},{11,13},{13,11},{18,20},{2... | collective-permute-start | bytes 245768 | tf_op jit(solution)/shard_map/ppermute | solution.py:145
  84.6 0.0 collective-permute-done.11.rest_1_
  84.6 3.8 %collective-permute-done.12.rest_2_ = f32[160,128]{1,0:T(8,128)S(1)} collective-permute-done((f32[160,128]{1,0:T(8,128)S(1)}, f32[160,128]{1,0:T(8,128)S(1)}, u32[]{:S(2)}, u32[]{:S(2)}) %collective-permute-start.12) | collective-permute-done | bytes 81952 | tf_op jit(solution)/shard_map/ppermute | solution.py:145
  88.4 0.7 shard_map.124
  89.1 7.9 %collective-permute-start.13 = (f32[128,128]{1,0:T(8,128)S(1)}, f32[128,128]{1,0:T(8,128)S(1)}, u32[]{:S(2)}, u32[]{:S(2)}) collective-permute-start(f32[128,128]{1,0:T(8,128)S(1)} %get-tuple-element.101), channel_id=1, source_target_pairs={{0,8},{16,24},{8,0},{24,16},{1,9},{17,25},{9,1},{25,17},{2,10},{18... | collective-permute-start | bytes 196616 | tf_op jit(solution)/shard_map/ppermute | solution.py:145
  97.0 1.9 %collective-permute-start.14 = (f32[128,128]{1,0:T(8,128)S(1)}, f32[128,128]{1,0:T(8,128)S(1)}, u32[]{:S(2)}, u32[]{:S(2)}) collective-permute-start(f32[128,128]{1,0:T(8,128)S(1)} %get-tuple-element.102), channel_id=1, source_target_pairs={{8,16},{16,8},{9,17},{17,9},{10,18},{18,10},{11,19},{19,11},{12,20... | collective-permute-start | bytes 196616 | tf_op jit(solution)/shard_map/ppermute | solution.py:145
  98.9 0.3 collective-permute-done.13.rest_3_
  99.2 3.9 %collective-permute-done.14.rest_4_ = f32[128,128]{1,0:T(8,128)S(1)} collective-permute-done((f32[128,128]{1,0:T(8,128)S(1)}, f32[128,128]{1,0:T(8,128)S(1)}, u32[]{:S(2)}, u32[]{:S(2)}) %collective-permute-start.14) | collective-permute-done | bytes 65568 | tf_op jit(solution)/shard_map/ppermute | solution.py:145
  103.1 1.8 %shard_map.125 = f32[1024,128]{1,0:T(8,128)} custom-call(s32[4]{0:T(128)S(1)} %pad_add_fusion.info, f32[1024,128]{1,0:T(8,128)S(1)} %get-tuple-element.93.core, f32[240,128]{1,0:T(8,128)S(1)} %collective-permute-done.10.rest_0_, f32[160,128]{1,0:T(8,128)S(1)} %collective-permute-done.11.rest_1_, f32[160,128]{1,0:T(8,128)S(1)} %collective-permute-done.12.rest_2_, ...), custom_call_target="tpu_custom_call" | custom-call | tf_op jit(solution)/shard_map/pallas_call | solution.py:125
Async XLA Ops:
  4.5 4.4 %collective-permute-start = (f32[136,128]{1,0:T(8,128)S(1)}, f32[136,128]{1,0:T(8,128)S(1)}, u32[]{:S(2)}, u32[]{:S(2)}) collective-permute-start(f32[136,128]{1,0:T(8,128)S(1)} %get-tuple-element.58), channel_id=1, source_target_pairs={{0,1},{1,0},{2,3},{3,2},{4,5},{5,4},{6,7},{7,6},{8,9},{9,8},{10,11... | collective-permute-start | bytes 208904 | tf_op jit(solution)/shard_map/ppermute | solution.py:145
  9.4 6.3 %collective-permute-start.1 = (f32[456,128]{1,0:T(8,128)S(1)}, f32[456,128]{1,0:T(8,128)S(1)}, u32[]{:S(2)}, u32[]{:S(2)}) collective-permute-start(f32[456,128]{1,0:T(8,128)S(1)} %get-tuple-element.60), channel_id=1, source_target_pairs={{0,8},{16,24},{8,0},{24,16},{1,9},{17,25},{9,1},{25,17},{2,10},{18... | collective-permute-start | bytes 700424 | tf_op jit(solution)/shard_map/ppermute | solution.py:145
  10.0 8.9 %collective-permute-start.2 = (f32[456,128]{1,0:T(8,128)S(1)}, f32[456,128]{1,0:T(8,128)S(1)}, u32[]{:S(2)}, u32[]{:S(2)}) collective-permute-start(f32[456,128]{1,0:T(8,128)S(1)} %get-tuple-element.61), channel_id=1, source_target_pairs={{8,16},{16,8},{9,17},{17,9},{10,18},{18,10},{11,19},{19,11},{12,20... | collective-permute-start | bytes 700424 | tf_op jit(solution)/shard_map/ppermute | solution.py:145
  20.2 2.6 %collective-permute-start.3 = (f32[648,128]{1,0:T(8,128)S(1)}, f32[648,128]{1,0:T(8,128)S(1)}, u32[]{:S(2)}, u32[]{:S(2)}) collective-permute-start(f32[648,128]{1,0:T(8,128)S(1)} %get-tuple-element.63), channel_id=1, source_target_pairs={{0,2},{4,6},{2,0},{6,4},{1,3},{5,7},{3,1},{7,5},{8,10},{12,14},{10... | collective-permute-start | bytes 995336 | tf_op jit(solution)/shard_map/ppermute | solution.py:145
  20.3 8.4 %collective-permute-start.4 = (f32[648,128]{1,0:T(8,128)S(1)}, f32[648,128]{1,0:T(8,128)S(1)}, u32[]{:S(2)}, u32[]{:S(2)}) collective-permute-start(f32[648,128]{1,0:T(8,128)S(1)} %get-tuple-element.64), channel_id=1, source_target_pairs={{2,4},{4,2},{3,5},{5,3},{10,12},{12,10},{11,13},{13,11},{18,20},{2... | collective-permute-start | bytes 995336 | tf_op jit(solution)/shard_map/ppermute | solution.py:145
  34.6 4.9 %collective-permute-start.5 = (f32[240,128]{1,0:T(8,128)S(1)}, f32[240,128]{1,0:T(8,128)S(1)}, u32[]{:S(2)}, u32[]{:S(2)}) collective-permute-start(f32[240,128]{1,0:T(8,128)S(1)} %get-tuple-element.67), channel_id=1, source_target_pairs={{0,1},{1,0},{2,3},{3,2},{4,5},{5,4},{6,7},{7,6},{8,9},{9,8},{10,11... | collective-permute-start | bytes 368648 | tf_op jit(solution)/shard_map/ppermute | solution.py:145
  41.5 6.4 %collective-permute-start.6 = (f32[440,128]{1,0:T(8,128)S(1)}, f32[440,128]{1,0:T(8,128)S(1)}, u32[]{:S(2)}, u32[]{:S(2)}) collective-permute-start(f32[440,128]{1,0:T(8,128)S(1)} %get-tuple-element.75), channel_id=1, source_target_pairs={{0,2},{4,6},{2,0},{6,4},{1,3},{5,7},{3,1},{7,5},{8,10},{12,14},{10... | collective-permute-start | bytes 675848 | tf_op jit(solution)/shard_map/ppermute | solution.py:145
  41.5 7.3 %collective-permute-start.7 = (f32[440,128]{1,0:T(8,128)S(1)}, f32[440,128]{1,0:T(8,128)S(1)}, u32[]{:S(2)}, u32[]{:S(2)}) collective-permute-start(f32[440,128]{1,0:T(8,128)S(1)} %get-tuple-element.76), channel_id=1, source_target_pairs={{2,4},{4,2},{3,5},{5,3},{10,12},{12,10},{11,13},{13,11},{18,20},{2... | collective-permute-start | bytes 675848 | tf_op jit(solution)/shard_map/ppermute | solution.py:145
  50.1 6.4 %collective-permute-start.8 = (f32[488,128]{1,0:T(8,128)S(1)}, f32[488,128]{1,0:T(8,128)S(1)}, u32[]{:S(2)}, u32[]{:S(2)}) collective-permute-start(f32[488,128]{1,0:T(8,128)S(1)} %get-tuple-element.91), channel_id=1, source_target_pairs={{0,8},{16,24},{8,0},{24,16},{1,9},{17,25},{9,1},{25,17},{2,10},{18... | collective-permute-start | bytes 749576 | tf_op jit(solution)/shard_map/ppermute | solution.py:145
  50.2 8.3 %collective-permute-start.9 = (f32[488,128]{1,0:T(8,128)S(1)}, f32[488,128]{1,0:T(8,128)S(1)}, u32[]{:S(2)}, u32[]{:S(2)}) collective-permute-start(f32[488,128]{1,0:T(8,128)S(1)} %get-tuple-element.92), channel_id=1, source_target_pairs={{8,16},{16,8},{9,17},{17,9},{10,18},{18,10},{11,19},{19,11},{12,20... | collective-permute-start | bytes 749576 | tf_op jit(solution)/shard_map/ppermute | solution.py:145
  76.8 4.9 %collective-permute-start.10 = (f32[240,128]{1,0:T(8,128)S(1)}, f32[240,128]{1,0:T(8,128)S(1)}, u32[]{:S(2)}, u32[]{:S(2)}) collective-permute-start(f32[240,128]{1,0:T(8,128)S(1)} %get-tuple-element.94), channel_id=1, source_target_pairs={{0,1},{1,0},{2,3},{3,2},{4,5},{5,4},{6,7},{7,6},{8,9},{9,8},{10,11... | collective-permute-start | bytes 368648 | tf_op jit(solution)/shard_map/ppermute | solution.py:145
  82.6 2.0 %collective-permute-start.11 = (f32[160,128]{1,0:T(8,128)S(1)}, f32[160,128]{1,0:T(8,128)S(1)}, u32[]{:S(2)}, u32[]{:S(2)}) collective-permute-start(f32[160,128]{1,0:T(8,128)S(1)} %get-tuple-element.98), channel_id=1, source_target_pairs={{0,2},{4,6},{2,0},{6,4},{1,3},{5,7},{3,1},{7,5},{8,10},{12,14},{10... | collective-permute-start | bytes 245768 | tf_op jit(solution)/shard_map/ppermute | solution.py:145
  82.6 5.8 %collective-permute-start.12 = (f32[160,128]{1,0:T(8,128)S(1)}, f32[160,128]{1,0:T(8,128)S(1)}, u32[]{:S(2)}, u32[]{:S(2)}) collective-permute-start(f32[160,128]{1,0:T(8,128)S(1)} %get-tuple-element.99), channel_id=1, source_target_pairs={{2,4},{4,2},{3,5},{5,3},{10,12},{12,10},{11,13},{13,11},{18,20},{2... | collective-permute-start | bytes 245768 | tf_op jit(solution)/shard_map/ppermute | solution.py:145
  89.1 10.1 %collective-permute-start.13 = (f32[128,128]{1,0:T(8,128)S(1)}, f32[128,128]{1,0:T(8,128)S(1)}, u32[]{:S(2)}, u32[]{:S(2)}) collective-permute-start(f32[128,128]{1,0:T(8,128)S(1)} %get-tuple-element.101), channel_id=1, source_target_pairs={{0,8},{16,24},{8,0},{24,16},{1,9},{17,25},{9,1},{25,17},{2,10},{18... | collective-permute-start | bytes 196616 | tf_op jit(solution)/shard_map/ppermute | solution.py:145
  97.0 6.1 %collective-permute-start.14 = (f32[128,128]{1,0:T(8,128)S(1)}, f32[128,128]{1,0:T(8,128)S(1)}, u32[]{:S(2)}, u32[]{:S(2)}) collective-permute-start(f32[128,128]{1,0:T(8,128)S(1)} %get-tuple-element.102), channel_id=1, source_target_pairs={{8,16},{16,8},{9,17},{17,9},{10,18},{18,10},{11,19},{19,11},{12,20... | collective-permute-start | bytes 196616 | tf_op jit(solution)/shard_map/ppermute | solution.py:145

commit v3 on v2

--- a/solution.py
+++ b/solution.py
@@ -126,7 +126,7 @@
         kernel,
         out_shape=outs,
         in_specs=specs,
-        out_specs=jax.tree.map(lambda _: out_spec, outs),
+        out_specs=out_spec if isinstance(out_spec, list) else jax.tree.map(lambda _: out_spec, outs),
         scratch_shapes=list(scratch),
         input_output_aliases=alias or {},
         compiler_params=pltpu.CompilerParams(vmem_limit_bytes=limit * 1024 * 1024),
@@ -204,7 +204,7 @@
             slab[pl.ds(b * SUB, SUB), :] = mix
 
     count = fr.bx * fr.by // (GROUP * SUB)
-    loop(count, block, 2)
+    loop(count, block, 4)
     for slab in slabs:
         slab[count * SUB : (count + 1) * SUB, :] = own[...]
 
@@ -234,9 +234,18 @@
     return pick(lower, fr.bx + H, 0), pick(lower, 0, 1)
 
 
-def static_y(fr, info, kap, frc, wgt, coefs_in, *rest):
+def stack(fr, own, *rest):
+    x_in, out = rest[:-1], rest[-1]
+    each = own.shape[0]
+    out[0:each, :] = own[...]
+    row = WIDTH * fr.by + fr.sides[2] * fr.x_pack
+    for i, buf in enumerate(x_in):
+        out[(1 + i) * each : (2 + i) * each, :] = buf[row : row + each, :]
+
+
+def static_y(fr, info, kap, frc, wgt, *rest):
     n0, n1, n2 = fr.sides
-    z_in, x_in, (k0, f0, w0, coefs), rest = rest[:n2], rest[n2 : n0 + n2], rest[n0 + n2 : n0 + n2 + 4], rest[n0 + n2 + 4 :]
+    z_in, x_in, (k0, f0, w0), rest = rest[:n2], rest[n2 : n0 + n2], rest[n0 + n2 : n0 + n2 + 3], rest[n0 + n2 + 3 :]
     slabs, tall = rest[:n1], rest[n1]
     _, lane = iotas()
     by, yf, per = fr.by, fr.yf, fr.by // SUB
@@ -251,11 +260,7 @@
                 frame[dst, :] = ref[src, :]
 
     loop(fr.bx, core, 4)
-    each = coefs_in.shape[0]
-    coefs[0:each, :] = coefs_in[...]
-    c_in = WIDTH * by + n2 * fr.x_pack
     for i, buf in enumerate(x_in):
-        coefs[(1 + i) * each : (2 + i) * each, :] = buf[c_in : c_in + each, :]
         lower = is_lower(info, 0, i)
         for frame, count, at in zip((k0, f0, w0), DEPTH, FIRST):
             first = pick(lower, fr.bx + H, H - count)
@@ -296,7 +301,6 @@
                 tiles = [tall[(b * GROUP + j) * SUB : (b * GROUP + j + 1) * SUB, :] for j in range(GROUP)]
                 slab[row : row + SUB, :] = pack_tiles(tiles, 0, lane)
                 row += SUB
-        slab[row : row + coefs.shape[0], :] = coefs[...]
 
 
 def static_end(fr, info, k_in, f_in, w_in, *rest):
@@ -392,29 +396,35 @@
             ref[a, :] = v
 
 
+def fetch(info, bases, out, sem):
+    def copy(p):
+        return pltpu.make_async_copy(bases.at[p], out.at[p], sem.at[p])
+
+    def start(p, _):
+        copy(p).start()
+        return 0
+
+    def wait(p, _):
+        copy(p).wait()
+        return 0
+
+    lax.fori_loop(0, info[0], start, 0)
+    lax.fori_loop(0, info[0], wait, 0)
+
+
 def prolong(fr, shape, info, off, bases, own, *rest):
     nb, together = shape
     n, m = fr.sides[1], fr.sides[2]
     received, (p0, p1), slabs = rest[:n], rest[n : n + 2], rest[n + 2 : n + m + 2]
-    table, keep, buf, sem = rest[n + m + 2 :]
+    table, keep = rest[n + m + 2 :]
     sub, lane = iotas()
     live = info[0]
-
-    def copy(p):
-        return pltpu.make_async_copy(bases.at[p], buf.at[p], sem.at[p])
-
-    def start(p, _):
-        copy(p).start()
-        return 0
-
-    lax.fori_loop(0, live, start, 0)
     zero(p0)
     zero(p1)
     each = (1 + fr.sides[0]) * (1 + m)
     for i, ref in enumerate((own, *received)):
         for j in range(each):
-            row = j * SUB + (fr.y_rows + m * fr.y_pack if i else 0)
-            table[i * each + j] = ref[row : row + SUB, :]
+            table[i * each + j] = ref[j * SUB : (j + 1) * SUB, :]
 
     def position(axis, step):
         came = 1 + ((info[1 + axis] + jnp.where(step == 0, 1, 0)) & 1)
@@ -423,12 +433,6 @@
     def some(step, _):
         numbers = [step * together + i for i in range(together)]
         per = CHUNKS // SUB
-        for p in numbers:
-
-            @pl.when(p < live)
-            def _():
-                copy(p).wait()
-
         rows = []
         for p in numbers:
             at = [position(axis, off[4 + axis, p]) for axis in range(3)]
@@ -436,7 +440,7 @@
             coef = jnp.sum(jnp.where(lane == off[7, p], row, 0.0), axis=1, keepdims=True)
             coef = jnp.broadcast_to(coef, (SUB, LANES))[0:nb]
             for first in range(0, CHUNKS, SUB):
-                parts = [buf[p, :, c * LANES : (c + 1) * LANES] * coef for c in range(first, first + SUB)]
+                parts = [bases[p, :, c * LANES : (c + 1) * LANES] * coef for c in range(first, first + SUB)]
                 rows.append(sum_rows(parts, sub))
         rows = block_transpose(rows, sub, lane)
         for i, v in enumerate(rows):
@@ -573,7 +577,8 @@
     return tiles_at
 
 
-def couple(fr, info, off, k0, k1, w0, w1, wt, scales, weights, kb):
+def couple(fr, part, info, off, k0, k1, w0, w1, *rest):
+    wt, scales, weights, kb = rest[-4:]
     sub, lane = iotas()
     live = info[0]
     first_y, last_y = sub == 0, sub == SUB - 1
@@ -617,22 +622,93 @@
         loop(PIECE, setup, 8)
         return 0
 
-    lax.fori_loop(0, (live + GROUP - 1) // GROUP, one_group, 0)
-
-
-def enrich(fr, info, off, p0, p1, k0, f0, k1, f1, wt, scales, weights, *rest):
+    lax.fori_loop(part[0], jnp.minimum((live + GROUP - 1) // GROUP, part[1]), one_group, 0)
+
+
+def residuals(fr, info, cf, kf, ff, rf, first, count, unroll):
+    sub, lane = iotas()
+    yf, tiles = fr.yf, fr.tiles
+
+    def next_z(a, b):
+        return pltpu.roll(jnp.where(lane == 0, b, a), LANES - 1, 1)
+
+    def last_z(a, b):
+        return pltpu.roll(jnp.where(lane == LANES - 1, b, a), 1, 1)
+
+    def at_edge(axis, count, first, last, position):
+        low = (position == first) & (info[1 + axis] == 0)
+        high = (position == last) & (info[1 + axis] == count - 1)
+        return jnp.where(low, 1.0, 0.0) + jnp.where(high, 1.0, 0.0)
+
+    out_y = [at_edge(1, fr.counts[1], TOP, TOP + fr.by - 1, sub + t * SUB) for t in range(tiles)]
+    out_z = at_edge(2, fr.counts[2], 0, LANES - 1, lane)
+
+    def flux_x(x):
+        fluxes = []
+        for t in range(tiles):
+            at, to = pl.ds(x * yf + t * SUB, SUB), pl.ds((x + 1) * yf + t * SUB, SUB)
+            fluxes += [(k[at, :] + k[to, :]) * (c[at, :] - c[to, :]) for c, k in zip(cf, kf)]
+        return fluxes
+
+    def residual(x, before):
+        r = x * yf
+        after = flux_x(x)
+        out_x = at_edge(0, fr.counts[0], H, H + fr.bx - 1, x)
+        last_y = [jnp.zeros((SUB, LANES), F32)] * 2
+        for t in range(tiles):
+            at, to = pl.ds(r + t * SUB, SUB), pl.ds(r + t * SUB + 1, SUB)
+            cs, ks = (cf[0][at, :], cf[1][at, :]), (kf[0][at, :], kf[1][at, :])
+            fz = []
+            for i in range(2):
+                cn, kn = next_z(cs[i], cs[1 - i]), next_z(ks[i], ks[1 - i])
+                fz.append((ks[i] + kn) * (cs[i] - cn))
+            for i, (c, k, f, out) in enumerate(zip(cf, kf, ff, rf)):
+                fy = pltpu.roll((ks[i] + k[to, :]) * (cs[i] - c[to, :]), 1, 0)
+                fy_next = (ks[i] + k[to, :]) * (cs[i] - c[to, :])
+                fy_last = jnp.where(sub == 0, last_y[i], fy)
+                last_y[i] = fy
+                outside = out_x + out_y[t] + (out_z if i == 0 else 0.0)
+                total = (after[2 * t + i] - before[2 * t + i]) + (fy_next - fy_last)
+                total = total + (fz[i] - last_z(fz[i], fz[1 - i])) + outside * (ks[i] * cs[i])
+                out[at, :] = jnp.where(ks[i] > 0, f[at, :] - 0.5 * total, 0.0)
+        return tuple(after)
+
+    def some(i, before):
+        for j in range(unroll):
+            before = residual(first + i * unroll + j, before)
+        return before
+
+    lax.fori_loop(0, count // unroll, some, tuple(flux_x(first - 1)))
+
+
+def masked(fr, cf, kf, first, count):
+    def plane(x):
+        for t in range(fr.tiles):
+            at = pl.ds((first + x) * fr.yf + t * SUB, SUB)
+            for c, k in zip(cf, kf):
+                c[at, :] = jnp.where(k[at, :] > 0, c[at, :], 0.0)
+
+    loop(count, plane, 3)
+
+
+def middle(fr, info, p0_in, p1_in, k0, f0, k1, f1, p0, p1, r0, r1):
+    del p0_in, p1_in
+    masked(fr, (p0, p1), (k0, k1), WIDE, fr.xf - 2 * WIDE)
+    residuals(fr, info, (p0, p1), (k0, k1), (f0, f1), (r0, r1), WIDE + 2, fr.xf - 2 * WIDE - 4, 4)
+
+
+def enrich(fr, info, off, p0, p1, r0_in, r1_in, k0, f0, k1, f1, wt, scales, weights, *rest):
     n0 = fr.sides[0]
     x_in, rest = rest[:n0], rest[n0:]
-    core, solved, y_edge, x_edge, slab = rest[:5]
-    c0, c1, r0, r1, q0, q1, rb, base, va, vb, here = rest[5:]
+    c0, c1, r0, r1, core, solved, y_edge, x_edge, slab = rest[:9]
+    q0, q1, rb, base, va, vb, here = rest[9:]
+    del p0, p1, r0_in, r1_in
     sub, lane = iotas()
     yf, tiles = fr.yf, fr.tiles
     live = info[0]
     main_rows = WIDE * yf
     edge = (lane >= LANES - SUB) | (lane < SUB)
 
-    c0[...] = p0[...]
-    c1[...] = p1[...]
     for i, buf in enumerate(x_in):
         row = pl.multiple_of(pick(is_lower(info, 0, i), fr.xf - WIDE, 0) * yf, SUB)
         a = pl.ds(row, main_rows)
@@ -645,64 +721,10 @@
             for a, v in zip(places, [c1[a, :] + v for a, v in zip(places, values)]):
                 c1[a, :] = v
 
-    def mask(b):
-        for j in range(GROUP):
-            at = pl.ds((b * GROUP + j) * SUB, SUB)
-            c0[at, :] = jnp.where(k0[at, :] > 0, c0[at, :], 0.0)
-            c1[at, :] = jnp.where(k1[at, :] > 0, c1[at, :], 0.0)
-
-    loop(fr.blocks, mask, 4)
-
-    def next_z(a, b):
-        return pltpu.roll(jnp.where(lane == 0, b, a), LANES - 1, 1)
-
-    def last_z(a, b):
-        return pltpu.roll(jnp.where(lane == LANES - 1, b, a), 1, 1)
-
-    def at_edge(axis, count, first, last, position):
-        low = (position == first) & (info[1 + axis] == 0)
-        high = (position == last) & (info[1 + axis] == count - 1)
-        return jnp.where(low, 1.0, 0.0) + jnp.where(high, 1.0, 0.0)
-
-    out_y = [at_edge(1, fr.counts[1], TOP, TOP + fr.by - 1, sub + t * SUB) for t in range(tiles)]
-    out_z = at_edge(2, fr.counts[2], 0, LANES - 1, lane)
-
-    def flux_x(x):
-        fluxes = []
-        for t in range(tiles):
-            at, to = pl.ds(x * yf + t * SUB, SUB), pl.ds((x + 1) * yf + t * SUB, SUB)
-            fluxes += [(k[at, :] + k[to, :]) * (c[at, :] - c[to, :]) for c, k in ((c0, k0), (c1, k1))]
-        return fluxes
-
-    def residual(x, before):
-        r = x * yf
-        after = flux_x(x)
-        out_x = at_edge(0, fr.counts[0], H, H + fr.bx - 1, x)
-        last_y = [jnp.zeros((SUB, LANES), F32)] * 2
-        for t in range(tiles):
-            at, to = pl.ds(r + t * SUB, SUB), pl.ds(r + t * SUB + 1, SUB)
-            cs, ks = (c0[at, :], c1[at, :]), (k0[at, :], k1[at, :])
-            fz = []
-            for i in range(2):
-                cn, kn = next_z(cs[i], cs[1 - i]), next_z(ks[i], ks[1 - i])
-                fz.append((ks[i] + kn) * (cs[i] - cn))
-            for i, (c, k, f, out) in enumerate(((c0, k0, f0, r0), (c1, k1, f1, r1))):
-                fy = pltpu.roll((ks[i] + k[to, :]) * (cs[i] - c[to, :]), 1, 0)
-                fy_next = (ks[i] + k[to, :]) * (cs[i] - c[to, :])
-                fy_last = jnp.where(sub == 0, last_y[i], fy)
-                last_y[i] = fy
-                outside = out_x + out_y[t] + (out_z if i == 0 else 0.0)
-                total = (after[2 * t + i] - before[2 * t + i]) + (fy_next - fy_last)
-                total = total + (fz[i] - last_z(fz[i], fz[1 - i])) + outside * (ks[i] * cs[i])
-                out[at, :] = jnp.where(ks[i] > 0, f[at, :] - 0.5 * total, 0.0)
-        return tuple(after)
-
-    def residuals(i, before):
-        for j in range(4):
-            before = residual(4 * i + j + 1, before)
-        return before
-
-    lax.fori_loop(0, fr.live_x // 4, residuals, tuple(flux_x(0)))
+    for first in (0, fr.xf - WIDE):
+        masked(fr, (c0, c1), (k0, k1), first, WIDE)
+    for first in (1, fr.xf - 1 - WIDE - 1):
+        residuals(fr, info, (c0, c1), (k0, k1), (f0, f1), (r0, r1), first, WIDE + 1, 5)
 
     zero(q0)
     zero(q1)
@@ -890,8 +912,8 @@
 
 
 def finish(fr, info, core, *rest):
-    n0, n1, n2 = fr.sides
-    z_in, y_in, x_in, out = rest[:n2], rest[n2 : n1 + n2], rest[n1 + n2 : -1], rest[-1]
+    n1, n2 = fr.sides[1:]
+    z_in, y_in, (out, edges, buf, sem) = rest[:n2], rest[n2 : n1 + n2], rest[n1 + n2 :]
     _, lane = iotas()
     by = fr.by
 
@@ -902,16 +924,38 @@
                 m = i * fr.tiles + t + 1
                 at = pl.ds(row + t * SUB, SUB)
                 pack = (b + MARGIN // 4) * (4 * fr.tiles // GROUP) + m // GROUP
-                out[at, :] = core[at, :] + z_part(info, n2, z_in, pack, m % GROUP, lane)
-            for k, buf in enumerate(y_in):
+                buf[at, :] = core[at, :] + z_part(info, n2, z_in, pack, m % GROUP, lane)
+            for k, part in enumerate(y_in):
                 a = pl.ds(row + pick(is_lower(info, 1, k), by - MARGIN, 0), MARGIN)
-                out[a, :] = out[a, :] + buf[pl.ds((4 * b + i + MARGIN) * MARGIN, MARGIN), :]
+                buf[a, :] = buf[a, :] + part[pl.ds((4 * b + i + MARGIN) * MARGIN, MARGIN), :]
 
     loop(fr.bx // 4, planes, 4)
     count = MARGIN * by
-    for i, buf in enumerate(x_in):
-        a = pl.ds(pl.multiple_of(pick(is_lower(info, 0, i), (fr.bx - MARGIN) * by, 0), SUB), count)
-        out[a, :] = out[a, :] + buf[...]
+    inner = pl.ds(count, fr.bx * by - 2 * count)
+    copy = pltpu.make_async_copy(buf.at[inner], out.at[inner], sem)
+    copy.start()
+    edges[0:count, :] = buf[0:count, :]
+    edges[count : 2 * count, :] = buf[fr.bx * by - count : fr.bx * by, :]
+    copy.wait()
+
+
+def finish_x(fr, info, out_in, edges, *rest):
+    x_in, (out, buf, sem) = rest[:-3], rest[-3:]
+    del out_in
+    count = MARGIN * fr.by
+    buf[...] = edges[...]
+    for i, part in enumerate(x_in):
+        a = pl.ds(pl.multiple_of(pick(is_lower(info, 0, i), count, 0), SUB), count)
+        buf[a, :] = buf[a, :] + part[...]
+    places = (0, fr.bx * fr.by - count)
+    copies = [
+        pltpu.make_async_copy(buf.at[pl.ds(i * count, count)], out.at[pl.ds(row, count)], sem.at[i])
+        for i, row in enumerate(places)
+    ]
+    for copy in copies:
+        copy.start()
+    for copy in copies:
+        copy.wait()
 
 
 def local(
@@ -974,27 +1018,30 @@
         [SMEM],
     )
     x_static = swap("gx", slabs)
-    each *= 1 + n0
-    k0, f0, w0, coefs, *slabs = call(
+    bases = call(fetch, jax.ShapeDtypeStruct(bases.shape, F32), [info, bases], [SMEM, HBM], [pltpu.SemaphoreType.DMA((slots,))], limit=8)
+    x_static, bases = lax.optimization_barrier((x_static, bases))
+    coefs = call(part(stack, fr), rows_of(each * (1 + n0)), [coefs, *x_static])
+    y_coefs = swap("gy", [coefs] * n1)
+    kap, coefs = lax.optimization_barrier((kap, coefs))
+    k0, f0, w0, *slabs = call(
         part(static_y, fr),
-        [fr.frame] * 3 + [rows_of(each)] + [rows_of(fr.y_rows + n2 * fr.y_pack + each)] * n1,
-        [info, kap, frc, wgt, coefs, *z_static, *x_static],
+        [fr.frame] * 3 + [rows_of(fr.y_rows + n2 * fr.y_pack)] * n1,
+        [info, kap, frc, wgt, *z_static, *x_static],
         [SMEM],
         [pltpu.VMEM((fr.y_pack * GROUP, LANES), F32)],
     )
+    slabs, y_coefs = lax.optimization_barrier((slabs, y_coefs))
     y_static = swap("gy", slabs)
 
     together = 4 if slots % 4 == 0 else 1
     p0, p1, *slabs = call(
         part(prolong, fr, (nb, together)),
         [fr.frame] * 2 + [rows_of(live_rows)] * n2,
-        [info, off, bases, coefs, *y_static],
-        [SMEM] * 2 + [HBM],
+        [info, off, bases, coefs, *y_coefs],
+        [SMEM] * 2,
         [
             pltpu.VMEM((27, SUB, LANES), F32),
             pltpu.VMEM((together * CHUNKS // SUB, SUB, LANES), F32),
-            pltpu.VMEM((slots, nb, cells), F32),
-            pltpu.SemaphoreType.DMA((slots,)),
         ],
         limit=16,
     )
@@ -1017,19 +1064,16 @@
     )
     received = swap("gy", slabs)
     groups = slots // GROUP
-    wt, scales, weights = call(
-        part(couple, fr),
-        [
-            jax.ShapeDtypeStruct((groups, 6, PROWS, LANES), F32),
-            jax.ShapeDtypeStruct((groups, PROWS, LANES), F32),
-            jax.ShapeDtypeStruct((groups, PROWS, LANES), F32),
-        ],
-        [info, off, k0, k1, w0, w1],
-        [SMEM] * 2,
-        [pltpu.VMEM((PROWS + 2 * PIECE, LANES), F32)],
-        limit=16,
-    )
-    received, wt = lax.optimization_barrier((received, wt))
+    split = (groups + 1) // 2
+    setup = [
+        jax.ShapeDtypeStruct((groups, 6, PROWS, LANES), F32),
+        jax.ShapeDtypeStruct((groups, PROWS, LANES), F32),
+        jax.ShapeDtypeStruct((groups, PROWS, LANES), F32),
+    ]
+    fields = [info, off, k0, k1, w0, w1]
+    buffer = [pltpu.VMEM((PROWS + 2 * PIECE, LANES), F32)]
+    setup = call(part(couple, fr, (0, split)), setup, fields, [SMEM] * 2, buffer, limit=16)
+    received, setup = lax.optimization_barrier((received, setup))
     p0, p1, *slabs = call(
         part(coarse_x, fr),
         [fr.frame] * 2 + [rows_of(WIDE * fr.yf + -(-WIDE * fr.tiles // GROUP) * SUB)] * n0,
@@ -1039,20 +1083,36 @@
     )
     received = swap("gx", slabs)
 
+    kinds = [jax.ShapeDtypeStruct(a.shape, F32) for a in setup]
+    setup = call(
+        part(couple, fr, (split, groups)),
+        kinds,
+        [*fields, *setup],
+        [SMEM] * 2,
+        buffer,
+        alias={6: 0, 7: 1, 8: 2},
+        limit=16,
+    )
+    p0, p1, r0, r1 = call(
+        part(middle, fr), [fr.frame] * 4, [info, p0, p1, k0, f0, k1, f1], [SMEM], alias={1: 0, 2: 1}, limit=16
+    )
+
     solve = pltpu.VMEM((2, PROWS, LANES), F32)
     padded = pltpu.VMEM((2, PROWS + 2 * PIECE, LANES), F32)
-    core, solved, y_edge, x_edge, slab = call(
+    _, _, _, _, core, solved, y_edge, x_edge, slab = call(
         part(enrich, fr),
-        [
+        [fr.frame] * 4
+        + [
             rows_of(bx * by),
             jax.ShapeDtypeStruct((groups, 2, PROWS, LANES), F32),
             rows_of(fr.live_x * 2 * SUB),
             rows_of(2 * MARGIN * by),
             rows_of(live_rows),
         ],
-        [info, off, p0, p1, k0, f0, k1, f1, wt, scales, weights, *received],
+        [info, off, p0, p1, r0, r1, k0, f0, k1, f1, *setup, *received],
         [SMEM] * 2,
-        [pltpu.VMEM((fr.rows, LANES), F32)] * 6 + [pltpu.VMEM((PROWS, LANES), F32), solve, padded, padded, pltpu.VMEM((6, PROWS, LANES), F32)],
+        [pltpu.VMEM((fr.rows, LANES), F32)] * 2 + [pltpu.VMEM((PROWS, LANES), F32), solve, padded, padded, pltpu.VMEM((6, PROWS, LANES), F32)],
+        alias={2: 0, 3: 1, 4: 2, 5: 3},
         limit=32,
     )
 
@@ -1082,7 +1142,24 @@
         [pltpu.VMEM((2 * MARGIN * by, LANES), F32)],
     )
     x_in = swap("gx", slabs)
-    update = call(part(finish, fr), rows_of(bx * by), [info, core, *z_in, *y_in, *x_in], [SMEM])
+    edge = rows_of(2 * MARGIN * by)
+    update, edges = call(
+        part(finish, fr),
+        [rows_of(bx * by), edge],
+        [info, core, *z_in, *y_in],
+        [SMEM],
+        [pltpu.VMEM((bx * by, LANES), F32), pltpu.SemaphoreType.DMA],
+        out_spec=[ANY, VMEM],
+    )
+    update = call(
+        part(finish_x, fr),
+        rows_of(bx * by),
+        [info, update, edges, *x_in],
+        [SMEM, ANY],
+        [pltpu.VMEM(edge.shape, F32), pltpu.SemaphoreType.DMA((2,))],
+        alias={1: 0},
+        out_spec=ANY,
+    )
     new_basis = basis.reshape(slots, CHUNKS, 2, LANES).swapaxes(1, 2)
     return update.reshape(bx, by, bz), new_basis.reshape(1, 1, 1, slots, 2, cells)
 

time: 107 us -> 100 us (0.935)
  the two profiles are of different devices: /device:TPU:10 before, /device:TPU:9 now
where the time goes in v3:
time: 100 us; the launch traced here: 98.2 us
  starting transfers between devices  46.2 us (46%)
  Pallas kernels  36.5 us (36%)
  waiting for transfers between devices  13.9 us (14%)
  between operations  1.53 us (2%)
    ppermute x17, starting transfers between devices, swap(): lax.ppermute(slab, axis, pairs + [(j, i) for i, j in pairs])  46.2 us
    pallas_call x18, Pallas kernels, call(): pl.pallas_call(kernel, out_shape=outs, in_specs=specs, out_specs=out_spec...  36.5 us
    ppermute x17, waiting for transfers between devices, swap(): lax.ppermute(slab, axis, pairs + [(j, i) for i, j in pairs])  13.9 us
  transfers between devices with their start and end apart: 17, of which 10 were waited for; matrix products, arithmetic and copies ran while one was open for 0% of the time, Pallas kernels for 18%

profile of v3, /device:TPU:9, one launch (start us, length us, event | category | flops | bytes accessed | tf_op | source)
XLA Modules:
  0.0 98.2 jit_solution(3946194282789891657)
XLA Ops:
  1.3 0.1 pad_add_fusion.info
  1.4 3.1 %shard_map.113 = (f32[1024,128]{1,0:T(8,128)S(1)}, f32[1024,128]{1,0:T(8,128)S(1)}, f32[1024,128]{1,0:T(8,128)S(1)}, f32[8,128]{1,0:T(8,128)S(1)}, s32[8,128]{1,0:T(8,128)S(1)}, /*index=5*/f32[136,128]{1,0:T(8,128)S(1)}) custom-call(s32[4]{0:T(128)S(1)} %pad_add_fusion.info, f32[4]{0:T(128)} %contrast.1, f32[4]{0:T(128)} %channel.1, f32[1024,128]{1,0:T(8,128)} %bitcast.27, ...), custom_call_target="tpu_custom_call" | custom-call | tf_op jit(solution)/shard_map/pallas_call | solution.py:125
  4.4 1.3 %collective-permute-start = (f32[136,128]{1,0:T(8,128)S(1)}, f32[136,128]{1,0:T(8,128)S(1)}, u32[]{:S(2)}, u32[]{:S(2)}) collective-permute-start(f32[136,128]{1,0:T(8,128)S(1)} %get-tuple-element.77), channel_id=1, source_target_pairs={{0,1},{1,0},{2,3},{3,2},{4,5},{5,4},{6,7},{7,6},{8,9},{9,8},{10,11... | collective-permute-start | bytes 208904 | tf_op jit(solution)/shard_map/ppermute | solution.py:145
  5.7 1.9 %collective-permute-done.rest_0_ = f32[136,128]{1,0:T(8,128)S(1)} collective-permute-done((f32[136,128]{1,0:T(8,128)S(1)}, f32[136,128]{1,0:T(8,128)S(1)}, u32[]{:S(2)}, u32[]{:S(2)}) %collective-permute-start) | collective-permute-done | bytes 69664 | tf_op jit(solution)/shard_map/ppermute | solution.py:145
  7.7 0.6 shard_map.114
  8.2 0.1 collective-permute-start.1
  8.3 4.5 %collective-permute-start.2 = (f32[456,128]{1,0:T(8,128)S(1)}, f32[456,128]{1,0:T(8,128)S(1)}, u32[]{:S(2)}, u32[]{:S(2)}) collective-permute-start(f32[456,128]{1,0:T(8,128)S(1)} %get-tuple-element.79), channel_id=1, source_target_pairs={{8,16},{16,8},{9,17},{17,9},{10,18},{18,10},{11,19},{19,11},{12,20... | collective-permute-start | bytes 700424 | tf_op jit(solution)/shard_map/ppermute | solution.py:145
  12.8 2.1 %shard_map.115.bases = f32[40,8,4096]{2,1,0:T(8,128)S(1)} custom-call(s32[4]{0:T(128)S(1)} %pad_add_fusion.info, f32[40,8,4096]{2,1,0:T(8,128)} %bitcast.24), custom_call_target="tpu_custom_call" | custom-call | tf_op jit(solution)/shard_map/pallas_call | solution.py:125
  14.9 0.0 collective-permute-done.1.rest_0_.rest_1_
  14.9 1.8 %collective-permute-done.2.rest_1_.rest_2_ = f32[456,128]{1,0:T(8,128)S(1)} collective-permute-done((f32[456,128]{1,0:T(8,128)S(1)}, f32[456,128]{1,0:T(8,128)S(1)}, u32[]{:S(2)}, u32[]{:S(2)}) %collective-permute-start.2) | collective-permute-done | bytes 233504 | tf_op jit(solution)/shard_map/ppermute | solution.py:145
  16.7 2.7 %collective-permute-start.3 = (f32[48,128]{1,0:T(8,128)S(1)}, f32[48,128]{1,0:T(8,128)S(1)}, u32[]{:S(2)}, u32[]{:S(2)}) collective-permute-start(f32[48,128]{1,0:T(8,128)S(1)} %shard_map.116.own), channel_id=1, source_target_pairs={{0,2},{4,6},{2,0},{6,4},{1,3},{5,7},{3,1},{7,5},{8,10},{12,14},{10... | collective-permute-start | bytes 73736 | tf_op jit(solution)/shard_map/ppermute | solution.py:145
  19.4 3.0 %collective-permute-start.4 = (f32[48,128]{1,0:T(8,128)S(1)}, f32[48,128]{1,0:T(8,128)S(1)}, u32[]{:S(2)}, u32[]{:S(2)}) collective-permute-start(f32[48,128]{1,0:T(8,128)S(1)} %shard_map.116.own), channel_id=1, source_target_pairs={{2,4},{4,2},{3,5},{5,3},{10,12},{12,10},{11,13},{13,11},{18,20},{2... | collective-permute-start | bytes 73736 | tf_op jit(solution)/shard_map/ppermute | solution.py:145
  22.4 1.4 %shard_map.117 = (f32[2048,128]{1,0:T(8,128)S(1)}, f32[2048,128]{1,0:T(8,128)S(1)}, f32[2048,128]{1,0:T(8,128)S(1)}, f32[600,128]{1,0:T(8,128)S(1)}, f32[600,128]{1,0:T(8,128)S(1)}) custom-call(s32[4]{0:T(128)S(1)} %pad_add_fusion.info, f32[1024,128]{1,0:T(8,128)S(1)} %get-tuple-element.85.kap, f32[1024,128]{1,0:T(8,128)S(1)} %get-tuple-element.74.frc, ...), custom_call_target="tpu_custom_call" | custom-call | tf_op jit(solution)/shard_map/pallas_call | solution.py:125
  23.9 0.7 collective-permute-done.4.rest_1_
  24.6 3.0 %collective-permute-start.7 = (f32[600,128]{1,0:T(8,128)S(1)}, f32[600,128]{1,0:T(8,128)S(1)}, u32[]{:S(2)}, u32[]{:S(2)}) collective-permute-start(f32[600,128]{1,0:T(8,128)S(1)} %get-tuple-element.97), channel_id=1, source_target_pairs={{2,4},{4,2},{3,5},{5,3},{10,12},{12,10},{11,13},{13,11},{18,20},{2... | collective-permute-start | bytes 921608 | tf_op jit(solution)/shard_map/ppermute | solution.py:145
  27.6 2.8 %shard_map.118 = (f32[2048,128]{1,0:T(8,128)S(1)}, f32[2048,128]{1,0:T(8,128)S(1)}, f32[240,128]{1,0:T(8,128)S(1)}) custom-call(s32[4]{0:T(128)S(1)} %pad_add_fusion.info, s32[8,128]{1,0:T(8,128)S(1)} %get-tuple-element.72.off, f32[40,8,4096]{2,1,0:T(8,128)S(1)} %shard_map.115.bases, f32[48,128]{1,0:T(8,128)S(1)} %shard_map.116.own, ...), custom_call_target="tpu_custom_call" | custom-call | tf_op jit(solution)/shard_map/pallas_call | solution.py:125
  30.4 1.9 %collective-permute-start.5 = (f32[240,128]{1,0:T(8,128)S(1)}, f32[240,128]{1,0:T(8,128)S(1)}, u32[]{:S(2)}, u32[]{:S(2)}) collective-permute-start(f32[240,128]{1,0:T(8,128)S(1)} %get-tuple-element.92), channel_id=1, source_target_pairs={{0,1},{1,0},{2,3},{3,2},{4,5},{5,4},{6,7},{7,6},{8,9},{9,8},{10,11... | collective-permute-start | bytes 368648 | tf_op jit(solution)/shard_map/ppermute | solution.py:145
  32.3 0.0 collective-permute-done.6.rest_3_
  32.3 0.5 collective-permute-done.7.rest_4_
  32.7 2.4 %shard_map.119 = (f32[2048,128]{1,0:T(8,128)S(1)}, f32[2048,128]{1,0:T(8,128)S(1)}, f32[2048,128]{1,0:T(8,128)S(1)}, f32[2048,128]{1,0:T(8,128)S(1)}, f32[2048,128]{1,0:T(8,128)S(1)}, /*index=5*/f32[2048,128]{1,0:T(8,128)S(1)}) custom-call(s32[4]{0:T(128)S(1)} %pad_add_fusion.info, ...), custom_call_target="tpu_custom_call", output_to_operand_aliasing={{0}: (1, {}), {1}: (2, {}), {2}: (3, {})} | custom-call | tf_op jit(solution)/shard_map/pallas_call | solution.py:125
  35.2 0.9 collective-permute-done.5.rest_0_
  36.1 1.9 %shard_map.120 = (f32[2048,128]{1,0:T(8,128)S(1)}, f32[2048,128]{1,0:T(8,128)S(1)}, f32[440,128]{1,0:T(8,128)S(1)}, f32[440,128]{1,0:T(8,128)S(1)}) custom-call(s32[4]{0:T(128)S(1)} %pad_add_fusion.info, f32[2048,128]{1,0:T(8,128)S(1)} %get-tuple-element.90.p0_in, ...), custom_call_target="tpu_custom_call", output_to_operand_aliasing={{0}: (1, {}), {1}: (2, {})} | custom-call | tf_op jit(solution)/shard_map/pallas_call | solution.py:125
  37.9 0.6 collective-permute-start.8
  38.5 3.0 %collective-permute-start.9 = (f32[440,128]{1,0:T(8,128)S(1)}, f32[440,128]{1,0:T(8,128)S(1)}, u32[]{:S(2)}, u32[]{:S(2)}) collective-permute-start(f32[440,128]{1,0:T(8,128)S(1)} %get-tuple-element.103), channel_id=1, source_target_pairs={{2,4},{4,2},{3,5},{5,3},{10,12},{12,10},{11,13},{13,11},{18,20},{2... | collective-permute-start | bytes 675848 | tf_op jit(solution)/shard_map/ppermute | solution.py:145
  41.6 1.9 %shard_map.121 = (f32[5,6,256,128]{3,2,1,0:T(8,128)S(1)}, f32[5,256,128]{2,1,0:T(8,128)S(1)}, f32[5,256,128]{2,1,0:T(8,128)S(1)}) custom-call(s32[4]{0:T(128)S(1)} %pad_add_fusion.info, s32[8,128]{1,0:T(8,128)S(1)} %get-tuple-element.72.off, f32[2048,128]{1,0:T(8,128)S(1)} %get-tuple-element.104.k0, f32[2048,128]{1,0:T(8,128)S(1)} %get-tuple-element.105.k1, ...), custom_call_target="tpu_custom_call" | custom-call | tf_op jit(solution)/shard_map/pallas_call | solution.py:125
  43.5 2.3 %collective-permute-done.9.rest_1_ = f32[440,128]{1,0:T(8,128)S(1)} collective-permute-done((f32[440,128]{1,0:T(8,128)S(1)}, f32[440,128]{1,0:T(8,128)S(1)}, u32[]{:S(2)}, u32[]{:S(2)}) %collective-permute-start.9) | collective-permute-done | bytes 225312 | tf_op jit(solution)/shard_map/ppermute | solution.py:145
  45.8 1.2 %shard_map.122 = (f32[2048,128]{1,0:T(8,128)S(1)}, f32[2048,128]{1,0:T(8,128)S(1)}, f32[488,128]{1,0:T(8,128)S(1)}, f32[488,128]{1,0:T(8,128)S(1)}) custom-call(s32[4]{0:T(128)S(1)} %pad_add_fusion.info, f32[2048,128]{1,0:T(8,128)S(1)} %get-tuple-element.100.p0_in, ...), custom_call_target="tpu_custom_call", output_to_operand_aliasing={{0}: (1, {}), {1}: (2, {})} | custom-call | tf_op jit(solution)/shard_map/pallas_call | solution.py:125
  47.0 0.1 collective-permute-start.10
  47.1 2.5 %collective-permute-start.11 = (f32[488,128]{1,0:T(8,128)S(1)}, f32[488,128]{1,0:T(8,128)S(1)}, u32[]{:S(2)}, u32[]{:S(2)}) collective-permute-start(f32[488,128]{1,0:T(8,128)S(1)} %get-tuple-element.128), channel_id=1, source_target_pairs={{8,16},{16,8},{9,17},{17,9},{10,18},{18,10},{11,19},{19,11},{12,20... | collective-permute-start | bytes 749576 | tf_op jit(solution)/shard_map/ppermute | solution.py:145
  49.6 0.6 shard_map.124
  50.2 2.5 %shard_map.123 = (f32[2048,128]{1,0:T(8,128)S(1)}, f32[2048,128]{1,0:T(8,128)S(1)}, f32[2048,128]{1,0:T(8,128)S(1)}, f32[2048,128]{1,0:T(8,128)S(1)}) custom-call(s32[4]{0:T(128)S(1)} %pad_add_fusion.info, f32[2048,128]{1,0:T(8,128)S(1)} %get-tuple-element.113.p0_in, ...), custom_call_target="tpu_custom_call", output_to_operand_aliasing={{0}: (1, {}), {1}: (2, {})} | custom-call | tf_op jit(solution)/shard_map/pallas_call | solution.py:125
  52.7 0.8 collective-permute-done.10.rest_0_
  53.5 1.6 %collective-permute-done.11.rest_1_ = f32[488,128]{1,0:T(8,128)S(1)} collective-permute-done((f32[488,128]{1,0:T(8,128)S(1)}, f32[488,128]{1,0:T(8,128)S(1)}, u32[]{:S(2)}, u32[]{:S(2)}) %collective-permute-start.11) | collective-permute-done | bytes 249888 | tf_op jit(solution)/shard_map/ppermute | solution.py:145
  55.1 9.2 %shard_map.125 = (f32[2048,128]{1,0:T(8,128)S(1)}, f32[2048,128]{1,0:T(8,128)S(1)}, f32[2048,128]{1,0:T(8,128)S(1)}, f32[2048,128]{1,0:T(8,128)S(1)}, f32[1024,1...) custom-call(s32[4]{0:T(128)S(1)} %pad_add_fusion.info, ...), custom_call_target="tpu_custom_call", output_to_operand_aliasing={{0}: (2, {}), {1}: (3, {}), {2}: (4, {}), {3}: (5, {})} | custom-call | tf_op jit(solution)/shard_map/pallas_call | solution.py:125
  64.3 3.6 %collective-permute-start.12 = (f32[240,128]{1,0:T(8,128)S(1)}, f32[240,128]{1,0:T(8,128)S(1)}, u32[]{:S(2)}, u32[]{:S(2)}) collective-permute-start(f32[240,128]{1,0:T(8,128)S(1)} %get-tuple-element.130), channel_id=1, source_target_pairs={{0,1},{1,0},{2,3},{3,2},{4,5},{5,4},{6,7},{7,6},{8,9},{9,8},{10,11... | collective-permute-start | bytes 368648 | tf_op jit(solution)/shard_map/ppermute | solution.py:145
  67.9 2.3 %shard_map.126 = f32[2560,128]{1,0:T(8,128)} custom-call(s32[4]{0:T(128)S(1)} %pad_add_fusion.info, f32[5,2,256,128]{3,2,1,0:T(8,128)S(1)} %get-tuple-element.131.solved), custom_call_target="tpu_custom_call" | custom-call | tf_op jit(solution)/shard_map/pallas_call | solution.py:125
  70.2 0.0 collective-permute-done.12.rest_0_
  70.2 0.8 shard_map.127
  71.0 6.7 %collective-permute-start.13 = (f32[160,128]{1,0:T(8,128)S(1)}, f32[160,128]{1,0:T(8,128)S(1)}, u32[]{:S(2)}, u32[]{:S(2)}) collective-permute-start(f32[160,128]{1,0:T(8,128)S(1)} %get-tuple-element.134), channel_id=1, source_target_pairs={{0,2},{4,6},{2,0},{6,4},{1,3},{5,7},{3,1},{7,5},{8,10},{12,14},{10... | collective-permute-start | bytes 245768 | tf_op jit(solution)/shard_map/ppermute | solution.py:145
  77.7 4.1 %collective-permute-start.14 = (f32[160,128]{1,0:T(8,128)S(1)}, f32[160,128]{1,0:T(8,128)S(1)}, u32[]{:S(2)}, u32[]{:S(2)}) collective-permute-start(f32[160,128]{1,0:T(8,128)S(1)} %get-tuple-element.135), channel_id=1, source_target_pairs={{2,4},{4,2},{3,5},{5,3},{10,12},{12,10},{11,13},{13,11},{18,20},{2... | collective-permute-start | bytes 245768 | tf_op jit(solution)/shard_map/ppermute | solution.py:145
  81.9 2.1 %collective-permute-done.14.rest_2_ = f32[160,128]{1,0:T(8,128)S(1)} collective-permute-done((f32[160,128]{1,0:T(8,128)S(1)}, f32[160,128]{1,0:T(8,128)S(1)}, u32[]{:S(2)}, u32[]{:S(2)}) %collective-permute-start.14) | collective-permute-done | bytes 81952 | tf_op jit(solution)/shard_map/ppermute | solution.py:145
  84.0 0.7 shard_map.129
  84.6 7.4 %collective-permute-start.15 = (f32[128,128]{1,0:T(8,128)S(1)}, f32[128,128]{1,0:T(8,128)S(1)}, u32[]{:S(2)}, u32[]{:S(2)}) collective-permute-start(f32[128,128]{1,0:T(8,128)S(1)} %get-tuple-element.139), channel_id=1, source_target_pairs={{0,8},{16,24},{8,0},{24,16},{1,9},{17,25},{9,1},{25,17},{2,10},{18... | collective-permute-start | bytes 196616 | tf_op jit(solution)/shard_map/ppermute | solution.py:145
  92.0 1.9 %collective-permute-start.16 = (f32[128,128]{1,0:T(8,128)S(1)}, f32[128,128]{1,0:T(8,128)S(1)}, u32[]{:S(2)}, u32[]{:S(2)}) collective-permute-start(f32[128,128]{1,0:T(8,128)S(1)} %get-tuple-element.140), channel_id=1, source_target_pairs={{8,16},{16,8},{9,17},{17,9},{10,18},{18,10},{11,19},{19,11},{12,20... | collective-permute-start | bytes 196616 | tf_op jit(solution)/shard_map/ppermute | solution.py:145
  93.9 1.8 %shard_map.128 = (f32[1024,128]{1,0:T(8,128)}, f32[256,128]{1,0:T(8,128)S(1)}) custom-call(s32[4]{0:T(128)S(1)} %pad_add_fusion.info, f32[1024,128]{1,0:T(8,128)S(1)} %get-tuple-element.129.core, f32[240,128]{1,0:T(8,128)S(1)} %collective-permute-done.12.rest_0_, f32[160,128]{1,0:T(8,128)S(1)} %collective-permute-done.13.rest_1_, ...), custom_call_target="tpu_custom_call" | custom-call | tf_op jit(solution)/shard_map/pallas_call | solution.py:125
  95.7 0.0 collective-permute-done.15.rest_0_
  95.7 1.3 %collective-permute-done.16.rest_1_ = f32[128,128]{1,0:T(8,128)S(1)} collective-permute-done((f32[128,128]{1,0:T(8,128)S(1)}, f32[128,128]{1,0:T(8,128)S(1)}, u32[]{:S(2)}, u32[]{:S(2)}) %collective-permute-start.16) | collective-permute-done | bytes 65568 | tf_op jit(solution)/shard_map/ppermute | solution.py:145
  97.0 1.2 %shard_map.130 = f32[1024,128]{1,0:T(8,128)} custom-call(s32[4]{0:T(128)S(1)} %pad_add_fusion.info, f32[1024,128]{1,0:T(8,128)} %get-tuple-element.136.out_in, f32[256,128]{1,0:T(8,128)S(1)} %get-tuple-element.137.edges, f32[128,128]{1,0:T(8,128)S(1)} %collective-permute-done.15.rest_0_, ...), custom_call_target="tpu_custom_call", output_to_operand_aliasing={{}: (1, {})} | custom-call | tf_op jit(solution)/shard_map/pallas_call | solution.py:125
  (5 shorter events, 0.0 us)
Async XLA Ops:
  4.4 3.2 %collective-permute-start = (f32[136,128]{1,0:T(8,128)S(1)}, f32[136,128]{1,0:T(8,128)S(1)}, u32[]{:S(2)}, u32[]{:S(2)}) collective-permute-start(f32[136,128]{1,0:T(8,128)S(1)} %get-tuple-element.77), channel_id=1, source_target_pairs={{0,1},{1,0},{2,3},{3,2},{4,5},{5,4},{6,7},{7,6},{8,9},{9,8},{10,11... | collective-permute-start | bytes 208904 | tf_op jit(solution)/shard_map/ppermute | solution.py:145
  8.2 6.7 %collective-permute-start.1 = (f32[456,128]{1,0:T(8,128)S(1)}, f32[456,128]{1,0:T(8,128)S(1)}, u32[]{:S(2)}, u32[]{:S(2)}) collective-permute-start(f32[456,128]{1,0:T(8,128)S(1)} %get-tuple-element.78), channel_id=1, source_target_pairs={{0,8},{16,24},{8,0},{24,16},{1,9},{17,25},{9,1},{25,17},{2,10},{18... | collective-permute-start | bytes 700424 | tf_op jit(solution)/shard_map/ppermute | solution.py:145
  8.3 8.4 %collective-permute-start.2 = (f32[456,128]{1,0:T(8,128)S(1)}, f32[456,128]{1,0:T(8,128)S(1)}, u32[]{:S(2)}, u32[]{:S(2)}) collective-permute-start(f32[456,128]{1,0:T(8,128)S(1)} %get-tuple-element.79), channel_id=1, source_target_pairs={{8,16},{16,8},{9,17},{17,9},{10,18},{18,10},{11,19},{19,11},{12,20... | collective-permute-start | bytes 700424 | tf_op jit(solution)/shard_map/ppermute | solution.py:145
  16.7 7.2 %collective-permute-start.3 = (f32[48,128]{1,0:T(8,128)S(1)}, f32[48,128]{1,0:T(8,128)S(1)}, u32[]{:S(2)}, u32[]{:S(2)}) collective-permute-start(f32[48,128]{1,0:T(8,128)S(1)} %shard_map.116.own), channel_id=1, source_target_pairs={{0,2},{4,6},{2,0},{6,4},{1,3},{5,7},{3,1},{7,5},{8,10},{12,14},{10... | collective-permute-start | bytes 73736 | tf_op jit(solution)/shard_map/ppermute | solution.py:145
  19.4 5.1 %collective-permute-start.4 = (f32[48,128]{1,0:T(8,128)S(1)}, f32[48,128]{1,0:T(8,128)S(1)}, u32[]{:S(2)}, u32[]{:S(2)}) collective-permute-start(f32[48,128]{1,0:T(8,128)S(1)} %shard_map.116.own), channel_id=1, source_target_pairs={{2,4},{4,2},{3,5},{5,3},{10,12},{12,10},{11,13},{13,11},{18,20},{2... | collective-permute-start | bytes 73736 | tf_op jit(solution)/shard_map/ppermute | solution.py:145
  24.6 7.7 %collective-permute-start.6 = (f32[600,128]{1,0:T(8,128)S(1)}, f32[600,128]{1,0:T(8,128)S(1)}, u32[]{:S(2)}, u32[]{:S(2)}) collective-permute-start(f32[600,128]{1,0:T(8,128)S(1)} %get-tuple-element.96), channel_id=1, source_target_pairs={{0,2},{4,6},{2,0},{6,4},{1,3},{5,7},{3,1},{7,5},{8,10},{12,14},{10... | collective-permute-start | bytes 921608 | tf_op jit(solution)/shard_map/ppermute | solution.py:145
  24.6 8.2 %collective-permute-start.7 = (f32[600,128]{1,0:T(8,128)S(1)}, f32[600,128]{1,0:T(8,128)S(1)}, u32[]{:S(2)}, u32[]{:S(2)}) collective-permute-start(f32[600,128]{1,0:T(8,128)S(1)} %get-tuple-element.97), channel_id=1, source_target_pairs={{2,4},{4,2},{3,5},{5,3},{10,12},{12,10},{11,13},{13,11},{18,20},{2... | collective-permute-start | bytes 921608 | tf_op jit(solution)/shard_map/ppermute | solution.py:145
  30.4 5.7 %collective-permute-start.5 = (f32[240,128]{1,0:T(8,128)S(1)}, f32[240,128]{1,0:T(8,128)S(1)}, u32[]{:S(2)}, u32[]{:S(2)}) collective-permute-start(f32[240,128]{1,0:T(8,128)S(1)} %get-tuple-element.92), channel_id=1, source_target_pairs={{0,1},{1,0},{2,3},{3,2},{4,5},{5,4},{6,7},{7,6},{8,9},{9,8},{10,11... | collective-permute-start | bytes 368648 | tf_op jit(solution)/shard_map/ppermute | solution.py:145
  37.9 5.5 %collective-permute-start.8 = (f32[440,128]{1,0:T(8,128)S(1)}, f32[440,128]{1,0:T(8,128)S(1)}, u32[]{:S(2)}, u32[]{:S(2)}) collective-permute-start(f32[440,128]{1,0:T(8,128)S(1)} %get-tuple-element.102), channel_id=1, source_target_pairs={{0,2},{4,6},{2,0},{6,4},{1,3},{5,7},{3,1},{7,5},{8,10},{12,14},{10... | collective-permute-start | bytes 675848 | tf_op jit(solution)/shard_map/ppermute | solution.py:145
  38.5 7.3 %collective-permute-start.9 = (f32[440,128]{1,0:T(8,128)S(1)}, f32[440,128]{1,0:T(8,128)S(1)}, u32[]{:S(2)}, u32[]{:S(2)}) collective-permute-start(f32[440,128]{1,0:T(8,128)S(1)} %get-tuple-element.103), channel_id=1, source_target_pairs={{2,4},{4,2},{3,5},{5,3},{10,12},{12,10},{11,13},{13,11},{18,20},{2... | collective-permute-start | bytes 675848 | tf_op jit(solution)/shard_map/ppermute | solution.py:145
  47.0 6.5 %collective-permute-start.10 = (f32[488,128]{1,0:T(8,128)S(1)}, f32[488,128]{1,0:T(8,128)S(1)}, u32[]{:S(2)}, u32[]{:S(2)}) collective-permute-start(f32[488,128]{1,0:T(8,128)S(1)} %get-tuple-element.127), channel_id=1, source_target_pairs={{0,8},{16,24},{8,0},{24,16},{1,9},{17,25},{9,1},{25,17},{2,10},{18... | collective-permute-start | bytes 749576 | tf_op jit(solution)/shard_map/ppermute | solution.py:145
  47.1 8.0 %collective-permute-start.11 = (f32[488,128]{1,0:T(8,128)S(1)}, f32[488,128]{1,0:T(8,128)S(1)}, u32[]{:S(2)}, u32[]{:S(2)}) collective-permute-start(f32[488,128]{1,0:T(8,128)S(1)} %get-tuple-element.128), channel_id=1, source_target_pairs={{8,16},{16,8},{9,17},{17,9},{10,18},{18,10},{11,19},{19,11},{12,20... | collective-permute-start | bytes 749576 | tf_op jit(solution)/shard_map/ppermute | solution.py:145
  64.3 5.9 %collective-permute-start.12 = (f32[240,128]{1,0:T(8,128)S(1)}, f32[240,128]{1,0:T(8,128)S(1)}, u32[]{:S(2)}, u32[]{:S(2)}) collective-permute-start(f32[240,128]{1,0:T(8,128)S(1)} %get-tuple-element.130), channel_id=1, source_target_pairs={{0,1},{1,0},{2,3},{3,2},{4,5},{5,4},{6,7},{7,6},{8,9},{9,8},{10,11... | collective-permute-start | bytes 368648 | tf_op jit(solution)/shard_map/ppermute | solution.py:145
  71.0 10.8 %collective-permute-start.13 = (f32[160,128]{1,0:T(8,128)S(1)}, f32[160,128]{1,0:T(8,128)S(1)}, u32[]{:S(2)}, u32[]{:S(2)}) collective-permute-start(f32[160,128]{1,0:T(8,128)S(1)} %get-tuple-element.134), channel_id=1, source_target_pairs={{0,2},{4,6},{2,0},{6,4},{1,3},{5,7},{3,1},{7,5},{8,10},{12,14},{10... | collective-permute-start | bytes 245768 | tf_op jit(solution)/shard_map/ppermute | solution.py:145
  77.7 6.3 %collective-permute-start.14 = (f32[160,128]{1,0:T(8,128)S(1)}, f32[160,128]{1,0:T(8,128)S(1)}, u32[]{:S(2)}, u32[]{:S(2)}) collective-permute-start(f32[160,128]{1,0:T(8,128)S(1)} %get-tuple-element.135), channel_id=1, source_target_pairs={{2,4},{4,2},{3,5},{5,3},{10,12},{12,10},{11,13},{13,11},{18,20},{2... | collective-permute-start | bytes 245768 | tf_op jit(solution)/shard_map/ppermute | solution.py:145
  84.6 11.1 %collective-permute-start.15 = (f32[128,128]{1,0:T(8,128)S(1)}, f32[128,128]{1,0:T(8,128)S(1)}, u32[]{:S(2)}, u32[]{:S(2)}) collective-permute-start(f32[128,128]{1,0:T(8,128)S(1)} %get-tuple-element.139), channel_id=1, source_target_pairs={{0,8},{16,24},{8,0},{24,16},{1,9},{17,25},{9,1},{25,17},{2,10},{18... | collective-permute-start | bytes 196616 | tf_op jit(solution)/shard_map/ppermute | solution.py:145
  92.0 5.0 %collective-permute-start.16 = (f32[128,128]{1,0:T(8,128)S(1)}, f32[128,128]{1,0:T(8,128)S(1)}, u32[]{:S(2)}, u32[]{:S(2)}) collective-permute-start(f32[128,128]{1,0:T(8,128)S(1)} %get-tuple-element.140), channel_id=1, source_target_pairs={{8,16},{16,8},{9,17},{17,9},{10,18},{18,10},{11,19},{19,11},{12,20... | collective-permute-start | bytes 196616 | tf_op jit(solution)/shard_map/ppermute | solution.py:145

commit v4 on v3

--- a/solution.py
+++ b/solution.py
@@ -164,22 +164,19 @@
     (kap, frc, wgt, own, table), slabs = rest[:5], rest[5 : 5 + n]
     k_buf, l_buf, c_buf, o_buf, i_buf, t_buf, sem = rest[5 + n :]
     _, lane = iotas()
-    moves = (
-        (contrast, t_buf.at[0]),
-        (channel, t_buf.at[1]),
-        (labels, l_buf),
-        (kappa, k_buf),
-        (forcing, frc),
-        (coef, c_buf),
-        (offsets, o_buf),
-        (links, i_buf),
-    )
+    half = fr.bx * fr.by // 2
+    halves = [pl.ds(i * half, half) for i in range(2)]
+    pairs = ((labels, l_buf), (kappa, k_buf), (forcing, frc))
+    moves = [(contrast, t_buf.at[0]), (channel, t_buf.at[1])]
+    for rows in halves:
+        moves += [(src.at[rows], dst.at[rows]) for src, dst in pairs]
+    moves += [(coef, c_buf), (offsets, o_buf), (links, i_buf)]
     copies = [pltpu.make_async_copy(src, dst, sem.at[i]) for i, (src, dst) in enumerate(moves)]
     for copy in copies:
         copy.start()
     zero(own)
     zero(table)
-    for copy in copies:
+    for copy in copies[8:]:
         copy.wait()
     own[0 : coef.shape[0], 0 : coef.shape[1]] = c_buf[...]
     for i in range(3):
@@ -204,7 +201,12 @@
             slab[pl.ds(b * SUB, SUB), :] = mix
 
     count = fr.bx * fr.by // (GROUP * SUB)
-    loop(count, block, 4)
+    for copy in copies[:5]:
+        copy.wait()
+    loop(count // 2, block, 8)
+    for copy in copies[5:8]:
+        copy.wait()
+    loop(count // 2, lambda b: block(b + count // 2), 8)
     for slab in slabs:
         slab[count * SUB : (count + 1) * SUB, :] = own[...]
 
@@ -472,7 +474,7 @@
             near = [jnp.where(main, x, y) for x, y in tiles]
             slab[pl.ds(b * SUB, SUB), :] = pack_tiles(near, SUB, lane)
 
-    loop(fr.live_blocks, block, 3)
+    loop(fr.live_blocks, block, 10)
 
 
 def coarse_y(fr, info, p0_in, p1_in, *rest):
@@ -496,7 +498,7 @@
                 p0[a, :] = v0
                 p1[a, :] = v1
 
-    loop(fr.live_blocks, block, 3)
+    loop(fr.live_blocks, block, 10)
 
     def plane(x):
         r = (x + 1) * fr.yf
@@ -593,7 +595,7 @@
                 r = x * PIECE + h * SUB
                 kb[pl.ds(PIECE + r, SUB), :], weights[group, pl.ds(r, SUB), :] = tiles_at(x, h)
 
-        loop(PIECE, gather, 4)
+        loop(PIECE, gather, 8)
 
         def setup(x):
             for h in range(HALVES):
@@ -749,7 +751,7 @@
                     base[i, at, :] = v
                     va[i, pl.ds(PIECE + r, SUB), :] = v
 
-        loop(PIECE, gather, 8)
+        loop(PIECE, gather, 16)
         here[...] = wt[group]
 
         def sweep(src, dst, out=None):
@@ -807,14 +809,14 @@
         part = [q1[pl.ds(yf + (b * GROUP + j) * SUB, SUB), :] for j in range(GROUP)]
         slab[pl.ds(b * SUB, SUB), :] = pack_tiles(part, SUB, lane)
 
-    loop(fr.live_blocks, block, 5)
+    loop(fr.live_blocks, block, 10)
 
     def core_rows(x):
         for t in range(fr.by // SUB):
             at = pl.ds((x + H) * yf + TOP + t * SUB, SUB)
             core[pl.ds(x * fr.by + t * SUB, SUB), :] = c0[at, :] + q0[at, :]
 
-    loop(fr.bx, core_rows, 4)
+    loop(fr.bx, core_rows, 8)
 
     def edge_rows(x):
         for j, t in enumerate((tiles - 1, 0)):
@@ -1006,7 +1008,7 @@
             pltpu.VMEM((3, 1, slots), jnp.int32),
             pltpu.VMEM((4, slots), jnp.int32),
             pltpu.SMEM((2, contrast.shape[0]), F32),
-            pltpu.SemaphoreType.DMA((8,)),
+            pltpu.SemaphoreType.DMA((11,)),
         ],
     )
     z_static = swap("gz", slabs)
@@ -1033,7 +1035,7 @@
     slabs, y_coefs = lax.optimization_barrier((slabs, y_coefs))
     y_static = swap("gy", slabs)
 
-    together = 4 if slots % 4 == 0 else 1
+    together = GROUP if slots % GROUP == 0 else 1
     p0, p1, *slabs = call(
         part(prolong, fr, (nb, together)),
         [fr.frame] * 2 + [rows_of(live_rows)] * n2,
@@ -1054,7 +1056,27 @@
         alias={1: 0, 2: 1, 3: 2},
         limit=16,
     )
-    received, k1 = lax.optimization_barrier((received, k1))
+    groups = slots // GROUP
+    cuts = (0, groups // 5, groups * 4 // 5, groups)
+    kinds = [
+        jax.ShapeDtypeStruct((groups, 6, PROWS, LANES), F32),
+        jax.ShapeDtypeStruct((groups, PROWS, LANES), F32),
+        jax.ShapeDtypeStruct((groups, PROWS, LANES), F32),
+    ]
+
+    def more(setup, first, last):
+        return call(
+            part(couple, fr, (first, last)),
+            kinds,
+            [info, off, k0, k1, w0, w1, *setup],
+            [SMEM] * 2,
+            [pltpu.VMEM((PROWS + 2 * PIECE, LANES), F32)],
+            alias={6 + i: i for i in range(len(setup))},
+            limit=16,
+        )
+
+    setup = more([], *cuts[0:2])
+    received, setup = lax.optimization_barrier((received, setup))
     p0, p1, *slabs = call(
         part(coarse_y, fr),
         [fr.frame] * 2 + [rows_of(fr.live_x * (WIDE + 2))] * n1,
@@ -1063,16 +1085,7 @@
         alias={1: 0, 2: 1},
     )
     received = swap("gy", slabs)
-    groups = slots // GROUP
-    split = (groups + 1) // 2
-    setup = [
-        jax.ShapeDtypeStruct((groups, 6, PROWS, LANES), F32),
-        jax.ShapeDtypeStruct((groups, PROWS, LANES), F32),
-        jax.ShapeDtypeStruct((groups, PROWS, LANES), F32),
-    ]
-    fields = [info, off, k0, k1, w0, w1]
-    buffer = [pltpu.VMEM((PROWS + 2 * PIECE, LANES), F32)]
-    setup = call(part(couple, fr, (0, split)), setup, fields, [SMEM] * 2, buffer, limit=16)
+    setup = more(setup, *cuts[1:3])
     received, setup = lax.optimization_barrier((received, setup))
     p0, p1, *slabs = call(
         part(coarse_x, fr),
@@ -1083,16 +1096,7 @@
     )
     received = swap("gx", slabs)
 
-    kinds = [jax.ShapeDtypeStruct(a.shape, F32) for a in setup]
-    setup = call(
-        part(couple, fr, (split, groups)),
-        kinds,
-        [*fields, *setup],
-        [SMEM] * 2,
-        buffer,
-        alias={6: 0, 7: 1, 8: 2},
-        limit=16,
-    )
+    setup = more(setup, *cuts[2:4])
     p0, p1, r0, r1 = call(
         part(middle, fr), [fr.frame] * 4, [info, p0, p1, k0, f0, k1, f1], [SMEM], alias={1: 0, 2: 1}, limit=16
     )

time: 100 us -> 99 us (0.990)
  the two profiles are of different devices: /device:TPU:9 before, /device:TPU:10 now
where the time goes in v4:
time: 99 us; the launch traced here: 97.1 us
  Pallas kernels  49.1 us (50%)
  starting transfers between devices  31 us (31%)
  waiting for transfers between devices  15.4 us (16%)
  between operations  1.56 us (2%)
    pallas_call x19, Pallas kernels, call(): pl.pallas_call(kernel, out_shape=outs, in_specs=specs, out_specs=out_spec...  49.1 us
    ppermute x17, starting transfers between devices, swap(): lax.ppermute(slab, axis, pairs + [(j, i) for i, j in pairs])  31 us
    ppermute x17, waiting for transfers between devices, swap(): lax.ppermute(slab, axis, pairs + [(j, i) for i, j in pairs])  15.4 us
  transfers between devices with their start and end apart: 17, of which 9 were waited for; matrix products, arithmetic and copies ran while one was open for 0% of the time, Pallas kernels for 24%

profile of v4, /device:TPU:10, one launch (start us, length us, event | category | flops | bytes accessed | tf_op | source)
XLA Modules:
  0.0 97.1 jit_solution(2297418772672625644)
XLA Ops:
  1.3 0.1 pad_add_fusion.info
  1.4 2.9 %shard_map.113 = (f32[1024,128]{1,0:T(8,128)S(1)}, f32[1024,128]{1,0:T(8,128)S(1)}, f32[1024,128]{1,0:T(8,128)S(1)}, f32[8,128]{1,0:T(8,128)S(1)}, s32[8,128]{1,0:T(8,128)S(1)}, /*index=5*/f32[136,128]{1,0:T(8,128)S(1)}) custom-call(s32[4]{0:T(128)S(1)} %pad_add_fusion.info, f32[4]{0:T(128)} %contrast.1, f32[4]{0:T(128)} %channel.1, f32[1024,128]{1,0:T(8,128)} %bitcast.27, ...), custom_call_target="tpu_custom_call" | custom-call | tf_op jit(solution)/shard_map/pallas_call | solution.py:125
  4.2 1.6 %collective-permute-start = (f32[136,128]{1,0:T(8,128)S(1)}, f32[136,128]{1,0:T(8,128)S(1)}, u32[]{:S(2)}, u32[]{:S(2)}) collective-permute-start(f32[136,128]{1,0:T(8,128)S(1)} %get-tuple-element.82), channel_id=1, source_target_pairs={{0,1},{1,0},{2,3},{3,2},{4,5},{5,4},{6,7},{7,6},{8,9},{9,8},{10,11... | collective-permute-start | bytes 208904 | tf_op jit(solution)/shard_map/ppermute | solution.py:145
  5.8 2.8 %collective-permute-done.rest_0_ = f32[136,128]{1,0:T(8,128)S(1)} collective-permute-done((f32[136,128]{1,0:T(8,128)S(1)}, f32[136,128]{1,0:T(8,128)S(1)}, u32[]{:S(2)}, u32[]{:S(2)}) %collective-permute-start) | collective-permute-done | bytes 69664 | tf_op jit(solution)/shard_map/ppermute | solution.py:145
  8.6 0.6 shard_map.114
  9.2 0.5 collective-permute-start.1
  9.7 4.6 %collective-permute-start.2 = (f32[456,128]{1,0:T(8,128)S(1)}, f32[456,128]{1,0:T(8,128)S(1)}, u32[]{:S(2)}, u32[]{:S(2)}) collective-permute-start(f32[456,128]{1,0:T(8,128)S(1)} %get-tuple-element.84), channel_id=1, source_target_pairs={{8,16},{16,8},{9,17},{17,9},{10,18},{18,10},{11,19},{19,11},{12,20... | collective-permute-start | bytes 700424 | tf_op jit(solution)/shard_map/ppermute | solution.py:145
  14.3 2.7 %shard_map.115.bases = f32[40,8,4096]{2,1,0:T(8,128)S(1)} custom-call(s32[4]{0:T(128)S(1)} %pad_add_fusion.info, f32[40,8,4096]{2,1,0:T(8,128)} %bitcast.24), custom_call_target="tpu_custom_call" | custom-call | tf_op jit(solution)/shard_map/pallas_call | solution.py:125
  17.0 0.0 collective-permute-done.1.rest_0_.rest_1_
  17.0 1.5 %collective-permute-done.2.rest_1_.rest_2_ = f32[456,128]{1,0:T(8,128)S(1)} collective-permute-done((f32[456,128]{1,0:T(8,128)S(1)}, f32[456,128]{1,0:T(8,128)S(1)}, u32[]{:S(2)}, u32[]{:S(2)}) %collective-permute-start.2) | collective-permute-done | bytes 233504 | tf_op jit(solution)/shard_map/ppermute | solution.py:145
  18.6 2.5 %collective-permute-start.4 = (f32[48,128]{1,0:T(8,128)S(1)}, f32[48,128]{1,0:T(8,128)S(1)}, u32[]{:S(2)}, u32[]{:S(2)}) collective-permute-start(f32[48,128]{1,0:T(8,128)S(1)} %shard_map.116.own), channel_id=1, source_target_pairs={{2,4},{4,2},{3,5},{5,3},{10,12},{12,10},{11,13},{13,11},{18,20},{2... | collective-permute-start | bytes 73736 | tf_op jit(solution)/shard_map/ppermute | solution.py:145
  21.1 1.4 %shard_map.117 = (f32[2048,128]{1,0:T(8,128)S(1)}, f32[2048,128]{1,0:T(8,128)S(1)}, f32[2048,128]{1,0:T(8,128)S(1)}, f32[600,128]{1,0:T(8,128)S(1)}, f32[600,128]{1,0:T(8,128)S(1)}) custom-call(s32[4]{0:T(128)S(1)} %pad_add_fusion.info, f32[1024,128]{1,0:T(8,128)S(1)} %get-tuple-element.90.kap, f32[1024,128]{1,0:T(8,128)S(1)} %get-tuple-element.79.frc, ...), custom_call_target="tpu_custom_call" | custom-call | tf_op jit(solution)/shard_map/pallas_call | solution.py:125
  22.5 0.0 collective-permute-done.3.rest_0_
  22.5 1.1 %collective-permute-done.4.rest_1_ = f32[48,128]{1,0:T(8,128)S(1)} collective-permute-done((f32[48,128]{1,0:T(8,128)S(1)}, f32[48,128]{1,0:T(8,128)S(1)}, u32[]{:S(2)}, u32[]{:S(2)}) %collective-permute-start.4) | collective-permute-done | bytes 24608 | tf_op jit(solution)/shard_map/ppermute | solution.py:145
  23.7 2.5 %collective-permute-start.7 = (f32[600,128]{1,0:T(8,128)S(1)}, f32[600,128]{1,0:T(8,128)S(1)}, u32[]{:S(2)}, u32[]{:S(2)}) collective-permute-start(f32[600,128]{1,0:T(8,128)S(1)} %get-tuple-element.102), channel_id=1, source_target_pairs={{2,4},{4,2},{3,5},{5,3},{10,12},{12,10},{11,13},{13,11},{18,20},{2... | collective-permute-start | bytes 921608 | tf_op jit(solution)/shard_map/ppermute | solution.py:145
  26.2 3.8 %shard_map.118 = (f32[2048,128]{1,0:T(8,128)S(1)}, f32[2048,128]{1,0:T(8,128)S(1)}, f32[240,128]{1,0:T(8,128)S(1)}) custom-call(s32[4]{0:T(128)S(1)} %pad_add_fusion.info, s32[8,128]{1,0:T(8,128)S(1)} %get-tuple-element.77.off, f32[40,8,4096]{2,1,0:T(8,128)S(1)} %shard_map.115.bases, f32[48,128]{1,0:T(8,128)S(1)} %shard_map.116.own, ...), custom_call_target="tpu_custom_call" | custom-call | tf_op jit(solution)/shard_map/pallas_call | solution.py:125
  30.1 0.6 collective-permute-start.5
  30.7 0.0 collective-permute-done.6.rest_3_
  30.7 1.2 %collective-permute-done.7.rest_4_ = f32[600,128]{1,0:T(8,128)S(1)} collective-permute-done((f32[600,128]{1,0:T(8,128)S(1)}, f32[600,128]{1,0:T(8,128)S(1)}, u32[]{:S(2)}, u32[]{:S(2)}) %collective-permute-start.7) | collective-permute-done | bytes 307232 | tf_op jit(solution)/shard_map/ppermute | solution.py:145
  31.9 2.4 %shard_map.119 = (f32[2048,128]{1,0:T(8,128)S(1)}, f32[2048,128]{1,0:T(8,128)S(1)}, f32[2048,128]{1,0:T(8,128)S(1)}, f32[2048,128]{1,0:T(8,128)S(1)}, f32[2048,128]{1,0:T(8,128)S(1)}, /*index=5*/f32[2048,128]{1,0:T(8,128)S(1)}) custom-call(s32[4]{0:T(128)S(1)} %pad_add_fusion.info, ...), custom_call_target="tpu_custom_call", output_to_operand_aliasing={{0}: (1, {}), {1}: (2, {}), {2}: (3, {})} | custom-call | tf_op jit(solution)/shard_map/pallas_call | solution.py:125
  34.3 1.7 %shard_map.120 = (f32[5,6,256,128]{3,2,1,0:T(8,128)S(1)}, f32[5,256,128]{2,1,0:T(8,128)S(1)}, f32[5,256,128]{2,1,0:T(8,128)S(1)}) custom-call(s32[4]{0:T(128)S(1)} %pad_add_fusion.info, s32[8,128]{1,0:T(8,128)S(1)} %get-tuple-element.77.off, f32[2048,128]{1,0:T(8,128)S(1)} %get-tuple-element.103.k0, f32[2048,128]{1,0:T(8,128)S(1)} %get-tuple-element.104.k1, ...), custom_call_target="tpu_custom_call" | custom-call | tf_op jit(solution)/shard_map/pallas_call | solution.py:125
  36.0 1.4 %shard_map.121 = (f32[2048,128]{1,0:T(8,128)S(1)}, f32[2048,128]{1,0:T(8,128)S(1)}, f32[440,128]{1,0:T(8,128)S(1)}, f32[440,128]{1,0:T(8,128)S(1)}) custom-call(s32[4]{0:T(128)S(1)} %pad_add_fusion.info, f32[2048,128]{1,0:T(8,128)S(1)} %get-tuple-element.95.p0_in, ...), custom_call_target="tpu_custom_call", output_to_operand_aliasing={{0}: (1, {}), {1}: (2, {})} | custom-call | tf_op jit(solution)/shard_map/pallas_call | solution.py:125
  37.4 0.1 collective-permute-start.8
  37.5 2.6 %collective-permute-start.9 = (f32[440,128]{1,0:T(8,128)S(1)}, f32[440,128]{1,0:T(8,128)S(1)}, u32[]{:S(2)}, u32[]{:S(2)}) collective-permute-start(f32[440,128]{1,0:T(8,128)S(1)} %get-tuple-element.114), channel_id=1, source_target_pairs={{2,4},{4,2},{3,5},{5,3},{10,12},{12,10},{11,13},{13,11},{18,20},{2... | collective-permute-start | bytes 675848 | tf_op jit(solution)/shard_map/ppermute | solution.py:145
  40.1 2.8 %shard_map.122 = (f32[5,6,256,128]{3,2,1,0:T(8,128)S(1)}, f32[5,256,128]{2,1,0:T(8,128)S(1)}, f32[5,256,128]{2,1,0:T(8,128)S(1)}) custom-call(s32[4]{0:T(128)S(1)} %pad_add_fusion.info, s32[8,128]{1,0:T(8,128)S(1)} %get-tuple-element.77.off, f32[2048,128]{1,0:T(8,128)S(1)} %get-tuple-element.103.k0, ...), custom_call_target="tpu_custom_call", output_to_operand_aliasing={{0}: (6, {}), {1}: (7, {}), {2}: (8, {})} | custom-call | tf_op jit(solution)/shard_map/pallas_call | solution.py:125
  42.9 0.0 collective-permute-done.8.rest_0_
  42.9 1.9 %collective-permute-done.9.rest_1_ = f32[440,128]{1,0:T(8,128)S(1)} collective-permute-done((f32[440,128]{1,0:T(8,128)S(1)}, f32[440,128]{1,0:T(8,128)S(1)}, u32[]{:S(2)}, u32[]{:S(2)}) %collective-permute-start.9) | collective-permute-done | bytes 225312 | tf_op jit(solution)/shard_map/ppermute | solution.py:145
  44.8 1.2 %shard_map.123 = (f32[2048,128]{1,0:T(8,128)S(1)}, f32[2048,128]{1,0:T(8,128)S(1)}, f32[488,128]{1,0:T(8,128)S(1)}, f32[488,128]{1,0:T(8,128)S(1)}) custom-call(s32[4]{0:T(128)S(1)} %pad_add_fusion.info, f32[2048,128]{1,0:T(8,128)S(1)} %get-tuple-element.111.p0_in, ...), custom_call_target="tpu_custom_call", output_to_operand_aliasing={{0}: (1, {}), {1}: (2, {})} | custom-call | tf_op jit(solution)/shard_map/pallas_call | solution.py:125
  46.1 0.1 collective-permute-start.10
  46.1 4.3 %collective-permute-start.11 = (f32[488,128]{1,0:T(8,128)S(1)}, f32[488,128]{1,0:T(8,128)S(1)}, u32[]{:S(2)}, u32[]{:S(2)}) collective-permute-start(f32[488,128]{1,0:T(8,128)S(1)} %get-tuple-element.138), channel_id=1, source_target_pairs={{8,16},{16,8},{9,17},{17,9},{10,18},{18,10},{11,19},{19,11},{12,20... | collective-permute-start | bytes 749576 | tf_op jit(solution)/shard_map/ppermute | solution.py:145
  50.5 0.6 shard_map.125
  51.1 2.5 %shard_map.124 = (f32[2048,128]{1,0:T(8,128)S(1)}, f32[2048,128]{1,0:T(8,128)S(1)}, f32[2048,128]{1,0:T(8,128)S(1)}, f32[2048,128]{1,0:T(8,128)S(1)}) custom-call(s32[4]{0:T(128)S(1)} %pad_add_fusion.info, f32[2048,128]{1,0:T(8,128)S(1)} %get-tuple-element.123.p0_in, ...), custom_call_target="tpu_custom_call", output_to_operand_aliasing={{0}: (1, {}), {1}: (2, {})} | custom-call | tf_op jit(solution)/shard_map/pallas_call | solution.py:125
  53.6 0.0 collective-permute-done.10.rest_0_
  53.6 1.1 %collective-permute-done.11.rest_1_ = f32[488,128]{1,0:T(8,128)S(1)} collective-permute-done((f32[488,128]{1,0:T(8,128)S(1)}, f32[488,128]{1,0:T(8,128)S(1)}, u32[]{:S(2)}, u32[]{:S(2)}) %collective-permute-start.11) | collective-permute-done | bytes 249888 | tf_op jit(solution)/shard_map/ppermute | solution.py:145
  54.7 17.2 %shard_map.126 = (f32[2048,128]{1,0:T(8,128)S(1)}, f32[2048,128]{1,0:T(8,128)S(1)}, f32[2048,128]{1,0:T(8,128)S(1)}, f32[2048,128]{1,0:T(8,128)S(1)}, f32[1024,1...) custom-call(s32[4]{0:T(128)S(1)} %pad_add_fusion.info, ...), custom_call_target="tpu_custom_call", output_to_operand_aliasing={{0}: (2, {}), {1}: (3, {}), {2}: (4, {}), {3}: (5, {})} | custom-call | tf_op jit(solution)/shard_map/pallas_call | solution.py:125
  71.9 0.1 collective-permute-start.12
  71.9 3.4 %shard_map.127 = f32[2560,128]{1,0:T(8,128)} custom-call(s32[4]{0:T(128)S(1)} %pad_add_fusion.info, f32[5,2,256,128]{3,2,1,0:T(8,128)S(1)} %get-tuple-element.141.solved), custom_call_target="tpu_custom_call" | custom-call | tf_op jit(solution)/shard_map/pallas_call | solution.py:125
  75.3 1.5 %collective-permute-done.12.rest_0_ = f32[240,128]{1,0:T(8,128)S(1)} collective-permute-done((f32[240,128]{1,0:T(8,128)S(1)}, f32[240,128]{1,0:T(8,128)S(1)}, u32[]{:S(2)}, u32[]{:S(2)}) %collective-permute-start.12) | collective-permute-done | bytes 122912 | tf_op jit(solution)/shard_map/ppermute | solution.py:145
  76.8 0.8 shard_map.128
  77.6 0.1 collective-permute-start.13
  77.7 1.9 %collective-permute-start.14 = (f32[160,128]{1,0:T(8,128)S(1)}, f32[160,128]{1,0:T(8,128)S(1)}, u32[]{:S(2)}, u32[]{:S(2)}) collective-permute-start(f32[160,128]{1,0:T(8,128)S(1)} %get-tuple-element.145), channel_id=1, source_target_pairs={{2,4},{4,2},{3,5},{5,3},{10,12},{12,10},{11,13},{13,11},{18,20},{2... | collective-permute-start | bytes 245768 | tf_op jit(solution)/shard_map/ppermute | solution.py:145
  79.7 3.8 %collective-permute-done.14.rest_2_ = f32[160,128]{1,0:T(8,128)S(1)} collective-permute-done((f32[160,128]{1,0:T(8,128)S(1)}, f32[160,128]{1,0:T(8,128)S(1)}, u32[]{:S(2)}, u32[]{:S(2)}) %collective-permute-start.14) | collective-permute-done | bytes 81952 | tf_op jit(solution)/shard_map/ppermute | solution.py:145
  83.5 0.7 shard_map.130
  84.2 0.1 collective-permute-start.15
  84.2 9.4 %collective-permute-start.16 = (f32[128,128]{1,0:T(8,128)S(1)}, f32[128,128]{1,0:T(8,128)S(1)}, u32[]{:S(2)}, u32[]{:S(2)}) collective-permute-start(f32[128,128]{1,0:T(8,128)S(1)} %get-tuple-element.150), channel_id=1, source_target_pairs={{8,16},{16,8},{9,17},{17,9},{10,18},{18,10},{11,19},{19,11},{12,20... | collective-permute-start | bytes 196616 | tf_op jit(solution)/shard_map/ppermute | solution.py:145
  93.6 1.8 %shard_map.129 = (f32[1024,128]{1,0:T(8,128)}, f32[256,128]{1,0:T(8,128)S(1)}) custom-call(s32[4]{0:T(128)S(1)} %pad_add_fusion.info, f32[1024,128]{1,0:T(8,128)S(1)} %get-tuple-element.139.core, f32[240,128]{1,0:T(8,128)S(1)} %collective-permute-done.12.rest_0_, f32[160,128]{1,0:T(8,128)S(1)} %collective-permute-done.13.rest_1_, ...), custom_call_target="tpu_custom_call" | custom-call | tf_op jit(solution)/shard_map/pallas_call | solution.py:125
  95.4 0.4 collective-permute-done.16.rest_1_
  95.8 1.2 %shard_map.131 = f32[1024,128]{1,0:T(8,128)} custom-call(s32[4]{0:T(128)S(1)} %pad_add_fusion.info, f32[1024,128]{1,0:T(8,128)} %get-tuple-element.146.out_in, f32[256,128]{1,0:T(8,128)S(1)} %get-tuple-element.147.edges, f32[128,128]{1,0:T(8,128)S(1)} %collective-permute-done.15.rest_0_, ...), custom_call_target="tpu_custom_call", output_to_operand_aliasing={{}: (1, {})} | custom-call | tf_op jit(solution)/shard_map/pallas_call | solution.py:125
  (6 shorter events, 0.0 us)
Async XLA Ops:
  4.2 4.4 %collective-permute-start = (f32[136,128]{1,0:T(8,128)S(1)}, f32[136,128]{1,0:T(8,128)S(1)}, u32[]{:S(2)}, u32[]{:S(2)}) collective-permute-start(f32[136,128]{1,0:T(8,128)S(1)} %get-tuple-element.82), channel_id=1, source_target_pairs={{0,1},{1,0},{2,3},{3,2},{4,5},{5,4},{6,7},{7,6},{8,9},{9,8},{10,11... | collective-permute-start | bytes 208904 | tf_op jit(solution)/shard_map/ppermute | solution.py:145
  9.2 7.8 %collective-permute-start.1 = (f32[456,128]{1,0:T(8,128)S(1)}, f32[456,128]{1,0:T(8,128)S(1)}, u32[]{:S(2)}, u32[]{:S(2)}) collective-permute-start(f32[456,128]{1,0:T(8,128)S(1)} %get-tuple-element.83), channel_id=1, source_target_pairs={{0,8},{16,24},{8,0},{24,16},{1,9},{17,25},{9,1},{25,17},{2,10},{18... | collective-permute-start | bytes 700424 | tf_op jit(solution)/shard_map/ppermute | solution.py:145
  9.7 8.9 %collective-permute-start.2 = (f32[456,128]{1,0:T(8,128)S(1)}, f32[456,128]{1,0:T(8,128)S(1)}, u32[]{:S(2)}, u32[]{:S(2)}) collective-permute-start(f32[456,128]{1,0:T(8,128)S(1)} %get-tuple-element.84), channel_id=1, source_target_pairs={{8,16},{16,8},{9,17},{17,9},{10,18},{18,10},{11,19},{19,11},{12,20... | collective-permute-start | bytes 700424 | tf_op jit(solution)/shard_map/ppermute | solution.py:145
  18.6 4.0 %collective-permute-start.3 = (f32[48,128]{1,0:T(8,128)S(1)}, f32[48,128]{1,0:T(8,128)S(1)}, u32[]{:S(2)}, u32[]{:S(2)}) collective-permute-start(f32[48,128]{1,0:T(8,128)S(1)} %shard_map.116.own), channel_id=1, source_target_pairs={{0,2},{4,6},{2,0},{6,4},{1,3},{5,7},{3,1},{7,5},{8,10},{12,14},{10... | collective-permute-start | bytes 73736 | tf_op jit(solution)/shard_map/ppermute | solution.py:145
  18.6 5.1 %collective-permute-start.4 = (f32[48,128]{1,0:T(8,128)S(1)}, f32[48,128]{1,0:T(8,128)S(1)}, u32[]{:S(2)}, u32[]{:S(2)}) collective-permute-start(f32[48,128]{1,0:T(8,128)S(1)} %shard_map.116.own), channel_id=1, source_target_pairs={{2,4},{4,2},{3,5},{5,3},{10,12},{12,10},{11,13},{13,11},{18,20},{2... | collective-permute-start | bytes 73736 | tf_op jit(solution)/shard_map/ppermute | solution.py:145
  23.7 7.0 %collective-permute-start.6 = (f32[600,128]{1,0:T(8,128)S(1)}, f32[600,128]{1,0:T(8,128)S(1)}, u32[]{:S(2)}, u32[]{:S(2)}) collective-permute-start(f32[600,128]{1,0:T(8,128)S(1)} %get-tuple-element.101), channel_id=1, source_target_pairs={{0,2},{4,6},{2,0},{6,4},{1,3},{5,7},{3,1},{7,5},{8,10},{12,14},{10... | collective-permute-start | bytes 921608 | tf_op jit(solution)/shard_map/ppermute | solution.py:145
  23.7 8.2 %collective-permute-start.7 = (f32[600,128]{1,0:T(8,128)S(1)}, f32[600,128]{1,0:T(8,128)S(1)}, u32[]{:S(2)}, u32[]{:S(2)}) collective-permute-start(f32[600,128]{1,0:T(8,128)S(1)} %get-tuple-element.102), channel_id=1, source_target_pairs={{2,4},{4,2},{3,5},{5,3},{10,12},{12,10},{11,13},{13,11},{18,20},{2... | collective-permute-start | bytes 921608 | tf_op jit(solution)/shard_map/ppermute | solution.py:145
  30.1 6.0 %collective-permute-start.5 = (f32[240,128]{1,0:T(8,128)S(1)}, f32[240,128]{1,0:T(8,128)S(1)}, u32[]{:S(2)}, u32[]{:S(2)}) collective-permute-start(f32[240,128]{1,0:T(8,128)S(1)} %get-tuple-element.97), channel_id=1, source_target_pairs={{0,1},{1,0},{2,3},{3,2},{4,5},{5,4},{6,7},{7,6},{8,9},{9,8},{10,11... | collective-permute-start | bytes 368648 | tf_op jit(solution)/shard_map/ppermute | solution.py:145
  37.4 5.5 %collective-permute-start.8 = (f32[440,128]{1,0:T(8,128)S(1)}, f32[440,128]{1,0:T(8,128)S(1)}, u32[]{:S(2)}, u32[]{:S(2)}) collective-permute-start(f32[440,128]{1,0:T(8,128)S(1)} %get-tuple-element.113), channel_id=1, source_target_pairs={{0,2},{4,6},{2,0},{6,4},{1,3},{5,7},{3,1},{7,5},{8,10},{12,14},{10... | collective-permute-start | bytes 675848 | tf_op jit(solution)/shard_map/ppermute | solution.py:145
  37.5 7.3 %collective-permute-start.9 = (f32[440,128]{1,0:T(8,128)S(1)}, f32[440,128]{1,0:T(8,128)S(1)}, u32[]{:S(2)}, u32[]{:S(2)}) collective-permute-start(f32[440,128]{1,0:T(8,128)S(1)} %get-tuple-element.114), channel_id=1, source_target_pairs={{2,4},{4,2},{3,5},{5,3},{10,12},{12,10},{11,13},{13,11},{18,20},{2... | collective-permute-start | bytes 675848 | tf_op jit(solution)/shard_map/ppermute | solution.py:145
  46.1 7.5 %collective-permute-start.10 = (f32[488,128]{1,0:T(8,128)S(1)}, f32[488,128]{1,0:T(8,128)S(1)}, u32[]{:S(2)}, u32[]{:S(2)}) collective-permute-start(f32[488,128]{1,0:T(8,128)S(1)} %get-tuple-element.137), channel_id=1, source_target_pairs={{0,8},{16,24},{8,0},{24,16},{1,9},{17,25},{9,1},{25,17},{2,10},{18... | collective-permute-start | bytes 749576 | tf_op jit(solution)/shard_map/ppermute | solution.py:145
  46.1 8.6 %collective-permute-start.11 = (f32[488,128]{1,0:T(8,128)S(1)}, f32[488,128]{1,0:T(8,128)S(1)}, u32[]{:S(2)}, u32[]{:S(2)}) collective-permute-start(f32[488,128]{1,0:T(8,128)S(1)} %get-tuple-element.138), channel_id=1, source_target_pairs={{8,16},{16,8},{9,17},{17,9},{10,18},{18,10},{11,19},{19,11},{12,20... | collective-permute-start | bytes 749576 | tf_op jit(solution)/shard_map/ppermute | solution.py:145
  71.9 4.9 %collective-permute-start.12 = (f32[240,128]{1,0:T(8,128)S(1)}, f32[240,128]{1,0:T(8,128)S(1)}, u32[]{:S(2)}, u32[]{:S(2)}) collective-permute-start(f32[240,128]{1,0:T(8,128)S(1)} %get-tuple-element.140), channel_id=1, source_target_pairs={{0,1},{1,0},{2,3},{3,2},{4,5},{5,4},{6,7},{7,6},{8,9},{9,8},{10,11... | collective-permute-start | bytes 368648 | tf_op jit(solution)/shard_map/ppermute | solution.py:145
  77.6 2.0 %collective-permute-start.13 = (f32[160,128]{1,0:T(8,128)S(1)}, f32[160,128]{1,0:T(8,128)S(1)}, u32[]{:S(2)}, u32[]{:S(2)}) collective-permute-start(f32[160,128]{1,0:T(8,128)S(1)} %get-tuple-element.144), channel_id=1, source_target_pairs={{0,2},{4,6},{2,0},{6,4},{1,3},{5,7},{3,1},{7,5},{8,10},{12,14},{10... | collective-permute-start | bytes 245768 | tf_op jit(solution)/shard_map/ppermute | solution.py:145
  77.7 5.8 %collective-permute-start.14 = (f32[160,128]{1,0:T(8,128)S(1)}, f32[160,128]{1,0:T(8,128)S(1)}, u32[]{:S(2)}, u32[]{:S(2)}) collective-permute-start(f32[160,128]{1,0:T(8,128)S(1)} %get-tuple-element.145), channel_id=1, source_target_pairs={{2,4},{4,2},{3,5},{5,3},{10,12},{12,10},{11,13},{13,11},{18,20},{2... | collective-permute-start | bytes 245768 | tf_op jit(solution)/shard_map/ppermute | solution.py:145
  84.2 11.2 %collective-permute-start.15 = (f32[128,128]{1,0:T(8,128)S(1)}, f32[128,128]{1,0:T(8,128)S(1)}, u32[]{:S(2)}, u32[]{:S(2)}) collective-permute-start(f32[128,128]{1,0:T(8,128)S(1)} %get-tuple-element.149), channel_id=1, source_target_pairs={{0,8},{16,24},{8,0},{24,16},{1,9},{17,25},{9,1},{25,17},{2,10},{18... | collective-permute-start | bytes 196616 | tf_op jit(solution)/shard_map/ppermute | solution.py:145
  84.2 11.6 %collective-permute-start.16 = (f32[128,128]{1,0:T(8,128)S(1)}, f32[128,128]{1,0:T(8,128)S(1)}, u32[]{:S(2)}, u32[]{:S(2)}) collective-permute-start(f32[128,128]{1,0:T(8,128)S(1)} %get-tuple-element.150), channel_id=1, source_target_pairs={{8,16},{16,8},{9,17},{17,9},{10,18},{18,10},{11,19},{19,11},{12,20... | collective-permute-start | bytes 196616 | tf_op jit(solution)/shard_map/ppermute | solution.py:145
